TPU v7x, 128 devices: a whole 4x4x4 slice. The times are simulated.
128 devices in a mesh: segment: 4 (over x), tensor: 16 (over z, y), dp: 2 (over core).
Axes of the slice: x: 4, y: 4, z: 4, core: 2. Of those that a mesh axis runs over, the one named last changes fastest.
Arguments:
- act_input: bfloat16 [4, 384, 12288], P('dp', None, 'tensor'), may hold values from -6 to 6
- cotangent: bfloat16 [4, 384, 12288], P('dp', None, 'tensor'), may hold values from -7.2 to 7.2
- lengths: int32 [4], P('dp'), may hold values from 1 to 384, 960 in all
- clip_scale: float32 [4], P('segment'), may hold values from 266.043 to 1064.172
- adapt_down: bfloat16 [4, 12288, 64], P('segment', 'tensor'), may hold values from -0.0546875 to 0.0546875
- adapt_up: bfloat16 [4, 64, 12288], P('segment', None, 'tensor'), may hold values from -0.375 to 0.375
Outputs:
- grad_down: float32 [4, 12288, 64], P('segment', ('tensor', 'dp'))
- grad_up: float32 [4, 64, 12288], P('segment', None, ('tensor', 'dp'))
Inputs may be any that keep to these rules, and one draw needn't show every extreme that they name: `lengths`: each example has at least one real row, and some example fills all 384 slots.
All inputs are finite; a program needn't handle non-finite values. No bound on the sum of `lengths` on one device may be relied on, other than what follows from the above.
Results may differ from a plain program's by a relative error of at most 0.011.
Values may be sent and summed in bfloat16 or wider, within the bound.
No kernel may reach another device: no remote copies, remote signals or barrier semaphores. Data moves between devices by JAX's collectives and lax.ppermute only.
A program may use at most 64 MiB of HBM per device.

v0:
```python
import jax
import jax.numpy as jnp
from jax import lax
from jax.sharding import PartitionSpec as P

SLOPE_C = 0.7978845608
CUBIC = 0.044715


def shifted(value, axis, steps):
    count = lax.axis_size(axis)
    leading, last = (max(0, -steps), min(count, count - steps))
    return lax.ppermute(value, axis, [(source, source + steps) for source in range(leading, last)])


def gelu_value(values):
    tangent = jnp.tanh(SLOPE_C * (values + CUBIC * values * values * values))
    return 0.5 * values * (1.0 + tangent)


def gelu_slope(values):
    tangent = jnp.tanh(SLOPE_C * (values + CUBIC * values * values * values))
    return 0.5 * (1.0 + tangent) + 0.5 * values * (1.0 - tangent * tangent) * SLOPE_C * (
        1.0 + 3.0 * CUBIC * values * values
    )


def bottleneck_total(partial_value):
    return lax.psum(partial_value, "tensor")


def shards(act_input, cotangent, lengths, clip_scale, adapt_down, adapt_up):
    phase_count = lax.axis_size("segment")
    phase_rank = lax.axis_index("segment")
    micro_count = act_input.shape[0]
    row_slots = act_input.shape[1]
    local_width = act_input.shape[2]
    bottle_width = adapt_down.shape[2]
    down_local = adapt_down[0]
    up_local = adapt_up[0]
    threshold = clip_scale[0]
    group_size = 1
    round_count = micro_count // group_size
    step_count = phase_count + round_count - 1

    def take_block(source, position):
        return lax.dynamic_slice_in_dim(source, position * group_size, group_size, 0)

    def forward_step(tick_index, carried):
        received, stored_input, stored_bottle = carried
        slot_index = tick_index - phase_rank
        active = jnp.logical_and(slot_index >= 0, slot_index < round_count)
        clamped = jnp.clip(slot_index, 0, round_count - 1)
        current = jnp.where(phase_rank == 0, take_block(act_input, clamped), received)
        bottle = bottleneck_total(
            jnp.einsum("gtd,dr->gtr", current, down_local, preferred_element_type=jnp.float32)
        )
        hidden = gelu_value(bottle).astype(jnp.bfloat16)
        branch = jnp.einsum("gtr,rd->gtd", hidden, up_local, preferred_element_type=jnp.float32)
        following = (current.astype(jnp.float32) + branch).astype(jnp.bfloat16)
        row_start = clamped * group_size
        stored_input = lax.dynamic_update_slice_in_dim(
            stored_input,
            jnp.where(active, current, take_block(stored_input, clamped)),
            row_start,
            0,
        )
        stored_bottle = lax.dynamic_update_slice_in_dim(
            stored_bottle,
            jnp.where(active, bottle, take_block(stored_bottle, clamped)),
            row_start,
            0,
        )
        received = shifted(following, "segment", 1)
        return (received, stored_input, stored_bottle)

    initial = (
        jnp.zeros((group_size, row_slots, local_width), jnp.bfloat16),
        jnp.zeros((micro_count, row_slots, local_width), jnp.bfloat16),
        jnp.zeros((micro_count, row_slots, bottle_width), jnp.float32),
    )
    leftover, stored_input, stored_bottle = lax.fori_loop(0, step_count, forward_step, initial)
    live_rows = jnp.arange(row_slots, dtype=jnp.int32)[None, :] < lengths[:, None]
    masked = jnp.where(live_rows[:, :, None], cotangent, jnp.zeros_like(cotangent))

    def backward_core(tick_index, received):
        slot_index = tick_index - (phase_count - 1 - phase_rank)
        active = jnp.logical_and(slot_index >= 0, slot_index < round_count)
        clamped = jnp.clip(slot_index, 0, round_count - 1)
        incoming = jnp.where(phase_rank == phase_count - 1, take_block(masked, clamped), received)
        current = take_block(stored_input, clamped)
        bottle = take_block(stored_bottle, clamped)
        hidden = gelu_value(bottle).astype(jnp.bfloat16)
        spread = bottleneck_total(
            jnp.einsum("gtd,rd->gtr", incoming, up_local, preferred_element_type=jnp.float32)
        )
        slope_grad = (spread * gelu_slope(bottle)).astype(jnp.bfloat16)
        backward = jnp.einsum(
            "gtr,dr->gtd", slope_grad, down_local, preferred_element_type=jnp.float32
        )
        previous = (incoming.astype(jnp.float32) + backward).astype(jnp.bfloat16)
        outgoing = shifted(previous, "segment", -1)
        grad_up_each = jnp.einsum(
            "gtr,gtd->grd", hidden, incoming, preferred_element_type=jnp.float32
        )
        grad_down_each = jnp.einsum(
            "gtd,gtr->gdr", current, slope_grad, preferred_element_type=jnp.float32
        )
        squares = jnp.sum(grad_down_each * grad_down_each, axis=(1, 2)) + jnp.sum(
            grad_up_each * grad_up_each, axis=(1, 2)
        )
        return (active, clamped, grad_down_each, grad_up_each, squares, outgoing)

    empty_inbox = jnp.zeros((group_size, row_slots, local_width), jnp.bfloat16)

    def backward_step(tick_index, carried):
        received, total_down, total_up = carried
        active, clamped, grad_down_each, grad_up_each, squares, outgoing = backward_core(
            tick_index, received
        )
        norm_total = jnp.sqrt(lax.psum(squares, "tensor"))
        factor = jnp.where(active, threshold / (norm_total + 0.01), 0.0)
        total_down = total_down + jnp.sum(factor[:, None, None] * grad_down_each, axis=0)
        total_up = total_up + jnp.sum(factor[:, None, None] * grad_up_each, axis=0)
        return (outgoing, total_down, total_up)

    start_state = (
        empty_inbox,
        jnp.zeros((local_width, bottle_width), jnp.float32),
        jnp.zeros((bottle_width, local_width), jnp.float32),
    )
    leftover, total_down, total_up = lax.fori_loop(0, step_count, backward_step, start_state)
    summed_down, summed_up = (
        lax.psum_scatter(total_down, "dp", scatter_dimension=0, tiled=True),
        lax.psum_scatter(total_up, "dp", scatter_dimension=1, tiled=True),
    )
    return (summed_down[None], summed_up[None])


def solution(mesh):
    return jax.shard_map(
        shards,
        mesh=mesh,
        in_specs=(
            P("dp", None, "tensor"),
            P("dp", None, "tensor"),
            P("dp"),
            P("segment"),
            P("segment", "tensor", None),
            P("segment", None, "tensor"),
        ),
        out_specs=(P("segment", ("tensor", "dp"), None), P("segment", None, ("tensor", "dp"))),
        check_vma=False,
    )
```

profile of v0, /device:TPU:1, one launch (start us, length us, event | category | flops | bytes accessed | tf_op | source)
XLA Modules:
  0.0 1223.6 jit_solution(5834056897023873622)
XLA Ops:
  9.8 2.5 broadcast_select_fusion
  12.4 510.7 %while.38 = (s32[]{:T(128)}, bf16[1,384,768]{2,1,0:T(8,128)(2,1)S(1)}, bf16[2,384,768]{2,1,0:T(8,128)(2,1)S(1)}, f32[2,384,64]{1,2,0:T(8,128)S(1)}, pred[]{:T(51...) while((s32[]{:T(128)}, ...), condition=%wide.region_2.3_spmd, body=%wide.region_0.2_spmd.sunk | while | flops 77242376 | bytes 8749349 | solution.py:82
  12.5 1.4 select_dynamic-update-slice_fusion.4
  14.8 86.0 %all-reduce.3.cloned.1.call-done = f32[1,384,64]{1,2,0:T(8,128)} async-done(((f32[1,384,64]{1,2,0:T(8,128)}), f32[1,384,64]{1,2,0:T(8,128)}) %all-reduce.3.cloned.1.call-update) | async-done | bytes 98320 | tf_op jit(solution)/shard_map/while/body/eval_jaxpr/psum | solution.py:29
  102.2 3.1 collective-permute-start
  105.4 10.0 collective-permute-done
  115.4 1.3 select_dynamic-update-slice_fusion.4
  117.7 85.2 %all-reduce.3.cloned.1.call-done = f32[1,384,64]{1,2,0:T(8,128)} async-done(((f32[1,384,64]{1,2,0:T(8,128)}), f32[1,384,64]{1,2,0:T(8,128)}) %all-reduce.3.cloned.1.call-update) | async-done | bytes 98320 | tf_op jit(solution)/shard_map/while/body/eval_jaxpr/psum | solution.py:29
  204.3 3.1 collective-permute-start
  207.4 10.0 collective-permute-done
  217.4 1.3 select_dynamic-update-slice_fusion.4
  219.8 85.3 %all-reduce.3.cloned.1.call-done = f32[1,384,64]{1,2,0:T(8,128)} async-done(((f32[1,384,64]{1,2,0:T(8,128)}), f32[1,384,64]{1,2,0:T(8,128)}) %all-reduce.3.cloned.1.call-update) | async-done | bytes 98320 | tf_op jit(solution)/shard_map/while/body/eval_jaxpr/psum | solution.py:29
  306.4 3.1 collective-permute-start
  309.5 10.0 collective-permute-done
  319.5 1.3 select_dynamic-update-slice_fusion.4
  321.9 85.0 %all-reduce.3.cloned.1.call-done = f32[1,384,64]{1,2,0:T(8,128)} async-done(((f32[1,384,64]{1,2,0:T(8,128)}), f32[1,384,64]{1,2,0:T(8,128)}) %all-reduce.3.cloned.1.call-update) | async-done | bytes 98320 | tf_op jit(solution)/shard_map/while/body/eval_jaxpr/psum | solution.py:29
  408.2 3.1 collective-permute-start
  411.4 10.0 collective-permute-done
  423.7 84.9 %all-reduce.3.cloned.1.call-done = f32[1,384,64]{1,2,0:T(8,128)} async-done(((f32[1,384,64]{1,2,0:T(8,128)}), f32[1,384,64]{1,2,0:T(8,128)}) %all-reduce.3.cloned.1.call-update) | async-done | bytes 98320 | tf_op jit(solution)/shard_map/while/body/eval_jaxpr/psum | solution.py:29
  510.0 3.1 collective-permute-start
  513.2 10.0 collective-permute-done
  523.2 658.1 %while.39 = (s32[]{:T(128)}, bf16[1,384,768]{2,1,0:T(8,128)(2,1)S(1)}, f32[768,64]{0,1:T(8,128)}, f32[64,768]{1,0:T(8,128)}, pred[]{:T(512)}, /*index=5*/s32[]{:...) while((s32[]{:T(128)}, ...), condition=%wide.region_8.9_spmd.clone, body=%wide.region_3.8_spmd.clone.sunk | while | flops 153845760 | bytes 12486143 | solution.py:132
  526.3 84.6 %all-reduce.5.cloned.1.call-done = f32[1,384,64]{1,2,0:T(8,128)} async-done(((f32[1,384,64]{1,2,0:T(8,128)}), f32[1,384,64]{1,2,0:T(8,128)}) %all-reduce.5.cloned.1.call-update) | async-done | bytes 98320 | tf_op jit(solution)/shard_map/while/body/eval_jaxpr/psum | solution.py:29
  610.9 1.4 fusion.69
  612.2 1.4 collective-permute-start.1
  615.8 32.0 %psum.45 = f32[1]{0:T(128)} all-reduce(f32[1]{0:T(128)} %bitcast.93), channel_id=1, replica_groups=mesh['segment'=4,'tensor'=16,'dp'=2] {'tensor'}, use_global_device_ids=true, to_apply=%region_7.7 | all-reduce | flops 1 | bytes 8 | tf_op jit(solution)/shard_map/while/body/eval_jaxpr/psum | solution.py:121
  653.7 89.0 %all-reduce.5.cloned.1.call-done = f32[1,384,64]{1,2,0:T(8,128)} async-done(((f32[1,384,64]{1,2,0:T(8,128)}), f32[1,384,64]{1,2,0:T(8,128)}) %all-reduce.5.cloned.1.call-update) | async-done | bytes 98320 | tf_op jit(solution)/shard_map/while/body/eval_jaxpr/psum | solution.py:29
  742.7 1.4 fusion.69
  744.1 1.4 collective-permute-start.1
  747.6 32.0 %psum.45 = f32[1]{0:T(128)} all-reduce(f32[1]{0:T(128)} %bitcast.93), channel_id=1, replica_groups=mesh['segment'=4,'tensor'=16,'dp'=2] {'tensor'}, use_global_device_ids=true, to_apply=%region_7.7 | all-reduce | flops 1 | bytes 8 | tf_op jit(solution)/shard_map/while/body/eval_jaxpr/psum | solution.py:121
  781.0 1.6 select_add_fusion.5
  786.4 89.0 %all-reduce.5.cloned.1.call-done = f32[1,384,64]{1,2,0:T(8,128)} async-done(((f32[1,384,64]{1,2,0:T(8,128)}), f32[1,384,64]{1,2,0:T(8,128)}) %all-reduce.5.cloned.1.call-update) | async-done | bytes 98320 | tf_op jit(solution)/shard_map/while/body/eval_jaxpr/psum | solution.py:29
  875.4 1.4 fusion.69
  876.8 1.4 collective-permute-start.1
  880.3 32.0 %psum.45 = f32[1]{0:T(128)} all-reduce(f32[1]{0:T(128)} %bitcast.93), channel_id=1, replica_groups=mesh['segment'=4,'tensor'=16,'dp'=2] {'tensor'}, use_global_device_ids=true, to_apply=%region_7.7 | all-reduce | flops 1 | bytes 8 | tf_op jit(solution)/shard_map/while/body/eval_jaxpr/psum | solution.py:121
  913.7 1.6 select_add_fusion.5
  919.1 89.0 %all-reduce.5.cloned.1.call-done = f32[1,384,64]{1,2,0:T(8,128)} async-done(((f32[1,384,64]{1,2,0:T(8,128)}), f32[1,384,64]{1,2,0:T(8,128)}) %all-reduce.5.cloned.1.call-update) | async-done | bytes 98320 | tf_op jit(solution)/shard_map/while/body/eval_jaxpr/psum | solution.py:29
  1008.2 1.4 fusion.69
  1009.5 1.4 collective-permute-start.1
  1013.1 32.0 %psum.45 = f32[1]{0:T(128)} all-reduce(f32[1]{0:T(128)} %bitcast.93), channel_id=1, replica_groups=mesh['segment'=4,'tensor'=16,'dp'=2] {'tensor'}, use_global_device_ids=true, to_apply=%region_7.7 | all-reduce | flops 1 | bytes 8 | tf_op jit(solution)/shard_map/while/body/eval_jaxpr/psum | solution.py:121
  1046.5 1.6 select_add_fusion.5
  1051.9 88.7 %all-reduce.5.cloned.1.call-done = f32[1,384,64]{1,2,0:T(8,128)} async-done(((f32[1,384,64]{1,2,0:T(8,128)}), f32[1,384,64]{1,2,0:T(8,128)}) %all-reduce.5.cloned.1.call-update) | async-done | bytes 98320 | tf_op jit(solution)/shard_map/while/body/eval_jaxpr/psum | solution.py:29
  1140.6 1.4 fusion.69
  1142.0 1.4 collective-permute-start.1
  1145.5 32.0 %psum.45 = f32[1]{0:T(128)} all-reduce(f32[1]{0:T(128)} %bitcast.93), channel_id=1, replica_groups=mesh['segment'=4,'tensor'=16,'dp'=2] {'tensor'}, use_global_device_ids=true, to_apply=%region_7.7 | all-reduce | flops 1 | bytes 8 | tf_op jit(solution)/shard_map/while/body/eval_jaxpr/psum | solution.py:121
  1178.9 1.6 select_add_fusion.5
  1182.4 19.4 %reduce-scatter.3.cloned.1.call-done = f32[384,64]{0,1:T(8,128)} async-done(((f32[768,64]{0,1:T(8,128)}), f32[384,64]{0,1:T(8,128)}) %reduce-scatter.3.cloned.1.call-update) | async-done | bytes 98320 | tf_op jit(solution)/shard_map/reduce_scatter | solution.py:134
  1201.9 14.3 %reduce-scatter.5.cloned.1.call-done = f32[64,384]{1,0:T(8,128)} async-done(((f32[64,768]{1,0:T(8,128)}), f32[64,384]{1,0:T(8,128)}) %reduce-scatter.5.cloned.1.call-update) | async-done | bytes 98320 | tf_op jit(solution)/shard_map/reduce_scatter | solution.py:135
  (129 shorter events, 39.9 us)
Async XLA Ops:
  12.4 88.4 %all-reduce.3.cloned.1.call-start = ((), (), s32[]{:S(2)}) async-start(), calls=%async_computation.4 | async-start | bytes 196608 | tf_op jit(solution)/shard_map/while/body/eval_jaxpr/psum | solution.py:29
  100.8 4.5 copy-start.2
  102.2 13.2 %collective-permute-start = (bf16[1,384,768]{2,1,0:T(8,128)(2,1)S(1)}, bf16[1,384,768]{2,1,0:T(8,128)(2,1)S(1)}, u32[]{:S(2)}, u32[]{:S(2)}) collective-permute-start(bf16[1,384,768]{2,1,0:T(8,128)(2,1)S(1)} %fusion.64), channel_id=1, source_target_pairs={{0,32},{32,64},{64,96},{1,33},{33,65},{65,97},{2,34},{34,66},{66,9... | collective-permute-start | bytes 1769480 | tf_op jit(solution)/shard_map/while/body/eval_jaxpr/ppermute | solution.py:13
  115.4 87.6 %all-reduce.3.cloned.1.call-start = ((), (), s32[]{:S(2)}) async-start(), calls=%async_computation.4 | async-start | bytes 196608 | tf_op jit(solution)/shard_map/while/body/eval_jaxpr/psum | solution.py:29
  202.9 4.5 copy-start.2
  204.3 13.2 %collective-permute-start = (bf16[1,384,768]{2,1,0:T(8,128)(2,1)S(1)}, bf16[1,384,768]{2,1,0:T(8,128)(2,1)S(1)}, u32[]{:S(2)}, u32[]{:S(2)}) collective-permute-start(bf16[1,384,768]{2,1,0:T(8,128)(2,1)S(1)} %fusion.64), channel_id=1, source_target_pairs={{0,32},{32,64},{64,96},{1,33},{33,65},{65,97},{2,34},{34,66},{66,9... | collective-permute-start | bytes 1769480 | tf_op jit(solution)/shard_map/while/body/eval_jaxpr/ppermute | solution.py:13
  217.4 87.6 %all-reduce.3.cloned.1.call-start = ((), (), s32[]{:S(2)}) async-start(), calls=%async_computation.4 | async-start | bytes 196608 | tf_op jit(solution)/shard_map/while/body/eval_jaxpr/psum | solution.py:29
  305.0 4.5 copy-start.2
  306.4 13.2 %collective-permute-start = (bf16[1,384,768]{2,1,0:T(8,128)(2,1)S(1)}, bf16[1,384,768]{2,1,0:T(8,128)(2,1)S(1)}, u32[]{:S(2)}, u32[]{:S(2)}) collective-permute-start(bf16[1,384,768]{2,1,0:T(8,128)(2,1)S(1)} %fusion.64), channel_id=1, source_target_pairs={{0,32},{32,64},{64,96},{1,33},{33,65},{65,97},{2,34},{34,66},{66,9... | collective-permute-start | bytes 1769480 | tf_op jit(solution)/shard_map/while/body/eval_jaxpr/ppermute | solution.py:13
  319.5 87.3 %all-reduce.3.cloned.1.call-start = ((), (), s32[]{:S(2)}) async-start(), calls=%async_computation.4 | async-start | bytes 196608 | tf_op jit(solution)/shard_map/while/body/eval_jaxpr/psum | solution.py:29
  406.9 4.5 copy-start.2
  408.2 13.2 %collective-permute-start = (bf16[1,384,768]{2,1,0:T(8,128)(2,1)S(1)}, bf16[1,384,768]{2,1,0:T(8,128)(2,1)S(1)}, u32[]{:S(2)}, u32[]{:S(2)}) collective-permute-start(bf16[1,384,768]{2,1,0:T(8,128)(2,1)S(1)} %fusion.64), channel_id=1, source_target_pairs={{0,32},{32,64},{64,96},{1,33},{33,65},{65,97},{2,34},{34,66},{66,9... | collective-permute-start | bytes 1769480 | tf_op jit(solution)/shard_map/while/body/eval_jaxpr/ppermute | solution.py:13
  421.4 87.3 %all-reduce.3.cloned.1.call-start = ((), (), s32[]{:S(2)}) async-start(), calls=%async_computation.4 | async-start | bytes 196608 | tf_op jit(solution)/shard_map/while/body/eval_jaxpr/psum | solution.py:29
  508.6 4.5 copy-start.2
  510.0 13.2 %collective-permute-start = (bf16[1,384,768]{2,1,0:T(8,128)(2,1)S(1)}, bf16[1,384,768]{2,1,0:T(8,128)(2,1)S(1)}, u32[]{:S(2)}, u32[]{:S(2)}) collective-permute-start(bf16[1,384,768]{2,1,0:T(8,128)(2,1)S(1)} %fusion.64), channel_id=1, source_target_pairs={{0,32},{32,64},{64,96},{1,33},{33,65},{65,97},{2,34},{34,66},{66,9... | collective-permute-start | bytes 1769480 | tf_op jit(solution)/shard_map/while/body/eval_jaxpr/ppermute | solution.py:13
  523.2 1.2 copy-start.1
  523.2 87.6 %all-reduce.5.cloned.1.call-start = ((), (), s32[]{:S(2)}) async-start(), calls=%async_computation.5 | async-start | bytes 196608 | tf_op jit(solution)/shard_map/while/body/eval_jaxpr/psum | solution.py:29
  610.9 2.8 copy-start
  612.2 37.7 %copy-start.3 = (f32[768,64]{0,1:T(8,128)S(1)}, f32[768,64]{0,1:T(8,128)}, u32[]{:S(2)}) copy-start(f32[768,64]{0,1:T(8,128)} %get-tuple-element.725) | copy-start | bytes 589828 | tf_op jit(solution)/shard_map/while
  612.2 37.8 %collective-permute-start.1 = (bf16[1,384,768]{2,1,0:T(8,128)(2,1)S(1)}, bf16[1,384,768]{2,1,0:T(8,128)(2,1)S(1)}, u32[]{:S(2)}, u32[]{:S(2)}) collective-permute-start(bf16[1,384,768]{2,1,0:T(8,128)(2,1)S(1)} %fusion.69), channel_id=1, source_target_pairs={{32,0},{64,32},{96,64},{33,1},{65,33},{97,65},{34,2},{66,34},{98,6... | collective-permute-start | bytes 1769480 | tf_op jit(solution)/shard_map/while/body/eval_jaxpr/ppermute | solution.py:13
  650.0 0.7 copy-start.4
  650.6 1.2 copy-start.1
  650.6 92.0 %all-reduce.5.cloned.1.call-start = ((), (), s32[]{:S(2)}) async-start(), calls=%async_computation.5 | async-start | bytes 196608 | tf_op jit(solution)/shard_map/while/body/eval_jaxpr/psum | solution.py:29
  742.7 2.8 copy-start
  744.1 38.6 %copy-start.3 = (f32[768,64]{0,1:T(8,128)S(1)}, f32[768,64]{0,1:T(8,128)}, u32[]{:S(2)}) copy-start(f32[768,64]{0,1:T(8,128)} %get-tuple-element.725) | copy-start | bytes 589828 | tf_op jit(solution)/shard_map/while
  744.1 38.7 %collective-permute-start.1 = (bf16[1,384,768]{2,1,0:T(8,128)(2,1)S(1)}, bf16[1,384,768]{2,1,0:T(8,128)(2,1)S(1)}, u32[]{:S(2)}, u32[]{:S(2)}) collective-permute-start(bf16[1,384,768]{2,1,0:T(8,128)(2,1)S(1)} %fusion.69), channel_id=1, source_target_pairs={{32,0},{64,32},{96,64},{33,1},{65,33},{97,65},{34,2},{66,34},{98,6... | collective-permute-start | bytes 1769480 | tf_op jit(solution)/shard_map/while/body/eval_jaxpr/ppermute | solution.py:13
  782.7 0.7 copy-start.4
  783.4 1.2 copy-start.1
  783.4 92.0 %all-reduce.5.cloned.1.call-start = ((), (), s32[]{:S(2)}) async-start(), calls=%async_computation.5 | async-start | bytes 196608 | tf_op jit(solution)/shard_map/while/body/eval_jaxpr/psum | solution.py:29
  875.4 2.8 copy-start
  876.8 38.6 %copy-start.3 = (f32[768,64]{0,1:T(8,128)S(1)}, f32[768,64]{0,1:T(8,128)}, u32[]{:S(2)}) copy-start(f32[768,64]{0,1:T(8,128)} %get-tuple-element.725) | copy-start | bytes 589828 | tf_op jit(solution)/shard_map/while
  876.8 38.7 %collective-permute-start.1 = (bf16[1,384,768]{2,1,0:T(8,128)(2,1)S(1)}, bf16[1,384,768]{2,1,0:T(8,128)(2,1)S(1)}, u32[]{:S(2)}, u32[]{:S(2)}) collective-permute-start(bf16[1,384,768]{2,1,0:T(8,128)(2,1)S(1)} %fusion.69), channel_id=1, source_target_pairs={{32,0},{64,32},{96,64},{33,1},{65,33},{97,65},{34,2},{66,34},{98,6... | collective-permute-start | bytes 1769480 | tf_op jit(solution)/shard_map/while/body/eval_jaxpr/ppermute | solution.py:13
  915.4 0.7 copy-start.4
  916.1 1.2 copy-start.1
  916.1 92.0 %all-reduce.5.cloned.1.call-start = ((), (), s32[]{:S(2)}) async-start(), calls=%async_computation.5 | async-start | bytes 196608 | tf_op jit(solution)/shard_map/while/body/eval_jaxpr/psum | solution.py:29
  1008.2 2.8 copy-start
  1009.5 38.6 %copy-start.3 = (f32[768,64]{0,1:T(8,128)S(1)}, f32[768,64]{0,1:T(8,128)}, u32[]{:S(2)}) copy-start(f32[768,64]{0,1:T(8,128)} %get-tuple-element.725) | copy-start | bytes 589828 | tf_op jit(solution)/shard_map/while
  1009.5 38.7 %collective-permute-start.1 = (bf16[1,384,768]{2,1,0:T(8,128)(2,1)S(1)}, bf16[1,384,768]{2,1,0:T(8,128)(2,1)S(1)}, u32[]{:S(2)}, u32[]{:S(2)}) collective-permute-start(bf16[1,384,768]{2,1,0:T(8,128)(2,1)S(1)} %fusion.69), channel_id=1, source_target_pairs={{32,0},{64,32},{96,64},{33,1},{65,33},{97,65},{34,2},{66,34},{98,6... | collective-permute-start | bytes 1769480 | tf_op jit(solution)/shard_map/while/body/eval_jaxpr/ppermute | solution.py:13
  1048.2 0.7 copy-start.4
  1048.9 1.2 copy-start.1
  1048.9 91.7 %all-reduce.5.cloned.1.call-start = ((), (), s32[]{:S(2)}) async-start(), calls=%async_computation.5 | async-start | bytes 196608 | tf_op jit(solution)/shard_map/while/body/eval_jaxpr/psum | solution.py:29
  1140.6 2.8 copy-start
  1141.9 38.6 %copy-start.3 = (f32[768,64]{0,1:T(8,128)S(1)}, f32[768,64]{0,1:T(8,128)}, u32[]{:S(2)}) copy-start(f32[768,64]{0,1:T(8,128)} %get-tuple-element.725) | copy-start | bytes 589828 | tf_op jit(solution)/shard_map/while
  1142.0 38.7 %collective-permute-start.1 = (bf16[1,384,768]{2,1,0:T(8,128)(2,1)S(1)}, bf16[1,384,768]{2,1,0:T(8,128)(2,1)S(1)}, u32[]{:S(2)}, u32[]{:S(2)}) collective-permute-start(bf16[1,384,768]{2,1,0:T(8,128)(2,1)S(1)} %fusion.69), channel_id=1, source_target_pairs={{32,0},{64,32},{96,64},{33,1},{65,33},{97,65},{34,2},{66,34},{98,6... | collective-permute-start | bytes 1769480 | tf_op jit(solution)/shard_map/while/body/eval_jaxpr/ppermute | solution.py:13
  1180.6 0.7 copy-start.4
  1181.3 20.6 %reduce-scatter.3.cloned.1.call-start = ((), (), s32[]{:S(2)}) async-start(), calls=%async_computation.2 | async-start | bytes 294912 | tf_op jit(solution)/shard_map/reduce_scatter | solution.py:134
  1181.9 34.3 %reduce-scatter.5.cloned.1.call-start = ((), (), s32[]{:S(2)}) async-start(), calls=%async_computation.3 | async-start | bytes 294912 | tf_op jit(solution)/shard_map/reduce_scatter | solution.py:135
Sparse Core Ops, SparseCore 0:
  17.1 83.7 all-reduce.2
  120.0 82.8 all-reduce.2
  222.1 82.9 all-reduce.2
  323.9 82.9 all-reduce.2
  425.7 82.9 all-reduce.2
  527.9 82.8 all-reduce.4
  655.6 87.0 all-reduce.4
  788.4 86.9 all-reduce.4
  921.1 87.0 all-reduce.4
  1053.5 87.0 all-reduce.4
Sparse Core Ops, SparseCore 1:
  1184.7 17.2 reduce-scatter.2
  1204.6 11.5 reduce-scatter.4
where the time goes:
time: 1230 us; the launch traced here: 1220 us
  waiting for transfers between devices  952 us (77%)
  blocking collectives  160 us (13%)
  matrix products  31.7 us (3%)
  other arithmetic  23.4 us (2%)
  starting transfers between devices  22.9 us (2%)
  between operations  15.5 us (1%)
  loops' own time  13.7 us (1%)
    psum x10, waiting for transfers between devices, bottleneck_total(): return lax.psum(partial_value, 'tensor')  867 us
    psum x5, blocking collectives, backward_step(): norm_total = jnp.sqrt(lax.psum(squares, 'tensor'))  160 us
    ppermute x10, waiting for transfers between devices, shifted(): lax.ppermute(value, axis, [(source, source + steps) for source in range(l...  50 us
  transfers between devices with their start and end apart: 22, of which 17 were waited for; matrix products, arithmetic and copies ran while one was open for 1% of the time, Pallas kernels for 0%

commit v1 on v0

v1 whole, which is shorter than its diff:
```python
import jax
import jax.numpy as jnp
from jax import lax
from jax.sharding import PartitionSpec as P

SLOPE_C = 0.7978845608
CUBIC = 0.044715
BF = jnp.bfloat16
F32 = jnp.float32


def gelu_both(values):
    squared = values * values
    tangent = jnp.tanh(SLOPE_C * values * (1.0 + CUBIC * squared))
    value = 0.5 * values * (1.0 + tangent)
    slope = 0.5 * (1.0 + tangent) + 0.5 * values * (1.0 - tangent * tangent) * SLOPE_C * (
        1.0 + 3.0 * CUBIC * squared
    )
    return value, slope


def dot(a, b, ca, cb):
    return lax.dot_general(a, b, (((ca,), (cb,)), ((), ())), preferred_element_type=F32)


def shards(act_input, cotangent, lengths, clip_scale, adapt_down, adapt_up):
    layers = lax.axis_size("segment")
    cuts = lax.axis_size("tensor")
    seg = lax.axis_index("segment")
    core = lax.axis_index("dp")
    micro, slots, width = act_input.shape
    rank = adapt_down.shape[2]
    rows = micro * slots
    chunk = rows // cuts
    half = rank // 2
    down = adapt_down[0]
    up = adapt_up[0]
    down_t = down.T

    received = []
    for k in range(1, layers):
        dest = (seg + k) % layers
        message = jnp.where(dest > seg, up, down_t)
        received.append(
            lax.ppermute(message, "segment", [(i, (i + k) % layers) for i in range(layers)])
        )

    live = jnp.arange(slots, dtype=jnp.int32)[None, :] < lengths[:, None]
    masked = jnp.where(live[:, :, None], cotangent, jnp.zeros_like(cotangent))
    first = dot(act_input.reshape(rows, width), down, 1, 0)
    last = dot(masked.reshape(rows, width), up, 1, 1)
    partial = jnp.concatenate([first, last], axis=1).astype(BF).reshape(cuts, chunk, 2 * rank)
    parts = lax.all_to_all(partial, "tensor", 0, 0, tiled=True)
    summed = jnp.sum(parts.astype(F32), axis=0).astype(BF)

    grams = []
    for k in range(1, layers):
        lower = (seg - k) % layers < seg
        left = jnp.where(lower, received[k - 1][half:], up[:half])
        right = jnp.where(lower, down_t, received[k - 1])
        grams.append(dot(left, right, 1, 1))
    gram = jnp.concatenate(grams, axis=0).astype(BF)
    gram = jnp.concatenate([gram[:48], gram[48:]], axis=1)
    message = jnp.concatenate([summed, gram], axis=0)
    spread_out = jnp.broadcast_to(message[None], (layers * cuts,) + message.shape)
    gathered = lax.all_to_all(spread_out, ("segment", "tensor"), 0, 0, tiled=True)
    gathered = gathered.reshape(layers, cuts, chunk + 48, 2 * rank)
    both = gathered[:, :, :chunk].reshape(layers, rows, 2 * rank).astype(F32)
    packed = jnp.sum(gathered[:, :, chunk:].astype(F32), axis=1).astype(BF)
    packed = jnp.concatenate([packed[:, :, :rank], packed[:, :, rank:]], axis=1)

    def gram_of(i, j):
        a, b = (i - j) % layers - 1, (j - i) % layers - 1
        return jnp.concatenate(
            [packed[i, a * half : (a + 1) * half], packed[j, b * half : (b + 1) * half]], axis=0
        )

    hidden, slope_of = [], []
    for j in range(layers):
        bottle = both[j, :, :rank]
        for i in range(j):
            bottle = bottle + dot(hidden[i], gram_of(i, j), 1, 0)
        value, slope = gelu_both(bottle)
        hidden.append(value.astype(BF))
        slope_of.append(slope)
    slopes = [None] * layers
    for i in reversed(range(layers)):
        spread = both[i, :, rank:]
        for j in range(i + 1, layers):
            spread = spread + dot(slopes[j], gram_of(i, j), 1, 1)
        slopes[i] = (spread * slope_of[i]).astype(BF)

    hidden = jnp.stack(hidden).reshape(layers, micro, slots, rank)
    slopes = jnp.stack(slopes).reshape(layers, micro, slots, rank)
    mine_h = lax.dynamic_index_in_dim(hidden, seg, 0, keepdims=False)
    mine_s = lax.dynamic_index_in_dim(slopes, seg, 0, keepdims=False)

    up_each = jnp.einsum("etr,etd->erd", mine_h, masked, preferred_element_type=F32)
    down_each = jnp.einsum("etr,etd->erd", mine_s, act_input, preferred_element_type=F32)
    for k in range(1, layers):
        peer = (seg - k) % layers
        lower = peer < seg
        theirs_h = lax.dynamic_index_in_dim(hidden, peer, 0, keepdims=False)
        theirs_s = lax.dynamic_index_in_dim(slopes, peer, 0, keepdims=False)
        left = jnp.where(lower, mine_s, mine_h)
        right = jnp.where(lower, theirs_h, theirs_s)
        mix = jnp.einsum("etr,etq->erq", left, right, preferred_element_type=F32).astype(BF)
        extra = jnp.einsum("erq,qd->erd", mix, received[k - 1], preferred_element_type=F32)
        up_each = up_each + jnp.where(lower, 0.0, extra)
        down_each = down_each + jnp.where(lower, extra, 0.0)
    each = jnp.concatenate([down_each, up_each], axis=1)
    squares = jnp.sum(each * each, axis=(1, 2))

    cores = lax.axis_size("dp")
    local = width // cores
    theirs = lax.dynamic_slice_in_dim(each, (1 - core) * local, local, 2)
    ours = lax.dynamic_slice_in_dim(each, core * local, local, 2)
    swapped = lax.ppermute(theirs.astype(BF), "dp", [(i, 1 - i) for i in range(cores)])
    note = jnp.broadcast_to(jnp.repeat(squares, 64)[None], (cuts * cores, 128))
    notes = lax.all_to_all(note, ("tensor", "dp"), 0, 0, tiled=True)
    totals = jnp.sum(notes.reshape(cuts, cores, micro, 64), axis=0)[:, :, 0]
    factors = clip_scale[0] / (jnp.sqrt(totals) + 0.01)
    own = lax.dynamic_index_in_dim(factors, core, 0, keepdims=False)
    other = lax.dynamic_index_in_dim(factors, 1 - core, 0, keepdims=False)
    out = jnp.sum(own[:, None, None] * ours, axis=0) + jnp.sum(
        other[:, None, None] * swapped.astype(F32), axis=0
    )
    return (out[:rank].T[None], out[rank:][None])


def solution(mesh):
    return jax.shard_map(
        shards,
        mesh=mesh,
        in_specs=(
            P("dp", None, "tensor"),
            P("dp", None, "tensor"),
            P("dp"),
            P("segment"),
            P("segment", "tensor", None),
            P("segment", None, "tensor"),
        ),
        out_specs=(P("segment", ("tensor", "dp"), None), P("segment", None, ("tensor", "dp"))),
        check_vma=False,
    )
```

time: 1230 us -> 119 us (0.10)
  waiting for transfers between devices: 952 us -> 33.8 us
  blocking collectives: 160 us -> 0 us
  local copies, waits for them, and re-layouts: 4.57 us -> 25 us
  other arithmetic: 23.4 us -> 7.76 us
  loops' own time: 13.7 us -> 0 us
  between operations: 15.5 us -> 1.88 us
    psum x10 -> x0, waiting for transfers between devices: 867 us -> none  [bottleneck_total(): return lax.psum(partial_value, 'tensor')]
    psum x5 -> x0, blocking collectives: 160 us -> none  [backward_step(): norm_total = jnp.sqrt(lax.psum(squares, 'tensor'))]
    ppermute x10 -> x4, waiting for transfers between devices: 50 us -> 0.05 us  [the longest x3 0.05 us: shards(): lax.ppermute(message, 'segment', [(i, (i + k) % layers) for i in range(la...]
    all_to_all x0 -> x3, waiting for transfers between devices: none -> 33.8 us  [the longest x1 20.6 us: shards(): lax.all_to_all(spread_out, ('segment', 'tensor'), 0, 0, tiled=True)]
    reduce_scatter x2 -> x0, waiting for transfers between devices: 33.8 us -> none  [the longest x1 19.4 us: shards(): lax.psum_scatter(total_down, 'dp', scatter_dimension=0, tiled=True)]
    all_to_all x0 -> x3, starting transfers between devices: none -> 20.5 us  [the longest x1 7.77 us: shards(): parts = lax.all_to_all(partial, 'tensor', 0, 0, tiled=True)]
    ppermute x10 -> x4, starting transfers between devices: 22.8 us -> 6.76 us  [the longest x3 6.33 us: shards(): lax.ppermute(message, 'segment', [(i, (i + k) % layers) for i in range(la...]
    another operation x2 -> x0, loops' own time: 13.7 us -> none  [the longest x1 13.5 us: shards(): lax.fori_loop(0, step_count, backward_step, start_state)]
  transfers between devices with their start and end apart: 22 -> 7, of which waited for: 17 -> 3; matrix products, arithmetic and copies ran while one was open for 1% -> 5% of each run, Pallas kernels for 0% -> 0%
where the time goes in v1:
time: 119 us; the launch traced here: 118 us
  waiting for transfers between devices  33.8 us (28%)
  starting transfers between devices  27.2 us (23%)
  local copies, waits for them, and re-layouts  25 us (21%)
  matrix products  22.4 us (19%)
  other arithmetic  7.76 us (7%)
  between operations  1.88 us (2%)
    all_to_all x1, waiting for transfers between devices, shards(): lax.all_to_all(spread_out, ('segment', 'tensor'), 0, 0, tiled=True)  20.6 us
    dot_general x17, matrix products, dot(): lax.dot_general(a, b, (((ca,), (cb,)), ((), ())), preferred_element_type=...  14.8 us
    unnamed x60, local copies, waits for them, and re-layouts  14.5 us
    all_to_all x1, starting transfers between devices, shards(): parts = lax.all_to_all(partial, 'tensor', 0, 0, tiled=True)  7.77 us
    all_to_all x1, starting transfers between devices, shards(): notes = lax.all_to_all(note, ('tensor', 'dp'), 0, 0, tiled=True)  7.19 us
    all_to_all x1, waiting for transfers between devices, shards(): parts = lax.all_to_all(partial, 'tensor', 0, 0, tiled=True)  6.66 us
    all_to_all x1, waiting for transfers between devices, shards(): notes = lax.all_to_all(note, ('tensor', 'dp'), 0, 0, tiled=True)  6.51 us
    ppermute x3, starting transfers between devices, shards(): lax.ppermute(message, 'segment', [(i, (i + k) % layers) for i in range(la...  6.33 us
  transfers between devices with their start and end apart: 7, of which 3 were waited for; matrix products, arithmetic and copies ran while one was open for 5% of the time, Pallas kernels for 0%

profile of v1, /device:TPU:1, one launch (start us, length us, event | category | flops | bytes accessed | tf_op | source)
XLA Modules:
  0.0 118.0 jit_solution(6707603361351994862)
XLA Ops:
  0.7 1.1 bitcast_select_fusion.14
  1.7 3.7 %collective-permute-start.1 = (bf16[64,768]{1,0:T(8,128)(2,1)S(1)}, bf16[64,768]{1,0:T(8,128)(2,1)S(1)}, u32[]{:S(2)}, u32[]{:S(2)}) collective-permute-start(bf16[64,768]{1,0:T(8,128)(2,1)S(1)} %get-tuple-element.19), channel_id=1, source_target_pairs={{0,64},{32,96},{64,0},{96,32},{1,65},{33,97},{65,1},{97,33},{2,66}... | collective-permute-start | bytes 294920 | tf_op jit(solution)/shard_map/ppermute | solution.py:45
  5.7 2.4 %collective-permute-start.2 = (bf16[64,768]{1,0:T(8,128)(2,1)S(1)}, bf16[64,768]{1,0:T(8,128)(2,1)S(1)}, u32[]{:S(2)}, u32[]{:S(2)}) collective-permute-start(bf16[64,768]{1,0:T(8,128)(2,1)S(1)} %get-tuple-element.20), channel_id=1, source_target_pairs={{0,96},{32,0},{64,32},{96,64},{1,97},{33,1},{65,33},{97,65},{2,98}... | collective-permute-start | bytes 294920 | tf_op jit(solution)/shard_map/ppermute | solution.py:45
  8.1 0.7 iota_compare_fusion.2
  8.8 1.5 %broadcast_select_fusion = bf16[2,384,768]{2,1,0:T(8,128)(2,1)S(1)} fusion(bf16[2,384,768]{2,1,0:T(8,128)(2,1)} %param.7, pred[2,384]{1,0:T(4,128)(4,1)S(1)} %iota_compare_fusion.2), kind=kLoop, calls=%fused_computation | loop fusion | flops 589824 | bytes 2360064 | tf_op jit(solution)/shard_map/jit(_where)/select_n | solution.py:49
  11.6 0.8 pad_maximum_fusion.1
  12.4 7.8 %all-to-all-start = ((bf16[16,48,128]{2,1,0:T(8,128)(2,1)}), bf16[16,48,128]{2,1,0:T(8,128)(2,1)S(1)}, u32[]{:S(2)}, u32[]{:S(2)}) async-start(bf16[16,48,128]{2,1,0:T(8,128)(2,1)} %pad_maximum_fusion.1), calls=%async_computation | async-start | bytes 393216 | tf_op jit(solution)/shard_map/all_to_all | solution.py:53
  20.8 6.7 %all-to-all-done = bf16[16,48,128]{2,1,0:T(8,128)(2,1)S(1)} async-done(((bf16[16,48,128]{2,1,0:T(8,128)(2,1)}), bf16[16,48,128]{2,1,0:T(8,128)(2,1)S(1)}, u32[]{:S(2)}, u32[]{:S(2)}) %all-to-all-start) | async-done | bytes 196640 | tf_op jit(solution)/shard_map/all_to_all | solution.py:53
  27.5 1.3 %broadcast_in_dim.50 = bf16[64,96,128]{2,1,0:T(8,128)(2,1)} broadcast(bf16[96,128]{1,0:T(8,128)(2,1)S(1)} %fusion.106), dimensions={1,2} | broadcast | bytes 1597440 | tf_op jit(solution)/shard_map/broadcast_in_dim | solution.py:65
  28.9 5.5 %all-to-all-start.1 = ((bf16[64,96,128]{2,1,0:T(8,128)(2,1)}), bf16[64,96,128]{2,1,0:T(8,128)(2,1)}, u32[]{:S(2)}, u32[]{:S(2)}) async-start(bf16[64,96,128]{2,1,0:T(8,128)(2,1)} %broadcast_in_dim.50), calls=%async_computation.1 | async-start | bytes 3145728 | tf_op jit(solution)/shard_map/all_to_all | solution.py:66
  35.1 20.6 %all-to-all-done.1 = bf16[64,96,128]{2,1,0:T(8,128)(2,1)} async-done(((bf16[64,96,128]{2,1,0:T(8,128)(2,1)}), bf16[64,96,128]{2,1,0:T(8,128)(2,1)}, u32[]{:S(2)}, u32[]{:S(2)}) %all-to-all-start.1) | async-done | bytes 1572896 | tf_op jit(solution)/shard_map/all_to_all | solution.py:66
  55.7 1.6 %slice_reduce_fusion = (bf16[4,48,128]{2,1,0:T(8,128)(2,1)S(1)}, bf16[4,16,48,128]{3,2,1,0:T(8,128)(2,1)S(1)}) fusion(bf16[4,16,96,128]{3,2,1,0:T(8,128)(2,1)} %bitcast.10), kind=kLoop, calls=%fused_computation.37 | loop fusion | flops 368640 | bytes 2408448 | tf_op jit(solution)/shard_map/reduce_sum | solution.py:69
  57.2 0.7 slice_bitcast_fusion.5
  58.2 1.8 %fusion.132 = (f32[1,768,64]{2,1,0:T(8,128)S(1)}, f32[1,768,64]{2,1,0:T(8,128)}, f32[1,768,64]{2,1,0:T(8,128)}, f32[1,768,64]{2,1,0:T(8,128)}, f32[1,768,64]{2,1...) fusion(f32[4,768,128]{2,1,0:T(8,128)S(1)} %bitcast_convert_fusion), kind=kLoop, calls=%fused_computation.186 | loop fusion | bytes 3145728 | tf_op jit(solution)/shard_map/slice | solution.py:88
  60.0 1.1 copy.76
  61.2 1.8 %copy.75 = f32[1,768,64]{1,2,0:T(8,128)} copy(f32[1,768,64]{2,1,0:T(8,128)} %get-tuple-element.7) | data formatting | bytes 393216
  63.0 1.8 %copy.77 = f32[1,768,64]{1,2,0:T(8,128)} copy(f32[1,768,64]{2,1,0:T(8,128)} %get-tuple-element.5) | data formatting | bytes 393216
  64.9 1.8 %copy.78 = f32[1,768,64]{1,2,0:T(8,128)} copy(f32[1,768,64]{2,1,0:T(8,128)} %get-tuple-element.11) | data formatting | bytes 393216
  66.7 1.8 %copy.74 = f32[1,768,64]{1,2,0:T(8,128)} copy(f32[1,768,64]{2,1,0:T(8,128)} %get-tuple-element.8) | data formatting | bytes 393216
  68.5 1.8 %copy.73 = f32[1,768,64]{1,2,0:T(8,128)} copy(f32[1,768,64]{2,1,0:T(8,128)} %get-tuple-element.9) | data formatting | bytes 393216
  70.3 0.8 copy.72
  71.2 1.9 %multiply_convert_fusion.3 = (bf16[768,64]{0,1:T(8,128)(2,1)S(1)}, f32[768,64]{0,1:T(8,128)}) fusion(bf16[32,64]{1,0:T(8,128)(2,1)S(1)} %get-tuple-element.29, bf16[32,64]{1,0:T(8,128)(2,1)S(1)} %get-tuple-element.30, bf16[1,768,64]{1,2,0:T(8,128)(2,1)S(1)} %multiply_convert_fusion, f32[1,768,64]{1,2,0:T(8,128)} %copy.77), kind=kOutput, calls=%fused_computation.55 | convolution fusion | flops 6799360 | bytes 598016 | tf_op jit(solution)/shard_map/dot_general | solution.py:23
  73.1 0.7 stack.36
  74.4 1.2 %convolution_add_fusion.8 = f32[768,64]{0,1:T(8,128)S(1)} fusion(f32[1,768,64]{1,2,0:T(8,128)} %copy.78, bf16[1,768,64]{1,2,0:T(8,128)(2,1)S(1)} %multiply_convert_fusion, bf16[32,64]{1,0:T(8,128)(2,1)S(1)} %get-tuple-element.24, bf16[32,64]{1,0:T(8,128)(2,1)S(1)} %get-tuple-element.21), kind=kOutput, calls=%fused_computation.14 | convolution fusion | flops 6356992 | bytes 499712 | tf_op jit(solution)/shard_map/dot_general | solution.py:23
  75.6 1.7 %multiply_convert_fusion.2 = (bf16[768,64]{0,1:T(8,128)(2,1)S(1)}, f32[768,64]{0,1:T(8,128)}) fusion(f32[768,64]{0,1:T(8,128)S(1)} %convolution_add_fusion.8, bf16[768,64]{0,1:T(8,128)(2,1)S(1)} %get-tuple-element.35, bf16[32,64]{1,0:T(8,128)(2,1)} %get-tuple-element.27, bf16[32,64]{1,0:T(8,128)(2,1)} %get-tuple-element.28), kind=kOutput, calls=%fused_computation.53 | convolution fusion | flops 6799360 | bytes 598016 | tf_op jit(solution)/shard_map/dot_general | solution.py:23
  77.3 0.7 stack.37
  78.5 1.3 %multiply_convert_fusion.1 = (bf16[768,64]{0,1:T(8,128)(2,1)S(1)}, bf16[768,64]{0,1:T(8,128)(2,1)S(1)}) fusion(f32[1,768,64]{1,2,0:T(8,128)} %copy.74, f32[768,64]{0,1:T(8,128)S(1)} %convolution_add_fusion.9, bf16[768,64]{0,1:T(8,128)(2,1)S(1)} %get-tuple-element.37, bf16[32,64]{1,0:T(8,128)(2,1)} %get-tuple-element.26, bf16[32,64]{1,0:T(8,128)(2,1)} %get-tuple-element.25), kind=kOutput, calls=%fused_computation.51 | convolution fusion | flops 7340032 | bytes 696320 | tf_op jit(solution)/shard_map/dot_general | solution.py:23
  79.8 0.7 stack.33
  80.5 1.3 %fusion.3 = bf16[768,64]{0,1:T(8,128)(2,1)S(1)} fusion(bf16[768,64]{0,1:T(8,128)(2,1)} %copy-done.15, f32[1,768,64]{1,2,0:T(8,128)} %copy.73, f32[768,64]{0,1:T(8,128)} %get-tuple-element.38, bf16[32,64]{1,0:T(8,128)(2,1)} %get-tuple-element.26, bf16[32,64]{1,0:T(8,128)(2,1)} %get-tuple-element.25), kind=kOutput, calls=%fused_computation.18 | convolution fusion | flops 7241728 | bytes 598016 | tf_op jit(solution)/shard_map/dot_general | solution.py:23
  81.8 0.7 stack.32
  82.5 1.6 %convolution_add_fusion.4 = f32[768,64]{0,1:T(8,128)} fusion(bf16[768,64]{0,1:T(8,128)(2,1)S(1)} %fusion.3, f32[1,768,64]{1,2,0:T(8,128)S(1)} %copy-done.3, bf16[32,64]{1,0:T(8,128)(2,1)} %get-tuple-element.27, bf16[32,64]{1,0:T(8,128)(2,1)} %get-tuple-element.28), kind=kOutput, calls=%fused_computation.9 | convolution fusion | flops 6356992 | bytes 499712 | tf_op jit(solution)/shard_map/dot_general | solution.py:23
  84.2 1.2 %fusion.4 = bf16[768,64]{0,1:T(8,128)(2,1)S(1)} fusion(f32[768,64]{0,1:T(8,128)} %convolution_add_fusion.4, bf16[768,64]{0,1:T(8,128)(2,1)S(1)} %copy-done.16, f32[768,64]{0,1:T(8,128)} %get-tuple-element.36, bf16[32,64]{1,0:T(8,128)(2,1)} %get-tuple-element.22, bf16[32,64]{1,0:T(8,128)(2,1)} %get-tuple-element.23), kind=kOutput, calls=%fused_computation.19 | convolution fusion | flops 7241728 | bytes 598016 | tf_op jit(solution)/shard_map/dot_general | solution.py:23
  85.6 0.9 convolution_add_fusion.1
  86.6 1.8 %fusion.5 = bf16[768,64]{0,1:T(8,128)(2,1)} fusion(f32[768,64]{0,1:T(8,128)S(1)} %convolution_add_fusion.1, bf16[768,64]{0,1:T(8,128)(2,1)} %copy-done.15, f32[1,768,64]{1,2,0:T(8,128)S(1)} %copy.76, bf16[32,64]{1,0:T(8,128)(2,1)} %get-tuple-element.31, bf16[32,64]{1,0:T(8,128)(2,1)} %get-tuple-element.32), kind=kOutput, calls=%fused_computation.20 | convolution fusion | flops 7241728 | bytes 598016 | tf_op jit(solution)/shard_map/dot_general | solution.py:23
  88.4 0.9 stack.30
  89.3 0.7 copy_dynamic-update-slice_fusion.6
  90.0 0.7 copy_dynamic-update-slice_fusion.5
  91.4 0.7 copy_dynamic-update-slice_fusion
  92.1 0.7 copy-done.2
  92.8 1.3 %fusion.6 = f32[2,64,768]{2,1,0:T(8,128)S(1)} fusion(bf16[64,768]{1,0:T(8,128)(2,1)} %copy-done.14, bf16[4,2,384,64]{2,3,1,0:T(8,128)(2,1)} %get-tuple-element.40, s32[]{:T(128)S(6)} %select_n.236, bf16[4,2,384,64]{2,3,1,0:T(8,128)(2,1)S(1)} %get-tuple-element.39, pred[]{:T(512)S(6)} %lt.95, s32[]{:T(128)S(6)} %select_n.231), kind=kOutput, calls=%fused_computation.24 | convolution fusion | flops 18980864 | bytes 886784 | tf_op jit(solution)/shard_map/erq,qd->erd/dot_general | solution.py:108
  94.2 1.4 %fusion.7 = f32[2,64,768]{2,1,0:T(8,128)S(1)} fusion(bf16[64,768]{1,0:T(8,128)(2,1)} %copy-done.11, bf16[4,2,384,64]{2,3,1,0:T(8,128)(2,1)} %get-tuple-element.40, s32[]{:T(128)S(6)} %select_n.244, bf16[4,2,384,64]{2,3,1,0:T(8,128)(2,1)} %copy-done.2, pred[]{:T(512)S(6)} %lt.98, s32[]{:T(128)S(6)} %select_n.231), kind=kOutput, calls=%fused_computation.25 | convolution fusion | flops 18980864 | bytes 886784 | tf_op jit(solution)/shard_map/erq,qd->erd/dot_general | solution.py:108
  95.6 2.2 %fusion.8 = f32[2,64,768]{2,1,0:T(8,128)} fusion(bf16[64,768]{1,0:T(8,128)(2,1)S(1)} %copy-done.13, bf16[4,2,384,64]{2,3,1,0:T(8,128)(2,1)} %get-tuple-element.40, s32[]{:T(128)S(6)} %select_n.252, bf16[4,2,384,64]{2,3,1,0:T(8,128)(2,1)} %copy-done.2, pred[]{:T(512)S(6)} %lt.101, s32[]{:T(128)S(6)} %select_n.231), kind=kOutput, calls=%fused_computation.26 | convolution fusion | flops 18980864 | bytes 886784 | tf_op jit(solution)/shard_map/erq,qd->erd/dot_general | solution.py:108
  97.8 1.4 %select_add_fusion = f32[2,64,768]{2,1,0:T(8,128)S(1)} fusion(f32[2,64,768]{2,1,0:T(8,128)} %fusion.8, f32[2,64,768]{2,1,0:T(8,128)S(1)} %fusion.7, f32[2,64,768]{2,1,0:T(8,128)S(1)} %fusion.6, pred[]{:T(512)S(6)} %lt.101, pred[]{:T(512)S(6)} %lt.98, pred[]{:T(512)S(6)} %lt.95, bf16[2,384,768]{2,1,0:T(8,128)(2,1)S(1)} %broadcast_select_fusion, ...), kind=kOutput, calls=%fused_computation.45 | convolution fusion | flops 76087296 | bytes 2850823 | tf_op jit(solution)/shard_map/etr,etd->erd/dot_general | solution.py:98
  99.2 1.2 %select_add_fusion.1 = f32[2,64,768]{2,1,0:T(8,128)S(1)} fusion(f32[2,64,768]{2,1,0:T(8,128)S(1)} %copy-done.1, f32[2,64,768]{2,1,0:T(8,128)S(1)} %fusion.7, f32[2,64,768]{2,1,0:T(8,128)S(1)} %fusion.6, pred[]{:T(512)S(6)} %lt.101, pred[]{:T(512)S(6)} %lt.98, pred[]{:T(512)S(6)} %lt.95, bf16[2,384,768]{2,1,0:T(8,128)(2,1)S(1)} %copy-done, ...), kind=kOutput, calls=%fused_computation.46 | convolution fusion | flops 76087296 | bytes 2850823 | tf_op jit(solution)/shard_map/etr,etd->erd/dot_general | solution.py:99
  101.4 7.2 %all-to-all-start.2 = ((f32[32,1,128]{2,1,0:T(1,128)}), f32[32,1,128]{2,1,0:T(1,128)S(1)}, u32[]{:S(2)}, u32[]{:S(2)}) async-start(f32[32,1,128]{2,1,0:T(1,128)} %broadcast_in_dim.54), calls=%async_computation.2 | async-start | bytes 32768 | tf_op jit(solution)/shard_map/all_to_all | solution.py:120
  109.1 6.5 %all-to-all-done.2 = f32[32,1,128]{2,1,0:T(1,128)S(1)} async-done(((f32[32,1,128]{2,1,0:T(1,128)}), f32[32,1,128]{2,1,0:T(1,128)S(1)}, u32[]{:S(2)}, u32[]{:S(2)}) %all-to-all-start.2) | async-done | bytes 16416 | tf_op jit(solution)/shard_map/all_to_all | solution.py:120
  116.1 0.7 reduce.9
  117.4 0.7 slice_bitcast_fusion
  (85 shorter events, 7.1 us)
Async XLA Ops:
  0.6 10.1 %copy-start = (bf16[2,384,768]{2,1,0:T(8,128)(2,1)S(1)}, bf16[2,384,768]{2,1,0:T(8,128)(2,1)}, u32[]{:S(2)}) copy-start(bf16[2,384,768]{2,1,0:T(8,128)(2,1)} %param.6) | copy-start | bytes 3538948
  1.7 18.5 %collective-permute-start.1 = (bf16[64,768]{1,0:T(8,128)(2,1)S(1)}, bf16[64,768]{1,0:T(8,128)(2,1)S(1)}, u32[]{:S(2)}, u32[]{:S(2)}) collective-permute-start(bf16[64,768]{1,0:T(8,128)(2,1)S(1)} %get-tuple-element.19), channel_id=1, source_target_pairs={{0,64},{32,96},{64,0},{96,32},{1,65},{33,97},{65,1},{97,33},{2,66}... | collective-permute-start | bytes 294920 | tf_op jit(solution)/shard_map/ppermute | solution.py:45
  5.4 15.1 %collective-permute-start = (bf16[64,768]{1,0:T(8,128)(2,1)S(1)}, bf16[64,768]{1,0:T(8,128)(2,1)S(1)}, u32[]{:S(2)}, u32[]{:S(2)}) collective-permute-start(bf16[64,768]{1,0:T(8,128)(2,1)S(1)} %get-tuple-element.18), channel_id=1, source_target_pairs={{0,32},{32,64},{64,96},{96,0},{1,33},{33,65},{65,97},{97,1},{2,34}... | collective-permute-start | bytes 294920 | tf_op jit(solution)/shard_map/ppermute | solution.py:45
  5.7 14.9 %collective-permute-start.2 = (bf16[64,768]{1,0:T(8,128)(2,1)S(1)}, bf16[64,768]{1,0:T(8,128)(2,1)S(1)}, u32[]{:S(2)}, u32[]{:S(2)}) collective-permute-start(bf16[64,768]{1,0:T(8,128)(2,1)S(1)} %get-tuple-element.20), channel_id=1, source_target_pairs={{0,96},{32,0},{64,32},{96,64},{1,97},{33,1},{65,33},{97,65},{2,98}... | collective-permute-start | bytes 294920 | tf_op jit(solution)/shard_map/ppermute | solution.py:45
  8.8 1.5 %copy-start.6 = (bf16[1,64,768]{2,1,0:T(8,128)(2,1)S(1)}, bf16[1,64,768]{2,1,0:T(8,128)(2,1)}, u32[]{:S(2)}) copy-start(bf16[1,64,768]{2,1,0:T(8,128)(2,1)} %param.11) | copy-start | bytes 294916
  10.3 0.9 copy-start.5
  12.4 15.0 %all-to-all-start = ((bf16[16,48,128]{2,1,0:T(8,128)(2,1)}), bf16[16,48,128]{2,1,0:T(8,128)(2,1)S(1)}, u32[]{:S(2)}, u32[]{:S(2)}) async-start(bf16[16,48,128]{2,1,0:T(8,128)(2,1)} %pad_maximum_fusion.1), calls=%async_computation | async-start | bytes 393216 | tf_op jit(solution)/shard_map/all_to_all | solution.py:53
  20.3 8.6 %copy-start.11 = (bf16[64,768]{1,0:T(8,128)(2,1)}, bf16[64,768]{1,0:T(8,128)(2,1)S(1)}, u32[]{:S(2)}) copy-start(bf16[64,768]{1,0:T(8,128)(2,1)S(1)} %collective-permute-done.1) | copy-start | bytes 294916
  20.4 8.4 %copy-start.14 = (bf16[64,768]{1,0:T(8,128)(2,1)}, bf16[64,768]{1,0:T(8,128)(2,1)S(1)}, u32[]{:S(2)}) copy-start(bf16[64,768]{1,0:T(8,128)(2,1)S(1)} %collective-permute-done) | copy-start | bytes 294916
  20.6 8.3 %copy-start.12 = (bf16[64,768]{1,0:T(8,128)(2,1)}, bf16[64,768]{1,0:T(8,128)(2,1)S(1)}, u32[]{:S(2)}) copy-start(bf16[64,768]{1,0:T(8,128)(2,1)S(1)} %collective-permute-done.2) | copy-start | bytes 294916
  28.9 26.8 %all-to-all-start.1 = ((bf16[64,96,128]{2,1,0:T(8,128)(2,1)}), bf16[64,96,128]{2,1,0:T(8,128)(2,1)}, u32[]{:S(2)}, u32[]{:S(2)}) async-start(bf16[64,96,128]{2,1,0:T(8,128)(2,1)} %broadcast_in_dim.50), calls=%async_computation.1 | async-start | bytes 3145728 | tf_op jit(solution)/shard_map/all_to_all | solution.py:66
  71.2 6.8 %copy-start.4 = (f32[1,768,64]{1,2,0:T(8,128)S(1)}, f32[1,768,64]{1,2,0:T(8,128)}, u32[]{:S(2)}) copy-start(f32[1,768,64]{1,2,0:T(8,128)} %copy.75) | copy-start | bytes 589828
  74.4 1.2 %copy-start.17 = (bf16[32,64]{1,0:T(8,128)(2,1)}, bf16[32,64]{1,0:T(8,128)(2,1)S(1)}, u32[]{:S(2)}) copy-start(bf16[32,64]{1,0:T(8,128)(2,1)S(1)} %get-tuple-element.21) | copy-start | bytes 12292
  74.4 1.2 %copy-start.18 = (bf16[32,64]{1,0:T(8,128)(2,1)}, bf16[32,64]{1,0:T(8,128)(2,1)S(1)}, u32[]{:S(2)}) copy-start(bf16[32,64]{1,0:T(8,128)(2,1)S(1)} %get-tuple-element.24) | copy-start | bytes 12292
  74.4 3.6 %copy-start.19 = (bf16[32,64]{1,0:T(8,128)(2,1)S(1)}, bf16[32,64]{1,0:T(8,128)(2,1)}, u32[]{:S(2)}) copy-start(bf16[32,64]{1,0:T(8,128)(2,1)} %get-tuple-element.31) | copy-start | bytes 12292
  74.4 3.6 %copy-start.20 = (bf16[32,64]{1,0:T(8,128)(2,1)S(1)}, bf16[32,64]{1,0:T(8,128)(2,1)}, u32[]{:S(2)}) copy-start(bf16[32,64]{1,0:T(8,128)(2,1)} %get-tuple-element.32) | copy-start | bytes 12292
  74.4 3.8 %copy-start.21 = (bf16[32,64]{1,0:T(8,128)(2,1)S(1)}, bf16[32,64]{1,0:T(8,128)(2,1)}, u32[]{:S(2)}) copy-start(bf16[32,64]{1,0:T(8,128)(2,1)} %get-tuple-element.22) | copy-start | bytes 12292
  74.4 3.8 %copy-start.22 = (bf16[32,64]{1,0:T(8,128)(2,1)S(1)}, bf16[32,64]{1,0:T(8,128)(2,1)}, u32[]{:S(2)}) copy-start(bf16[32,64]{1,0:T(8,128)(2,1)} %get-tuple-element.23) | copy-start | bytes 12292
  78.4 4.0 %copy-start.3 = (f32[1,768,64]{1,2,0:T(8,128)S(1)}, f32[1,768,64]{1,2,0:T(8,128)}, u32[]{:S(2)}) copy-start(f32[1,768,64]{1,2,0:T(8,128)} %copy.72) | copy-start | bytes 589828
  79.8 0.7 copy-start.15
  80.5 3.7 %copy-start.16 = (bf16[768,64]{0,1:T(8,128)(2,1)S(1)}, bf16[768,64]{0,1:T(8,128)(2,1)}, u32[]{:S(2)}) copy-start(bf16[768,64]{0,1:T(8,128)(2,1)} %copy-done.15) | copy-start | bytes 294916
  85.6 5.0 %copy-start.9 = (bf16[1,2,384,64]{2,1,3,0:T(2,128)(2,1)S(1)}, bf16[1,2,384,64]{2,1,3,0:T(2,128)(2,1)}, u32[]{:S(2)}) copy-start(bf16[1,2,384,64]{2,1,3,0:T(2,128)(2,1)} %stack.32) | copy-start | bytes 294916
  86.5 4.8 %copy-start.7 = (bf16[1,2,384,64]{2,1,3,0:T(2,128)(2,1)S(1)}, bf16[1,2,384,64]{2,1,3,0:T(2,128)(2,1)}, u32[]{:S(2)}) copy-start(bf16[1,2,384,64]{2,1,3,0:T(2,128)(2,1)} %stack.36) | copy-start | bytes 294916
  86.6 4.8 %copy-start.8 = (bf16[1,2,384,64]{2,1,3,0:T(2,128)(2,1)S(1)}, bf16[1,2,384,64]{2,1,3,0:T(2,128)(2,1)}, u32[]{:S(2)}) copy-start(bf16[1,2,384,64]{2,1,3,0:T(2,128)(2,1)} %stack.37) | copy-start | bytes 294916
  86.6 4.8 %copy-start.10 = (bf16[1,2,384,64]{2,1,3,0:T(2,128)(2,1)S(1)}, bf16[1,2,384,64]{2,1,3,0:T(2,128)(2,1)}, u32[]{:S(2)}) copy-start(bf16[1,2,384,64]{2,1,3,0:T(2,128)(2,1)} %stack.33) | copy-start | bytes 294916
  91.3 4.3 %copy-start.13 = (bf16[64,768]{1,0:T(8,128)(2,1)S(1)}, bf16[64,768]{1,0:T(8,128)(2,1)}, u32[]{:S(2)}) copy-start(bf16[64,768]{1,0:T(8,128)(2,1)} %copy-done.12) | copy-start | bytes 294916
  92.1 0.8 copy-start.2
  97.8 1.4 %copy-start.1 = (f32[2,64,768]{2,1,0:T(8,128)S(1)}, f32[2,64,768]{2,1,0:T(8,128)}, u32[]{:S(2)}) copy-start(f32[2,64,768]{2,1,0:T(8,128)} %fusion.8) | copy-start | bytes 1179652
  101.4 14.2 %all-to-all-start.2 = ((f32[32,1,128]{2,1,0:T(1,128)}), f32[32,1,128]{2,1,0:T(1,128)S(1)}, u32[]{:S(2)}, u32[]{:S(2)}) async-start(f32[32,1,128]{2,1,0:T(1,128)} %broadcast_in_dim.54), calls=%async_computation.2 | async-start | bytes 32768 | tf_op jit(solution)/shard_map/all_to_all | solution.py:120
  108.7 8.5 %collective-permute-start.3 = (bf16[2,128,384]{2,1,0:T(8,128)(2,1)S(1)}, bf16[2,128,384]{2,1,0:T(8,128)(2,1)S(1)}, u32[]{:S(2)}, u32[]{:S(2)}) collective-permute-start(bf16[2,128,384]{2,1,0:T(8,128)(2,1)S(1)} %fusion.15), channel_id=1, source_target_pairs={{0,1},{1,0},{2,3},{3,2},{4,5},{5,4},{6,7},{7,6},{8,9},{9,8},{10,11... | collective-permute-start | bytes 589832 | tf_op jit(solution)/shard_map/ppermute | solution.py:118

commit v2 on v1

v2 whole, which is shorter than its diff:
```python
import jax
import jax.numpy as jnp
from jax import lax
from jax.experimental import pallas as pl
from jax.experimental.pallas import tpu as pltpu
from jax.sharding import PartitionSpec as P

SLOPE_C = 0.7978845608
CUBIC = 0.044715
BF = jnp.bfloat16
F32 = jnp.float32
VMEM = pl.BlockSpec(memory_space=pltpu.VMEM)
SMEM = pl.BlockSpec(memory_space=pltpu.SMEM)
ANY = pl.BlockSpec(memory_space=pl.ANY)

LAYERS = 4
CUTS = 16
SLOTS = 384
WIDTH = 768
RANK = 64
HALF = RANK // 2
LANES = 2 * RANK
PIECE = SLOTS // CUTS
PACK = 48
LOCAL = WIDTH // 2


def dot(a, b, ca, cb):
    return lax.dot_general(a, b, (((ca,), (cb,)), ((), ())), preferred_element_type=F32)


def gelu_both(values):
    squared = values * values
    tangent = jnp.tanh(values * (SLOPE_C + SLOPE_C * CUBIC * squared))
    half = 0.5 + 0.5 * tangent
    slope = half + values * (0.5 - 0.5 * tangent * tangent) * (
        SLOPE_C + 3.0 * SLOPE_C * CUBIC * squared
    )
    return values * half, slope


PROJECT_STEPS = 2
PROJECT_ROWS = SLOTS // PROJECT_STEPS


def project_body(lengths, act, cot, down, up, out):
    base = pl.program_id(0) * PROJECT_ROWS
    rows = 2 * PROJECT_ROWS
    first = dot(act[...].reshape(rows, WIDTH), down[0], 1, 0)
    last = dot(cot[...].reshape(rows, WIDTH), up[0], 1, 1)
    first = jnp.concatenate([first[:PROJECT_ROWS], first[PROJECT_ROWS:]], axis=1)
    last = jnp.concatenate([last[:PROJECT_ROWS], last[PROJECT_ROWS:]], axis=1)
    slot = lax.broadcasted_iota(jnp.int32, (PROJECT_ROWS, LANES), 0) + base
    lane = lax.broadcasted_iota(jnp.int32, (PROJECT_ROWS, LANES), 1)
    last = jnp.where(slot < jnp.where(lane < RANK, lengths[0], lengths[1]), last, 0.0)
    for i in range(PROJECT_ROWS // PIECE):
        part = slice(i * PIECE, (i + 1) * PIECE)
        out[i] = jnp.concatenate([first[part], last[part]], axis=0).astype(BF)


def project(lengths, act, cot, down, up):
    block = pl.BlockSpec((2, PROJECT_ROWS, WIDTH), lambda i: (0, i, 0))
    return pl.pallas_call(
        project_body,
        grid=(PROJECT_STEPS,),
        in_specs=[
            SMEM,
            block,
            block,
            pl.BlockSpec((1, WIDTH, RANK), lambda i: (0, 0, 0)),
            pl.BlockSpec((1, RANK, WIDTH), lambda i: (0, 0, 0)),
        ],
        out_specs=pl.BlockSpec((CUTS // PROJECT_STEPS, 2 * PIECE, LANES), lambda i: (i, 0, 0)),
        out_shape=jax.ShapeDtypeStruct((CUTS, 2 * PIECE, LANES), BF),
        compiler_params=pltpu.CompilerParams(vmem_limit_bytes=16 << 20),
        cost_estimate=pl.CostEstimate(flops=150000000, bytes_accessed=2800000, transcendentals=0),
    )(lengths, act, cot, down, up)


def reduce_body(parts, up, down_t, one, two, three, out):
    seg = lax.axis_index("segment")
    total = parts[0].astype(F32)
    for i in range(1, CUTS):
        total = total + parts[i].astype(F32)
    pieces = []
    for k, other in ((1, one), (2, two), (3, three)):
        lower = seg >= k
        left = jnp.where(lower, other[HALF:], up[0, :HALF])
        right = jnp.where(lower, down_t[...], other[...])
        pieces.append(dot(left, right, 1, 1))
    grams = jnp.concatenate(pieces, axis=0)
    grams = jnp.concatenate([grams[:PACK], grams[PACK:]], axis=1)
    message = jnp.concatenate([total, grams], axis=0).astype(BF)
    for i in range(LAYERS * CUTS):
        out[i] = message


def reduce_parts(parts, up, down_t, peers):
    return pl.pallas_call(
        reduce_body,
        in_specs=[VMEM] * 6,
        out_specs=VMEM,
        out_shape=jax.ShapeDtypeStruct((LAYERS * CUTS, 2 * PIECE + PACK, LANES), BF),
        compiler_params=pltpu.CompilerParams(vmem_limit_bytes=16 << 20),
        cost_estimate=pl.CostEstimate(flops=10000000, bytes_accessed=2300000, transcendentals=0),
    )(parts, up, down_t, *peers)


def gradient_body(
    lengths, gathered, one, two, three, act_hbm, cot_hbm,
    theirs, ours, note,
    act, cot, first, last, hidden, slopes, steep, each, sems,
):
    seg = lax.axis_index("segment")
    core = lax.axis_index("dp")
    act_copy = pltpu.make_async_copy(act_hbm, act, sems.at[0])
    cot_copy = pltpu.make_async_copy(cot_hbm, cot, sems.at[1])
    act_copy.start()
    cot_copy.start()

    packed = []
    for layer in range(LAYERS):
        total = None
        for t in range(CUTS):
            at = layer * CUTS + t
            block = gathered[at, : 2 * PIECE].astype(F32)
            first[layer, t * PIECE : (t + 1) * PIECE] = block[:PIECE]
            last[layer, t * PIECE : (t + 1) * PIECE] = block[PIECE:]
            gram = gathered[at, 2 * PIECE :].astype(F32)
            total = gram if total is None else total + gram
        packed.append(jnp.concatenate([total[:, :RANK], total[:, RANK:]], axis=0))

    def gram_of(i, j):
        a, b = (i - j) % LAYERS - 1, (j - i) % LAYERS - 1
        gram = jnp.concatenate(
            [packed[i][a * HALF : (a + 1) * HALF], packed[j][b * HALF : (b + 1) * HALF]], axis=0
        )
        zero = jnp.zeros_like(gram)
        return jnp.concatenate(
            [jnp.concatenate([gram, zero], axis=1), jnp.concatenate([zero, gram], axis=1)], axis=0
        ).astype(BF)

    grams = {(i, j): gram_of(i, j) for j in range(LAYERS) for i in range(j)}

    for j in range(LAYERS):
        bottle = first[j]
        for i in range(j):
            bottle = bottle + dot(hidden[i], grams[i, j], 1, 0)
        value, slope = gelu_both(bottle)
        hidden[j] = value.astype(BF)
        steep[j] = slope
    for i in reversed(range(LAYERS)):
        spread = last[i]
        for j in range(i + 1, LAYERS):
            spread = spread + dot(slopes[j], grams[i, j], 1, 1)
        slopes[i] = (spread * steep[i]).astype(BF)

    slot = lax.broadcasted_iota(jnp.int32, (SLOTS, LANES), 0)
    lane = lax.broadcasted_iota(jnp.int32, (SLOTS, LANES), 1)
    live = slot < jnp.where(lane < RANK, lengths[0], lengths[1])
    mine_h = jnp.where(live, hidden[seg].astype(F32), 0.0).T.astype(BF)
    mine_s = slopes[seg].astype(F32).T.astype(BF)

    lefts = []
    for k in range(1, LAYERS):
        peer = lax.rem(seg + LAYERS - k, LAYERS)
        lower = seg >= k
        left = jnp.where(lower, mine_s, mine_h)
        right = jnp.where(lower, hidden[peer], slopes[peer])
        mix = dot(left, right, 1, 0)
        mix = jnp.concatenate([mix[:RANK, :RANK], mix[RANK:, RANK:]], axis=0)
        lefts.append(
            jnp.concatenate([jnp.where(lower, mix, 0.0), jnp.where(lower, 0.0, mix)], axis=0)
        )
    left = jnp.concatenate(lefts, axis=1).astype(BF)
    peers = jnp.concatenate([one[...], two[...], three[...]], axis=0)
    act_copy.wait()
    cot_copy.wait()
    each[...] = dot(left, peers, 1, 0)
    for e in range(2):
        rows = slice(e * RANK, (e + 1) * RANK)
        other = slice((2 + e) * RANK, (3 + e) * RANK)
        down_grad = each[rows] + dot(mine_s[rows], act[e], 1, 0)
        up_grad = each[other] + dot(mine_h[rows], cot[e], 1, 0)
        each[rows] = down_grad
        each[other] = up_grad
        square = jnp.sum(down_grad * down_grad + up_grad * up_grad)
        note[:, rows] = jnp.full((2 * CUTS, RANK), square, F32)
    keep = pl.multiple_of(core * LOCAL, 128)
    give = pl.multiple_of((1 - core) * LOCAL, 128)
    ours[...] = each[:, pl.ds(keep, LOCAL)]
    theirs[...] = each[:, pl.ds(give, LOCAL)].astype(BF)


def gradients(lengths, gathered, peers, act, cot):
    wide = (LAYERS, SLOTS, LANES)
    return pl.pallas_call(
        gradient_body,
        in_specs=[SMEM] + [VMEM] * 4 + [ANY] * 2,
        out_specs=[VMEM] * 3,
        out_shape=[
            jax.ShapeDtypeStruct((4 * RANK, LOCAL), BF),
            jax.ShapeDtypeStruct((4 * RANK, LOCAL), F32),
            jax.ShapeDtypeStruct((2 * CUTS, LANES), F32),
        ],
        scratch_shapes=[
            pltpu.VMEM((2, SLOTS, WIDTH), BF),
            pltpu.VMEM((2, SLOTS, WIDTH), BF),
            pltpu.VMEM(wide, F32),
            pltpu.VMEM(wide, F32),
            pltpu.VMEM(wide, BF),
            pltpu.VMEM(wide, BF),
            pltpu.VMEM(wide, F32),
            pltpu.VMEM((4 * RANK, WIDTH), F32),
            pltpu.SemaphoreType.DMA((2,)),
        ],
        compiler_params=pltpu.CompilerParams(vmem_limit_bytes=32 << 20),
        cost_estimate=pl.CostEstimate(
            flops=600000000, bytes_accessed=5000000, transcendentals=200000
        ),
    )(lengths, gathered, *peers, act, cot)


def scale_body(clip, notes, ours, swapped, out_down, out_up):
    core = lax.axis_index("dp")
    row = lax.broadcasted_iota(jnp.int32, (2 * CUTS, LANES), 0)
    is_own = lax.rem(row, 2) == core
    values = notes[...]

    def factors(picked):
        total = jnp.sum(jnp.where(picked, values, 0.0), axis=0, keepdims=True)
        return clip[0] / (jnp.sqrt(total) + 0.01)

    own = factors(is_own)
    other = factors(jnp.logical_not(is_own))

    def combined(start):
        total = None
        for e in range(2):
            rows = slice(start + e * RANK, start + (e + 1) * RANK)
            at = slice(e * RANK, e * RANK + 1)
            term = own[:, at] * ours[rows] + other[:, at] * swapped[rows].astype(F32)
            total = term if total is None else total + term
        return total

    out_down[0] = combined(0).T
    out_up[0] = combined(2 * RANK)


def scaled(clip, notes, ours, swapped):
    return pl.pallas_call(
        scale_body,
        in_specs=[SMEM] + [VMEM] * 3,
        out_specs=[VMEM] * 2,
        out_shape=[
            jax.ShapeDtypeStruct((1, LOCAL, RANK), F32),
            jax.ShapeDtypeStruct((1, RANK, LOCAL), F32),
        ],
        compiler_params=pltpu.CompilerParams(vmem_limit_bytes=16 << 20),
        cost_estimate=pl.CostEstimate(flops=300000, bytes_accessed=900000, transcendentals=0),
    )(clip, notes, ours, swapped)


def shards(act_input, cotangent, lengths, clip_scale, adapt_down, adapt_up):
    seg = lax.axis_index("segment")
    up = adapt_up[0]
    down_t = adapt_down[0].T
    peers = []
    for k in range(1, LAYERS):
        message = jnp.where(seg + k < LAYERS, up, down_t)
        peers.append(
            lax.ppermute(message, "segment", [(i, (i + k) % LAYERS) for i in range(LAYERS)])
        )
    partial = project(lengths, act_input, cotangent, adapt_down, adapt_up)
    parts = lax.all_to_all(partial, "tensor", 0, 0, tiled=True)
    message = reduce_parts(parts, adapt_up, down_t, peers)
    gathered = lax.all_to_all(message, ("segment", "tensor"), 0, 0, tiled=True)
    theirs, ours, note = gradients(lengths, gathered, peers, act_input, cotangent)
    swapped = lax.ppermute(theirs, "dp", [(0, 1), (1, 0)])
    notes = lax.all_to_all(note, ("tensor", "dp"), 0, 0, tiled=True)
    return scaled(clip_scale, notes, ours, swapped)


def solution(mesh):
    return jax.shard_map(
        shards,
        mesh=mesh,
        in_specs=(
            P("dp", None, "tensor"),
            P("dp", None, "tensor"),
            P("dp"),
            P("segment"),
            P("segment", "tensor", None),
            P("segment", None, "tensor"),
        ),
        out_specs=(P("segment", ("tensor", "dp"), None), P("segment", None, ("tensor", "dp"))),
        check_vma=False,
    )
```

time: 119 us -> 77.1 us (0.65)
  blocking collectives: 0 us -> 30.8 us
  waiting for transfers between devices: 33.8 us -> 9.7 us
  matrix products: 22.4 us -> 0 us
  local copies, waits for them, and re-layouts: 25 us -> 5.93 us
  Pallas kernels: 0 us -> 7.76 us
  other arithmetic: 7.76 us -> 0.03 us
  starting transfers between devices: 27.2 us -> 21.1 us
    all_to_all x0 -> x1, blocking collectives: none -> 30.8 us  [shards(): gathered = lax.all_to_all(message, ('segment', 'tensor'), 0, 0, tiled=True)]
    dot_general x22 -> x0, matrix products: 22.4 us -> none  [the longest x17 14.8 us: dot(): lax.dot_general(a, b, (((ca,), (cb,)), ((), ())), preferred_element_type=...]
    all_to_all x1 -> x0, waiting for transfers between devices: 20.6 us -> none  [shards(): lax.all_to_all(spread_out, ('segment', 'tensor'), 0, 0, tiled=True)]
    unnamed x60 -> x19, local copies, waits for them, and re-layouts: 14.5 us -> 5.17 us
    pallas_call x0 -> x4, Pallas kernels: none -> 7.76 us  [the longest x1 4.26 us: gradients(): pl.pallas_call(gradient_body, in_specs=[SMEM] + [VMEM] * 4 + [ANY] * 2, o...]
    all_to_all x1, waiting for transfers between devices: 6.66 us -> 0.01 us  [shards(): parts = lax.all_to_all(partial, 'tensor', 0, 0, tiled=True)]
    all_to_all x1 -> x0, starting transfers between devices: 5.52 us -> none  [shards(): lax.all_to_all(spread_out, ('segment', 'tensor'), 0, 0, tiled=True)]
    another operation x8 -> x0, local copies, waits for them, and re-layouts: 4.33 us -> none  [the longest x4 2.29 us: shards(): slopes = jnp.stack(slopes).reshape(layers, micro, slots, rank)]
  transfers between devices with their start and end apart: 7 -> 6, of which waited for: 3 -> 3; matrix products, arithmetic and copies ran while one was open for 5% -> 0% of each run, Pallas kernels for 0% -> 0%
where the time goes in v2:
time: 77.1 us; the launch traced here: 76.7 us
  blocking collectives  30.8 us (40%)
  starting transfers between devices  21.1 us (27%)
  waiting for transfers between devices  9.7 us (13%)
  Pallas kernels  7.76 us (10%)
  local copies, waits for them, and re-layouts  5.93 us (8%)
  between operations  1.39 us (2%)
    all_to_all x1, blocking collectives, shards(): gathered = lax.all_to_all(message, ('segment', 'tensor'), 0, 0, tiled=True)  30.8 us
    all_to_all x1, starting transfers between devices, shards(): parts = lax.all_to_all(partial, 'tensor', 0, 0, tiled=True)  8.6 us
    all_to_all x1, waiting for transfers between devices, shards(): notes = lax.all_to_all(note, ('tensor', 'dp'), 0, 0, tiled=True)  6.22 us
    unnamed x19, local copies, waits for them, and re-layouts  5.17 us
    ppermute x3, starting transfers between devices, shards(): lax.ppermute(message, 'segment', [(i, (i + k) % LAYERS) for i in range(LA...  4.89 us
    pallas_call x1, Pallas kernels, gradients(): pl.pallas_call(gradient_body, in_specs=[SMEM] + [VMEM] * 4 + [ANY] * 2, o...  4.26 us
    ppermute x1, starting transfers between devices, shards(): swapped = lax.ppermute(theirs, 'dp', [(0, 1), (1, 0)])  3.97 us
    all_to_all x1, starting transfers between devices, shards(): notes = lax.all_to_all(note, ('tensor', 'dp'), 0, 0, tiled=True)  3.61 us
  transfers between devices with their start and end apart: 6, of which 3 were waited for; matrix products, arithmetic and copies ran while one was open for 0% of the time, Pallas kernels for 0%

profile of v2, /device:TPU:1, one launch (start us, length us, event | category | flops | bytes accessed | tf_op | source)
XLA Modules:
  0.0 76.7 jit_solution(902575571473141048)
XLA Ops:
  0.6 1.1 %copy.10.down = bf16[1,768,64]{2,1,0:T(8,128)(2,1)S(1)} copy(bf16[1,768,64]{1,2,0:T(8,128)(2,1)} %param.10) | data formatting | bytes 196608 | tf_op args[4]
  1.7 0.0 copy-start
  1.7 1.3 %copy-done = bf16[2,384,768]{2,1,0:T(8,128)(2,1)S(1)} copy-done((bf16[2,384,768]{2,1,0:T(8,128)(2,1)S(1)}, bf16[2,384,768]{2,1,0:T(8,128)(2,1)}, u32[]{:S(2)}) %copy-start) | copy-done | bytes 1179672
  3.0 0.0 copy-start.2
  3.0 1.3 %copy-done.2 = bf16[2,384,768]{2,1,0:T(8,128)(2,1)S(1)} copy-done((bf16[2,384,768]{2,1,0:T(8,128)(2,1)S(1)}, bf16[2,384,768]{2,1,0:T(8,128)(2,1)}, u32[]{:S(2)}) %copy-start.2) | copy-done | bytes 1179672
  4.2 0.0 copy-start.4
  4.2 0.9 %copy-done.4 = bf16[1,64,768]{2,1,0:T(8,128)(2,1)S(1)} copy-done((bf16[1,64,768]{2,1,0:T(8,128)(2,1)S(1)}, bf16[1,64,768]{2,1,0:T(8,128)(2,1)}, u32[]{:S(2)}) %copy-start.4) | copy-done | bytes 98328
  5.1 0.0 copy-start.7
  5.1 0.7 copy-done.7
  5.8 0.0 copy-start.5
  5.8 0.0 copy-start.6
  5.8 2.4 %shard_map.77 = bf16[16,48,128]{2,1,0:T(8,128)(2,1)} custom-call(s32[2]{0:T(128)S(1)} %copy-done.7, bf16[2,384,768]{2,1,0:T(8,128)(2,1)S(1)} %copy-done, bf16[2,384,768]{2,1,0:T(8,128)(2,1)S(1)} %copy-done.2, bf16[1,768,64]{2,1,0:T(8,128)(2,1)S(1)} %copy.10.down, bf16[1,64,768]{2,1,0:T(8,128)(2,1)S(1)} %copy-done.4), custom_call_target="tpu_custom_call" | custom-call | flops 150000000 | bytes 2800000 | tf_op jit(solution)/shard_map/pallas_call | solution.py:63
  8.2 8.6 %all-to-all-start = ((bf16[16,48,128]{2,1,0:T(8,128)(2,1)}), bf16[16,48,128]{2,1,0:T(8,128)(2,1)S(1)}, u32[]{:S(2)}, u32[]{:S(2)}) async-start(bf16[16,48,128]{2,1,0:T(8,128)(2,1)} %shard_map.77), calls=%async_computation | async-start | bytes 393216 | tf_op jit(solution)/shard_map/all_to_all | solution.py:275
  16.8 0.0 copy-done.5
  16.8 0.0 copy-done.6
  16.8 1.3 %collective-permute-start = (bf16[64,768]{1,0:T(8,128)(2,1)S(1)}, bf16[64,768]{1,0:T(8,128)(2,1)S(1)}, u32[]{:S(2)}, u32[]{:S(2)}) collective-permute-start(bf16[64,768]{1,0:T(8,128)(2,1)S(1)} %get-tuple-element.14), channel_id=1, source_target_pairs={{0,32},{32,64},{64,96},{96,0},{1,33},{33,65},{65,97},{97,1},{2,34}... | collective-permute-start | bytes 294920 | tf_op jit(solution)/shard_map/ppermute | solution.py:272
  18.1 2.5 %collective-permute-start.1 = (bf16[64,768]{1,0:T(8,128)(2,1)S(1)}, bf16[64,768]{1,0:T(8,128)(2,1)S(1)}, u32[]{:S(2)}, u32[]{:S(2)}) collective-permute-start(bf16[64,768]{1,0:T(8,128)(2,1)S(1)} %get-tuple-element.13), channel_id=1, source_target_pairs={{0,64},{32,96},{64,0},{96,32},{1,65},{33,97},{65,1},{97,33},{2,66}... | collective-permute-start | bytes 294920 | tf_op jit(solution)/shard_map/ppermute | solution.py:272
  20.6 1.2 %collective-permute-start.2 = (bf16[64,768]{1,0:T(8,128)(2,1)S(1)}, bf16[64,768]{1,0:T(8,128)(2,1)S(1)}, u32[]{:S(2)}, u32[]{:S(2)}) collective-permute-start(bf16[64,768]{1,0:T(8,128)(2,1)S(1)} %get-tuple-element.12), channel_id=1, source_target_pairs={{0,96},{32,0},{64,32},{96,64},{1,97},{33,1},{65,33},{97,65},{2,98}... | collective-permute-start | bytes 294920 | tf_op jit(solution)/shard_map/ppermute | solution.py:272
  21.7 0.0 collective-permute-done.one
  21.7 2.8 %collective-permute-done.1.two = bf16[64,768]{1,0:T(8,128)(2,1)S(1)} collective-permute-done((bf16[64,768]{1,0:T(8,128)(2,1)S(1)}, bf16[64,768]{1,0:T(8,128)(2,1)S(1)}, u32[]{:S(2)}, u32[]{:S(2)}) %collective-permute-start.1) | collective-permute-done | bytes 98336 | tf_op jit(solution)/shard_map/ppermute | solution.py:272
  24.5 0.7 collective-permute-done.2.three
  25.2 0.0 all-to-all-done.parts
  25.2 0.3 shard_map.78
  25.5 0.0 copy-start.1
  25.5 0.0 copy-start.3
  25.6 0.0 copy-start.8
  25.6 30.8 %all_to_all.21.gathered = bf16[64,96,128]{2,1,0:T(8,128)(2,1)S(1)} all-to-all(bf16[64,96,128]{2,1,0:T(8,128)(2,1)S(1)} %shard_map.78), channel_id=1, replica_groups=mesh['segment'=4,'tensor'=16,'dp'=2] {'segment','tensor'}, dimensions={0} | all-to-all | bytes 3145728 | tf_op jit(solution)/shard_map/all_to_all | solution.py:277
  56.4 0.0 copy-done.1
  56.4 0.0 copy-done.3
  56.4 0.0 copy-done.8
  56.4 4.3 %shard_map.79 = (bf16[256,384]{1,0:T(8,128)(2,1)S(1)}, f32[256,384]{1,0:T(8,128)S(1)}, f32[32,128]{1,0:T(8,128)}) custom-call(s32[2]{0:T(128)S(1)} %copy-done.8, bf16[64,96,128]{2,1,0:T(8,128)(2,1)S(1)} %all_to_all.21.gathered, bf16[64,768]{1,0:T(8,128)(2,1)S(1)} %collective-permute-done.one, bf16[64,768]{1,0:T(8,128)(2,1)S(1)} %collective-permute-done.1.two, ...), custom_call_target="tpu_custom_call" | custom-call | flops 600000000 | bytes 5000000 | tf_op jit(solution)/shard_map/pallas_call | solution.py:197
  60.7 4.0 %collective-permute-start.3 = (bf16[256,384]{1,0:T(8,128)(2,1)S(1)}, bf16[256,384]{1,0:T(8,128)(2,1)S(1)}, u32[]{:S(2)}, u32[]{:S(2)}) collective-permute-start(bf16[256,384]{1,0:T(8,128)(2,1)S(1)} %get-tuple-element.7), channel_id=1, source_target_pairs={{0,1},{1,0},{2,3},{3,2},{4,5},{5,4},{6,7},{7,6},{8,9},{9,8},{10,11... | collective-permute-start | bytes 589832 | tf_op jit(solution)/shard_map/ppermute | solution.py:279
  64.6 3.6 %all-to-all-start.2 = ((f32[32,1,128]{2,1,0:T(1,128)}), f32[32,1,128]{2,1,0:T(1,128)S(1)}, u32[]{:S(2)}, u32[]{:S(2)}) async-start(f32[32,1,128]{2,1,0:T(1,128)} %bitcast.5), calls=%async_computation.2 | async-start | bytes 32768 | tf_op jit(solution)/shard_map/all_to_all | solution.py:280
  68.9 6.2 %all-to-all-done.2 = f32[32,1,128]{2,1,0:T(1,128)S(1)} async-done(((f32[32,1,128]{2,1,0:T(1,128)}), f32[32,1,128]{2,1,0:T(1,128)S(1)}, u32[]{:S(2)}, u32[]{:S(2)}) %all-to-all-start.2) | async-done | bytes 16416 | tf_op jit(solution)/shard_map/all_to_all | solution.py:280
  75.1 0.0 collective-permute-done.3.swapped
  75.1 0.8 %shard_map.80 = (f32[1,384,64]{2,1,0:T(8,128)S(1)}, f32[1,64,384]{2,1,0:T(8,128)}) custom-call(f32[1]{0:T(128)S(6)} %copy.13.clip, f32[32,128]{1,0:T(8,128)S(1)} %bitcast.15, f32[256,384]{1,0:T(8,128)S(1)} %get-tuple-element.6.ours, bf16[256,384]{1,0:T(8,128)(2,1)S(1)} %collective-permute-done.3.swapped), custom_call_target="tpu_custom_call" | custom-call | flops 300000 | bytes 900000 | tf_op jit(solution)/shard_map/pallas_call | solution.py:251
  75.9 0.8 copy.12
  (1 shorter events, 0.0 us)
Async XLA Ops:
  1.7 1.3 %copy-start = (bf16[2,384,768]{2,1,0:T(8,128)(2,1)S(1)}, bf16[2,384,768]{2,1,0:T(8,128)(2,1)}, u32[]{:S(2)}) copy-start(bf16[2,384,768]{2,1,0:T(8,128)(2,1)} %act_hbm.1) | copy-start | bytes 3538948
  3.0 1.3 %copy-start.2 = (bf16[2,384,768]{2,1,0:T(8,128)(2,1)S(1)}, bf16[2,384,768]{2,1,0:T(8,128)(2,1)}, u32[]{:S(2)}) copy-start(bf16[2,384,768]{2,1,0:T(8,128)(2,1)} %cot_hbm.1) | copy-start | bytes 3538948
  4.2 0.9 %copy-start.4 = (bf16[1,64,768]{2,1,0:T(8,128)(2,1)S(1)}, bf16[1,64,768]{2,1,0:T(8,128)(2,1)}, u32[]{:S(2)}) copy-start(bf16[1,64,768]{2,1,0:T(8,128)(2,1)} %up.3) | copy-start | bytes 294916
  5.1 0.7 copy-start.7
  5.8 11.0 %copy-start.5 = (bf16[1,64,768]{2,1,0:T(8,128)(2,1)S(1)}, bf16[1,64,768]{2,1,0:T(8,128)(2,1)}, u32[]{:S(2)}) copy-start(bf16[1,64,768]{2,1,0:T(8,128)(2,1)} %up.3) | copy-start | bytes 294916
  5.8 11.0 %copy-start.6 = (bf16[1,768,64]{1,2,0:T(8,128)(2,1)S(1)}, bf16[1,768,64]{1,2,0:T(8,128)(2,1)}, u32[]{:S(2)}) copy-start(bf16[1,768,64]{1,2,0:T(8,128)(2,1)} %param.10) | copy-start | bytes 294916
  8.2 17.0 %all-to-all-start = ((bf16[16,48,128]{2,1,0:T(8,128)(2,1)}), bf16[16,48,128]{2,1,0:T(8,128)(2,1)S(1)}, u32[]{:S(2)}, u32[]{:S(2)}) async-start(bf16[16,48,128]{2,1,0:T(8,128)(2,1)} %shard_map.77), calls=%async_computation | async-start | bytes 393216 | tf_op jit(solution)/shard_map/all_to_all | solution.py:275
  16.8 4.9 %collective-permute-start = (bf16[64,768]{1,0:T(8,128)(2,1)S(1)}, bf16[64,768]{1,0:T(8,128)(2,1)S(1)}, u32[]{:S(2)}, u32[]{:S(2)}) collective-permute-start(bf16[64,768]{1,0:T(8,128)(2,1)S(1)} %get-tuple-element.14), channel_id=1, source_target_pairs={{0,32},{32,64},{64,96},{96,0},{1,33},{33,65},{65,97},{97,1},{2,34}... | collective-permute-start | bytes 294920 | tf_op jit(solution)/shard_map/ppermute | solution.py:272
  18.1 6.4 %collective-permute-start.1 = (bf16[64,768]{1,0:T(8,128)(2,1)S(1)}, bf16[64,768]{1,0:T(8,128)(2,1)S(1)}, u32[]{:S(2)}, u32[]{:S(2)}) collective-permute-start(bf16[64,768]{1,0:T(8,128)(2,1)S(1)} %get-tuple-element.13), channel_id=1, source_target_pairs={{0,64},{32,96},{64,0},{96,32},{1,65},{33,97},{65,1},{97,33},{2,66}... | collective-permute-start | bytes 294920 | tf_op jit(solution)/shard_map/ppermute | solution.py:272
  20.6 4.6 %collective-permute-start.2 = (bf16[64,768]{1,0:T(8,128)(2,1)S(1)}, bf16[64,768]{1,0:T(8,128)(2,1)S(1)}, u32[]{:S(2)}, u32[]{:S(2)}) collective-permute-start(bf16[64,768]{1,0:T(8,128)(2,1)S(1)} %get-tuple-element.12), channel_id=1, source_target_pairs={{0,96},{32,0},{64,32},{96,64},{1,97},{33,1},{65,33},{97,65},{2,98}... | collective-permute-start | bytes 294920 | tf_op jit(solution)/shard_map/ppermute | solution.py:272
  25.5 30.9 %copy-start.1 = (bf16[2,384,768]{2,1,0:T(8,128)(2,1)S(1)}, bf16[2,384,768]{2,1,0:T(8,128)(2,1)}, u32[]{:S(2)}) copy-start(bf16[2,384,768]{2,1,0:T(8,128)(2,1)} %act_hbm.1) | copy-start | bytes 3538948
  25.5 30.9 %copy-start.3 = (bf16[2,384,768]{2,1,0:T(8,128)(2,1)S(1)}, bf16[2,384,768]{2,1,0:T(8,128)(2,1)}, u32[]{:S(2)}) copy-start(bf16[2,384,768]{2,1,0:T(8,128)(2,1)} %cot_hbm.1) | copy-start | bytes 3538948
  25.6 30.8 %copy-start.8 = (s32[2]{0:T(128)S(1)}, s32[2]{0:T(128)}, u32[]{:S(2)}) copy-start(s32[2]{0:T(128)} %lengths.3) | copy-start | bytes 28
  60.7 14.5 %collective-permute-start.3 = (bf16[256,384]{1,0:T(8,128)(2,1)S(1)}, bf16[256,384]{1,0:T(8,128)(2,1)S(1)}, u32[]{:S(2)}, u32[]{:S(2)}) collective-permute-start(bf16[256,384]{1,0:T(8,128)(2,1)S(1)} %get-tuple-element.7), channel_id=1, source_target_pairs={{0,1},{1,0},{2,3},{3,2},{4,5},{5,4},{6,7},{7,6},{8,9},{9,8},{10,11... | collective-permute-start | bytes 589832 | tf_op jit(solution)/shard_map/ppermute | solution.py:279
  64.6 10.5 %all-to-all-start.2 = ((f32[32,1,128]{2,1,0:T(1,128)}), f32[32,1,128]{2,1,0:T(1,128)S(1)}, u32[]{:S(2)}, u32[]{:S(2)}) async-start(f32[32,1,128]{2,1,0:T(1,128)} %bitcast.5), calls=%async_computation.2 | async-start | bytes 32768 | tf_op jit(solution)/shard_map/all_to_all | solution.py:280

commit v3 on v2

--- a/solution.py
+++ b/solution.py
@@ -11,7 +11,7 @@
 F32 = jnp.float32
 VMEM = pl.BlockSpec(memory_space=pltpu.VMEM)
 SMEM = pl.BlockSpec(memory_space=pltpu.SMEM)
-ANY = pl.BlockSpec(memory_space=pl.ANY)
+HBM = pl.BlockSpec(memory_space=pltpu.HBM)
 
 LAYERS = 4
 CUTS = 16
@@ -21,7 +21,7 @@
 HALF = RANK // 2
 LANES = 2 * RANK
 PIECE = SLOTS // CUTS
-PACK = 48
+EXTRA = 16
 LOCAL = WIDTH // 2
 
 
@@ -39,71 +39,104 @@
     return values * half, slope
 
 
-PROJECT_STEPS = 2
-PROJECT_ROWS = SLOTS // PROJECT_STEPS
-
-
-def project_body(lengths, act, cot, down, up, out):
-    base = pl.program_id(0) * PROJECT_ROWS
-    rows = 2 * PROJECT_ROWS
-    first = dot(act[...].reshape(rows, WIDTH), down[0], 1, 0)
-    last = dot(cot[...].reshape(rows, WIDTH), up[0], 1, 1)
-    first = jnp.concatenate([first[:PROJECT_ROWS], first[PROJECT_ROWS:]], axis=1)
-    last = jnp.concatenate([last[:PROJECT_ROWS], last[PROJECT_ROWS:]], axis=1)
-    slot = lax.broadcasted_iota(jnp.int32, (PROJECT_ROWS, LANES), 0) + base
-    lane = lax.broadcasted_iota(jnp.int32, (PROJECT_ROWS, LANES), 1)
-    last = jnp.where(slot < jnp.where(lane < RANK, lengths[0], lengths[1]), last, 0.0)
-    for i in range(PROJECT_ROWS // PIECE):
-        part = slice(i * PIECE, (i + 1) * PIECE)
-        out[i] = jnp.concatenate([first[part], last[part]], axis=0).astype(BF)
-
-
-def project(lengths, act, cot, down, up):
-    block = pl.BlockSpec((2, PROJECT_ROWS, WIDTH), lambda i: (0, i, 0))
+STEPS = 4
+STEP_ROWS = SLOTS // STEPS
+
+
+def project_body(act_hbm, cot_hbm, down_t, up, out, act, cot, sems):
+    copies = []
+    for i in range(STEPS):
+        rows = pl.ds(i * STEP_ROWS, STEP_ROWS)
+        pair = []
+        for j, (source, target) in enumerate(((act_hbm, act), (cot_hbm, cot))):
+            copy = pltpu.make_async_copy(source.at[:, rows], target.at[:, rows], sems.at[i, j])
+            copy.start()
+            pair.append(copy)
+        copies.append(pair)
+    for i in range(STEPS):
+        rows = pl.ds(i * STEP_ROWS, STEP_ROWS)
+        copies[i][0].wait()
+        first = dot(act[:, rows].reshape(2 * STEP_ROWS, WIDTH), down_t[...], 1, 1)
+        copies[i][1].wait()
+        last = dot(cot[:, rows].reshape(2 * STEP_ROWS, WIDTH), up[0], 1, 1)
+        first = jnp.concatenate([first[:STEP_ROWS], first[STEP_ROWS:]], axis=1)
+        last = jnp.concatenate([last[:STEP_ROWS], last[STEP_ROWS:]], axis=1)
+        for j in range(STEP_ROWS // PIECE):
+            part = slice(j * PIECE, (j + 1) * PIECE)
+            out[i * (STEP_ROWS // PIECE) + j] = jnp.concatenate(
+                [first[part], last[part]], axis=0
+            ).astype(BF)
+
+
+def project(act, cot, down_t, up):
     return pl.pallas_call(
         project_body,
-        grid=(PROJECT_STEPS,),
-        in_specs=[
-            SMEM,
-            block,
-            block,
-            pl.BlockSpec((1, WIDTH, RANK), lambda i: (0, 0, 0)),
-            pl.BlockSpec((1, RANK, WIDTH), lambda i: (0, 0, 0)),
+        in_specs=[HBM, HBM, VMEM, VMEM],
+        out_specs=VMEM,
+        out_shape=jax.ShapeDtypeStruct((CUTS, 2 * PIECE, LANES), BF),
+        scratch_shapes=[
+            pltpu.VMEM((2, SLOTS, WIDTH), BF),
+            pltpu.VMEM((2, SLOTS, WIDTH), BF),
+            pltpu.SemaphoreType.DMA((STEPS, 2)),
         ],
-        out_specs=pl.BlockSpec((CUTS // PROJECT_STEPS, 2 * PIECE, LANES), lambda i: (i, 0, 0)),
-        out_shape=jax.ShapeDtypeStruct((CUTS, 2 * PIECE, LANES), BF),
         compiler_params=pltpu.CompilerParams(vmem_limit_bytes=16 << 20),
         cost_estimate=pl.CostEstimate(flops=150000000, bytes_accessed=2800000, transcendentals=0),
-    )(lengths, act, cot, down, up)
-
-
-def reduce_body(parts, up, down_t, one, two, three, out):
+    )(act, cot, down_t, up)
+
+
+def weave_body(partial, up, down_t, one, two, three, out):
     seg = lax.axis_index("segment")
-    total = parts[0].astype(F32)
-    for i in range(1, CUTS):
-        total = total + parts[i].astype(F32)
-    pieces = []
     for k, other in ((1, one), (2, two), (3, three)):
         lower = seg >= k
         left = jnp.where(lower, other[HALF:], up[0, :HALF])
         right = jnp.where(lower, down_t[...], other[...])
-        pieces.append(dot(left, right, 1, 1))
-    grams = jnp.concatenate(pieces, axis=0)
-    grams = jnp.concatenate([grams[:PACK], grams[PACK:]], axis=1)
-    message = jnp.concatenate([total, grams], axis=0).astype(BF)
+        gram = dot(left, right, 1, 1)
+        gram = jnp.concatenate([gram, jnp.zeros_like(gram)], axis=1)
+        for q in range(4):
+            tile = gram[q * 8 : (q + 1) * 8]
+            out[(k - 1) * 4 + q, 2 * PIECE :] = jnp.concatenate(
+                [tile, jnp.zeros_like(tile)], axis=0
+            ).astype(BF)
+    for t in range(CUTS):
+        out[t, : 2 * PIECE] = partial[t]
+    for t in range(12, CUTS):
+        out[t, 2 * PIECE :] = jnp.zeros((EXTRA, LANES), BF)
+
+
+def weave(partial, up, down_t, peers):
+    return pl.pallas_call(
+        weave_body,
+        in_specs=[VMEM] * 6,
+        out_specs=VMEM,
+        out_shape=jax.ShapeDtypeStruct((CUTS, 2 * PIECE + EXTRA, LANES), BF),
+        compiler_params=pltpu.CompilerParams(vmem_limit_bytes=16 << 20),
+        cost_estimate=pl.CostEstimate(flops=10000000, bytes_accessed=1000000, transcendentals=0),
+    )(partial, up, down_t, *peers)
+
+
+def reduce_body(lengths, parts, out):
+    base = lax.axis_index("tensor") * PIECE
+    total = parts[0].astype(F32)
+    for i in range(1, CUTS):
+        total = total + parts[i].astype(F32)
+    slot = lax.broadcasted_iota(jnp.int32, (PIECE, LANES), 0) + base
+    lane = lax.broadcasted_iota(jnp.int32, (PIECE, LANES), 1)
+    live = slot < jnp.where(lane < RANK, lengths[0], lengths[1])
+    last = jnp.where(live, total[PIECE : 2 * PIECE], 0.0)
+    message = jnp.concatenate([total[:PIECE], last, total[2 * PIECE :]], axis=0).astype(BF)
     for i in range(LAYERS * CUTS):
         out[i] = message
 
 
-def reduce_parts(parts, up, down_t, peers):
+def reduce_parts(lengths, parts):
     return pl.pallas_call(
         reduce_body,
-        in_specs=[VMEM] * 6,
+        in_specs=[SMEM, VMEM],
         out_specs=VMEM,
-        out_shape=jax.ShapeDtypeStruct((LAYERS * CUTS, 2 * PIECE + PACK, LANES), BF),
+        out_shape=jax.ShapeDtypeStruct((LAYERS * CUTS, 2 * PIECE + EXTRA, LANES), BF),
         compiler_params=pltpu.CompilerParams(vmem_limit_bytes=16 << 20),
-        cost_estimate=pl.CostEstimate(flops=10000000, bytes_accessed=2300000, transcendentals=0),
-    )(parts, up, down_t, *peers)
+        cost_estimate=pl.CostEstimate(flops=200000, bytes_accessed=1300000, transcendentals=0),
+    )(lengths, parts)
 
 
 def gradient_body(
@@ -120,15 +153,14 @@
 
     packed = []
     for layer in range(LAYERS):
-        total = None
+        tiles = []
         for t in range(CUTS):
-            at = layer * CUTS + t
-            block = gathered[at, : 2 * PIECE].astype(F32)
+            block = gathered[layer * CUTS + t].astype(F32)
             first[layer, t * PIECE : (t + 1) * PIECE] = block[:PIECE]
-            last[layer, t * PIECE : (t + 1) * PIECE] = block[PIECE:]
-            gram = gathered[at, 2 * PIECE :].astype(F32)
-            total = gram if total is None else total + gram
-        packed.append(jnp.concatenate([total[:, :RANK], total[:, RANK:]], axis=0))
+            last[layer, t * PIECE : (t + 1) * PIECE] = block[PIECE : 2 * PIECE]
+            if t < 12:
+                tiles.append(block[2 * PIECE : 2 * PIECE + 8, :RANK])
+        packed.append(jnp.concatenate(tiles, axis=0))
 
     def gram_of(i, j):
         a, b = (i - j) % LAYERS - 1, (j - i) % LAYERS - 1
@@ -196,7 +228,7 @@
     wide = (LAYERS, SLOTS, LANES)
     return pl.pallas_call(
         gradient_body,
-        in_specs=[SMEM] + [VMEM] * 4 + [ANY] * 2,
+        in_specs=[SMEM] + [VMEM] * 4 + [HBM] * 2,
         out_specs=[VMEM] * 3,
         out_shape=[
             jax.ShapeDtypeStruct((4 * RANK, LOCAL), BF),
@@ -243,7 +275,7 @@
             total = term if total is None else total + term
         return total
 
-    out_down[0] = combined(0).T
+    out_down[0] = combined(0)
     out_up[0] = combined(2 * RANK)
 
 
@@ -253,7 +285,7 @@
         in_specs=[SMEM] + [VMEM] * 3,
         out_specs=[VMEM] * 2,
         out_shape=[
-            jax.ShapeDtypeStruct((1, LOCAL, RANK), F32),
+            jax.ShapeDtypeStruct((1, RANK, LOCAL), F32),
             jax.ShapeDtypeStruct((1, RANK, LOCAL), F32),
         ],
         compiler_params=pltpu.CompilerParams(vmem_limit_bytes=16 << 20),
@@ -271,14 +303,16 @@
         peers.append(
             lax.ppermute(message, "segment", [(i, (i + k) % LAYERS) for i in range(LAYERS)])
         )
-    partial = project(lengths, act_input, cotangent, adapt_down, adapt_up)
-    parts = lax.all_to_all(partial, "tensor", 0, 0, tiled=True)
-    message = reduce_parts(parts, adapt_up, down_t, peers)
+    partial = project(act_input, cotangent, down_t, adapt_up)
+    woven = weave(partial, adapt_up, down_t, peers)
+    parts = lax.all_to_all(woven, "tensor", 0, 0, tiled=True)
+    message = reduce_parts(lengths, parts)
     gathered = lax.all_to_all(message, ("segment", "tensor"), 0, 0, tiled=True)
     theirs, ours, note = gradients(lengths, gathered, peers, act_input, cotangent)
     swapped = lax.ppermute(theirs, "dp", [(0, 1), (1, 0)])
     notes = lax.all_to_all(note, ("tensor", "dp"), 0, 0, tiled=True)
-    return scaled(clip_scale, notes, ours, swapped)
+    grad_down, grad_up = scaled(clip_scale, notes, ours, swapped)
+    return jnp.swapaxes(grad_down, 1, 2), grad_up
 
 
 def solution(mesh):

time: 77.1 us -> 70.2 us (0.911)
  starting transfers between devices: 21.1 us -> 12.8 us
  blocking collectives: 30.8 us -> 35.2 us
  waiting for transfers between devices: 9.7 us -> 6.23 us
  local copies, waits for them, and re-layouts: 5.93 us -> 4.34 us
  Pallas kernels: 7.76 us -> 8.83 us
  other arithmetic: 0.03 us -> 0.97 us
    all_to_all x0 -> x1, blocking collectives: none -> 15.2 us  [shards(): parts = lax.all_to_all(woven, 'tensor', 0, 0, tiled=True)]
    all_to_all x1, blocking collectives: 30.8 us -> 20 us  [shards(): gathered = lax.all_to_all(message, ('segment', 'tensor'), 0, 0, tiled=True)]
    all_to_all x1 -> x0, starting transfers between devices: 8.6 us -> none  [shards(): parts = lax.all_to_all(partial, 'tensor', 0, 0, tiled=True)]
    ppermute x3, waiting for transfers between devices: 3.48 us -> 0.01 us  [shards(): lax.ppermute(message, 'segment', [(i, (i + k) % LAYERS) for i in range(LA...]
    pallas_call x3 -> x4, Pallas kernels: 6.96 us -> 8.02 us  [the longest x1 4.2 us: gradients(): pl.pallas_call(gradient_body, in_specs=[SMEM] + [VMEM] * 4 + [HBM] * 2, o...]
    select_n x1, other arithmetic: 0.03 us -> 0.97 us  [shards(): message = jnp.where(seg + k < LAYERS, up, down_t)]
    unnamed x19 -> x14, local copies, waits for them, and re-layouts: 5.17 us -> 4.34 us
    ppermute x3, starting transfers between devices: 4.89 us -> 5.71 us  [shards(): lax.ppermute(message, 'segment', [(i, (i + k) % LAYERS) for i in range(LA...]
  transfers between devices with their start and end apart: 6 -> 5, of which waited for: 3 -> 1; matrix products, arithmetic and copies ran while one was open for 0% -> 0% of each run, Pallas kernels for 0% -> 4%
where the time goes in v3:
time: 70.2 us; the launch traced here: 69.8 us
  blocking collectives  35.2 us (50%)
  starting transfers between devices  12.8 us (18%)
  Pallas kernels  8.83 us (13%)
  waiting for transfers between devices  6.23 us (9%)
  local copies, waits for them, and re-layouts  4.34 us (6%)
  between operations  1.38 us (2%)
  other arithmetic  0.97 us (1%)
    all_to_all x1, blocking collectives, shards(): gathered = lax.all_to_all(message, ('segment', 'tensor'), 0, 0, tiled=True)  20 us
    all_to_all x1, blocking collectives, shards(): parts = lax.all_to_all(woven, 'tensor', 0, 0, tiled=True)  15.2 us
    all_to_all x1, waiting for transfers between devices, shards(): notes = lax.all_to_all(note, ('tensor', 'dp'), 0, 0, tiled=True)  6.22 us
    ppermute x3, starting transfers between devices, shards(): lax.ppermute(message, 'segment', [(i, (i + k) % LAYERS) for i in range(LA...  5.71 us
    unnamed x14, local copies, waits for them, and re-layouts  4.34 us
    pallas_call x1, Pallas kernels, gradients(): pl.pallas_call(gradient_body, in_specs=[SMEM] + [VMEM] * 4 + [HBM] * 2, o...  4.2 us
    all_to_all x1, starting transfers between devices, shards(): notes = lax.all_to_all(note, ('tensor', 'dp'), 0, 0, tiled=True)  3.62 us
    ppermute x1, starting transfers between devices, shards(): swapped = lax.ppermute(theirs, 'dp', [(0, 1), (1, 0)])  3.51 us
  transfers between devices with their start and end apart: 5, of which 1 were waited for; matrix products, arithmetic and copies ran while one was open for 0% of the time, Pallas kernels for 4%

profile of v3, /device:TPU:1, one launch (start us, length us, event | category | flops | bytes accessed | tf_op | source)
XLA Modules:
  0.0 69.8 jit_solution(9253435381901927769)
XLA Ops:
  0.6 1.0 %bitcast_select_fusion = (bf16[64,768]{1,0:T(8,128)(2,1)S(1)}, bf16[64,768]{1,0:T(8,128)(2,1)S(1)}, bf16[64,768]{1,0:T(8,128)(2,1)S(1)}) fusion(bf16[1,64,768]{2,1,0:T(8,128)(2,1)} %up.3, pred[]{:T(512)S(6)} %lt.11, bf16[1,768,64]{1,2,0:T(8,128)(2,1)} %param.10, pred[]{:T(512)S(6)} %lt.10, pred[]{:T(512)S(6)} %lt.9), kind=kLoop, calls=%fused_computation | loop fusion | flops 147456 | bytes 491523 | tf_op jit(solution)/shard_map/jit(_where)/select_n | solution.py:302
  1.6 2.1 %collective-permute-start = (bf16[64,768]{1,0:T(8,128)(2,1)S(1)}, bf16[64,768]{1,0:T(8,128)(2,1)S(1)}, u32[]{:S(2)}, u32[]{:S(2)}) collective-permute-start(bf16[64,768]{1,0:T(8,128)(2,1)S(1)} %get-tuple-element.14), channel_id=1, source_target_pairs={{0,32},{32,64},{64,96},{96,0},{1,33},{33,65},{65,97},{97,1},{2,34}... | collective-permute-start | bytes 294920 | tf_op jit(solution)/shard_map/ppermute | solution.py:304
  3.7 2.5 %collective-permute-start.1 = (bf16[64,768]{1,0:T(8,128)(2,1)S(1)}, bf16[64,768]{1,0:T(8,128)(2,1)S(1)}, u32[]{:S(2)}, u32[]{:S(2)}) collective-permute-start(bf16[64,768]{1,0:T(8,128)(2,1)S(1)} %get-tuple-element.13), channel_id=1, source_target_pairs={{0,64},{32,96},{64,0},{96,32},{1,65},{33,97},{65,1},{97,33},{2,66}... | collective-permute-start | bytes 294920 | tf_op jit(solution)/shard_map/ppermute | solution.py:304
  6.2 1.2 %collective-permute-start.2 = (bf16[64,768]{1,0:T(8,128)(2,1)S(1)}, bf16[64,768]{1,0:T(8,128)(2,1)S(1)}, u32[]{:S(2)}, u32[]{:S(2)}) collective-permute-start(bf16[64,768]{1,0:T(8,128)(2,1)S(1)} %get-tuple-element.12), channel_id=1, source_target_pairs={{0,96},{32,0},{64,32},{96,64},{1,97},{33,1},{65,33},{97,65},{2,98}... | collective-permute-start | bytes 294920 | tf_op jit(solution)/shard_map/ppermute | solution.py:304
  7.3 0.0 copy-start
  7.3 1.3 %copy-done = bf16[2,384,768]{2,1,0:T(8,128)(2,1)S(1)} copy-done((bf16[2,384,768]{2,1,0:T(8,128)(2,1)S(1)}, bf16[2,384,768]{2,1,0:T(8,128)(2,1)}, u32[]{:S(2)}) %copy-start) | copy-done | bytes 1179672
  8.6 0.0 copy-start.2
  8.6 1.3 %copy-done.2 = bf16[2,384,768]{2,1,0:T(8,128)(2,1)S(1)} copy-done((bf16[2,384,768]{2,1,0:T(8,128)(2,1)S(1)}, bf16[2,384,768]{2,1,0:T(8,128)(2,1)}, u32[]{:S(2)}) %copy-start.2) | copy-done | bytes 1179672
  9.9 0.0 copy-start.4
  9.9 0.9 %copy-done.4 = bf16[1,768,64]{1,2,0:T(8,128)(2,1)S(1)} copy-done((bf16[1,768,64]{1,2,0:T(8,128)(2,1)S(1)}, bf16[1,768,64]{1,2,0:T(8,128)(2,1)}, u32[]{:S(2)}) %copy-start.4) | copy-done | bytes 98328
  10.8 0.0 copy-start.5
  10.8 0.9 %copy-done.5 = bf16[1,64,768]{2,1,0:T(8,128)(2,1)S(1)} copy-done((bf16[1,64,768]{2,1,0:T(8,128)(2,1)S(1)}, bf16[1,64,768]{2,1,0:T(8,128)(2,1)}, u32[]{:S(2)}) %copy-start.5) | copy-done | bytes 98328
  11.7 2.9 %shard_map.77.partial = bf16[16,48,128]{2,1,0:T(8,128)(2,1)S(1)} custom-call(bf16[2,384,768]{2,1,0:T(8,128)(2,1)S(1)} %copy-done, bf16[2,384,768]{2,1,0:T(8,128)(2,1)S(1)} %copy-done.2, bf16[64,768]{1,0:T(8,128)(2,1)S(1)} %bitcast.15, bf16[1,64,768]{2,1,0:T(8,128)(2,1)S(1)} %copy-done.5), custom_call_target="tpu_custom_call" | custom-call | flops 150000000 | bytes 2800000 | tf_op jit(solution)/shard_map/pallas_call | solution.py:72
  14.6 0.0 copy-start.6
  14.6 0.0 collective-permute-done.one
  14.6 0.0 collective-permute-done.1.two
  14.6 0.0 collective-permute-done.2.three
  14.6 0.2 shard_map.78
  14.9 15.2 %all_to_all.21.parts = bf16[16,64,128]{2,1,0:T(8,128)(2,1)S(1)} all-to-all(bf16[16,64,128]{2,1,0:T(8,128)(2,1)S(1)} %shard_map.78), channel_id=1, replica_groups=mesh['segment'=4,'tensor'=16,'dp'=2] {'tensor'}, dimensions={0} | all-to-all | bytes 524288 | tf_op jit(solution)/shard_map/all_to_all | solution.py:308
  30.1 0.0 copy-done.6
  30.1 0.0 copy-start.3
  30.1 0.7 shard_map.79
  30.8 0.0 copy-start.1
  30.8 20.0 %all_to_all.22.gathered = bf16[64,64,128]{2,1,0:T(8,128)(2,1)S(1)} all-to-all(bf16[64,64,128]{2,1,0:T(8,128)(2,1)S(1)} %shard_map.79), channel_id=1, replica_groups=mesh['segment'=4,'tensor'=16,'dp'=2] {'segment','tensor'}, dimensions={0} | all-to-all | bytes 2097152 | tf_op jit(solution)/shard_map/all_to_all | solution.py:310
  50.8 0.0 copy-done.3
  50.8 0.0 copy-done.1
  50.8 4.2 %shard_map.80 = (bf16[256,384]{1,0:T(8,128)(2,1)S(1)}, f32[256,384]{1,0:T(8,128)S(1)}, f32[32,128]{1,0:T(8,128)}) custom-call(s32[2]{0:T(128)S(1)} %copy-done.6, bf16[64,64,128]{2,1,0:T(8,128)(2,1)S(1)} %all_to_all.22.gathered, bf16[64,768]{1,0:T(8,128)(2,1)S(1)} %collective-permute-done.one, bf16[64,768]{1,0:T(8,128)(2,1)S(1)} %collective-permute-done.1.two, ...), custom_call_target="tpu_custom_call" | custom-call | flops 600000000 | bytes 5000000 | tf_op jit(solution)/shard_map/pallas_call | solution.py:229
  55.0 3.5 %collective-permute-start.3 = (bf16[256,384]{1,0:T(8,128)(2,1)S(1)}, bf16[256,384]{1,0:T(8,128)(2,1)S(1)}, u32[]{:S(2)}, u32[]{:S(2)}) collective-permute-start(bf16[256,384]{1,0:T(8,128)(2,1)S(1)} %get-tuple-element.9), channel_id=1, source_target_pairs={{0,1},{1,0},{2,3},{3,2},{4,5},{5,4},{6,7},{7,6},{8,9},{9,8},{10,11... | collective-permute-start | bytes 589832 | tf_op jit(solution)/shard_map/ppermute | solution.py:312
  58.5 3.6 %all-to-all-start.2 = ((f32[32,1,128]{2,1,0:T(1,128)}), f32[32,1,128]{2,1,0:T(1,128)S(1)}, u32[]{:S(2)}, u32[]{:S(2)}) async-start(f32[32,1,128]{2,1,0:T(1,128)} %bitcast.5), calls=%async_computation.2 | async-start | bytes 32768 | tf_op jit(solution)/shard_map/all_to_all | solution.py:313
  62.8 6.2 %all-to-all-done.2 = f32[32,1,128]{2,1,0:T(1,128)S(1)} async-done(((f32[32,1,128]{2,1,0:T(1,128)}), f32[32,1,128]{2,1,0:T(1,128)S(1)}, u32[]{:S(2)}, u32[]{:S(2)}) %all-to-all-start.2) | async-done | bytes 16416 | tf_op jit(solution)/shard_map/all_to_all | solution.py:313
  69.0 0.0 collective-permute-done.3.swapped
  69.0 0.8 %shard_map.81 = (f32[1,64,384]{2,1,0:T(8,128)}, f32[1,64,384]{2,1,0:T(8,128)}) custom-call(f32[1]{0:T(128)S(6)} %copy.9.clip, f32[32,128]{1,0:T(8,128)S(1)} %bitcast.17, f32[256,384]{1,0:T(8,128)S(1)} %get-tuple-element.8.ours, bf16[256,384]{1,0:T(8,128)(2,1)S(1)} %collective-permute-done.3.swapped), custom_call_target="tpu_custom_call" | custom-call | flops 300000 | bytes 900000 | tf_op jit(solution)/shard_map/pallas_call | solution.py:283
Async XLA Ops:
  1.6 13.0 %collective-permute-start = (bf16[64,768]{1,0:T(8,128)(2,1)S(1)}, bf16[64,768]{1,0:T(8,128)(2,1)S(1)}, u32[]{:S(2)}, u32[]{:S(2)}) collective-permute-start(bf16[64,768]{1,0:T(8,128)(2,1)S(1)} %get-tuple-element.14), channel_id=1, source_target_pairs={{0,32},{32,64},{64,96},{96,0},{1,33},{33,65},{65,97},{97,1},{2,34}... | collective-permute-start | bytes 294920 | tf_op jit(solution)/shard_map/ppermute | solution.py:304
  3.7 10.9 %collective-permute-start.1 = (bf16[64,768]{1,0:T(8,128)(2,1)S(1)}, bf16[64,768]{1,0:T(8,128)(2,1)S(1)}, u32[]{:S(2)}, u32[]{:S(2)}) collective-permute-start(bf16[64,768]{1,0:T(8,128)(2,1)S(1)} %get-tuple-element.13), channel_id=1, source_target_pairs={{0,64},{32,96},{64,0},{96,32},{1,65},{33,97},{65,1},{97,33},{2,66}... | collective-permute-start | bytes 294920 | tf_op jit(solution)/shard_map/ppermute | solution.py:304
  6.2 8.4 %collective-permute-start.2 = (bf16[64,768]{1,0:T(8,128)(2,1)S(1)}, bf16[64,768]{1,0:T(8,128)(2,1)S(1)}, u32[]{:S(2)}, u32[]{:S(2)}) collective-permute-start(bf16[64,768]{1,0:T(8,128)(2,1)S(1)} %get-tuple-element.12), channel_id=1, source_target_pairs={{0,96},{32,0},{64,32},{96,64},{1,97},{33,1},{65,33},{97,65},{2,98}... | collective-permute-start | bytes 294920 | tf_op jit(solution)/shard_map/ppermute | solution.py:304
  7.3 1.3 %copy-start = (bf16[2,384,768]{2,1,0:T(8,128)(2,1)S(1)}, bf16[2,384,768]{2,1,0:T(8,128)(2,1)}, u32[]{:S(2)}) copy-start(bf16[2,384,768]{2,1,0:T(8,128)(2,1)} %act_hbm.3) | copy-start | bytes 3538948
  8.6 1.3 %copy-start.2 = (bf16[2,384,768]{2,1,0:T(8,128)(2,1)S(1)}, bf16[2,384,768]{2,1,0:T(8,128)(2,1)}, u32[]{:S(2)}) copy-start(bf16[2,384,768]{2,1,0:T(8,128)(2,1)} %cot_hbm.3) | copy-start | bytes 3538948
  9.9 0.9 %copy-start.4 = (bf16[1,768,64]{1,2,0:T(8,128)(2,1)S(1)}, bf16[1,768,64]{1,2,0:T(8,128)(2,1)}, u32[]{:S(2)}) copy-start(bf16[1,768,64]{1,2,0:T(8,128)(2,1)} %param.10) | copy-start | bytes 294916
  10.8 0.9 %copy-start.5 = (bf16[1,64,768]{2,1,0:T(8,128)(2,1)S(1)}, bf16[1,64,768]{2,1,0:T(8,128)(2,1)}, u32[]{:S(2)}) copy-start(bf16[1,64,768]{2,1,0:T(8,128)(2,1)} %up.3) | copy-start | bytes 294916
  14.6 15.5 %copy-start.6 = (s32[2]{0:T(128)S(1)}, s32[2]{0:T(128)}, u32[]{:S(2)}) copy-start(s32[2]{0:T(128)} %lengths.3) | copy-start | bytes 28
  30.1 20.7 %copy-start.3 = (bf16[2,384,768]{2,1,0:T(8,128)(2,1)S(1)}, bf16[2,384,768]{2,1,0:T(8,128)(2,1)}, u32[]{:S(2)}) copy-start(bf16[2,384,768]{2,1,0:T(8,128)(2,1)} %cot_hbm.3) | copy-start | bytes 3538948
  30.8 20.0 %copy-start.1 = (bf16[2,384,768]{2,1,0:T(8,128)(2,1)S(1)}, bf16[2,384,768]{2,1,0:T(8,128)(2,1)}, u32[]{:S(2)}) copy-start(bf16[2,384,768]{2,1,0:T(8,128)(2,1)} %act_hbm.3) | copy-start | bytes 3538948
  55.0 14.0 %collective-permute-start.3 = (bf16[256,384]{1,0:T(8,128)(2,1)S(1)}, bf16[256,384]{1,0:T(8,128)(2,1)S(1)}, u32[]{:S(2)}, u32[]{:S(2)}) collective-permute-start(bf16[256,384]{1,0:T(8,128)(2,1)S(1)} %get-tuple-element.9), channel_id=1, source_target_pairs={{0,1},{1,0},{2,3},{3,2},{4,5},{5,4},{6,7},{7,6},{8,9},{9,8},{10,11... | collective-permute-start | bytes 589832 | tf_op jit(solution)/shard_map/ppermute | solution.py:312
  58.5 10.5 %all-to-all-start.2 = ((f32[32,1,128]{2,1,0:T(1,128)}), f32[32,1,128]{2,1,0:T(1,128)S(1)}, u32[]{:S(2)}, u32[]{:S(2)}) async-start(f32[32,1,128]{2,1,0:T(1,128)} %bitcast.5), calls=%async_computation.2 | async-start | bytes 32768 | tf_op jit(solution)/shard_map/all_to_all | solution.py:313

commit v4 on v3

--- a/solution.py
+++ b/solution.py
@@ -39,11 +39,11 @@
     return values * half, slope
 
 
-STEPS = 4
+STEPS = 2
 STEP_ROWS = SLOTS // STEPS
 
 
-def project_body(act_hbm, cot_hbm, down_t, up, out, act, cot, sems):
+def project_body(act_hbm, cot_hbm, sent, kept, out, act, cot, sems):
     copies = []
     for i in range(STEPS):
         rows = pl.ds(i * STEP_ROWS, STEP_ROWS)
@@ -53,14 +53,15 @@
             copy.start()
             pair.append(copy)
         copies.append(pair)
+    final = lax.axis_index("segment") == LAYERS - 1
+    down = jnp.where(final, sent[...], kept[...]).T
+    up_t = jnp.where(final, kept[...], sent[...]).T
     for i in range(STEPS):
         rows = pl.ds(i * STEP_ROWS, STEP_ROWS)
         copies[i][0].wait()
-        first = dot(act[:, rows].reshape(2 * STEP_ROWS, WIDTH), down_t[...], 1, 1)
+        first = jnp.concatenate([dot(act[e, rows], down, 1, 0) for e in range(2)], axis=1)
         copies[i][1].wait()
-        last = dot(cot[:, rows].reshape(2 * STEP_ROWS, WIDTH), up[0], 1, 1)
-        first = jnp.concatenate([first[:STEP_ROWS], first[STEP_ROWS:]], axis=1)
-        last = jnp.concatenate([last[:STEP_ROWS], last[STEP_ROWS:]], axis=1)
+        last = jnp.concatenate([dot(cot[e, rows], up_t, 1, 0) for e in range(2)], axis=1)
         for j in range(STEP_ROWS // PIECE):
             part = slice(j * PIECE, (j + 1) * PIECE)
             out[i * (STEP_ROWS // PIECE) + j] = jnp.concatenate(
@@ -68,7 +69,7 @@
             ).astype(BF)
 
 
-def project(act, cot, down_t, up):
+def project(act, cot, sent, kept):
     return pl.pallas_call(
         project_body,
         in_specs=[HBM, HBM, VMEM, VMEM],
@@ -79,17 +80,17 @@
             pltpu.VMEM((2, SLOTS, WIDTH), BF),
             pltpu.SemaphoreType.DMA((STEPS, 2)),
         ],
-        compiler_params=pltpu.CompilerParams(vmem_limit_bytes=16 << 20),
+        compiler_params=pltpu.CompilerParams(vmem_limit_bytes=53 << 20),
         cost_estimate=pl.CostEstimate(flops=150000000, bytes_accessed=2800000, transcendentals=0),
-    )(act, cot, down_t, up)
-
-
-def weave_body(partial, up, down_t, one, two, three, out):
+    )(act, cot, sent, kept)
+
+
+def weave_body(partial, to_one, to_two, to_three, one, two, three, out):
     seg = lax.axis_index("segment")
-    for k, other in ((1, one), (2, two), (3, three)):
+    for k, own, other in ((1, to_three, one), (2, to_two, two), (3, to_one, three)):
         lower = seg >= k
-        left = jnp.where(lower, other[HALF:], up[0, :HALF])
-        right = jnp.where(lower, down_t[...], other[...])
+        left = jnp.where(lower, other[HALF:], own[:HALF])
+        right = jnp.where(lower, own[...], other[...])
         gram = dot(left, right, 1, 1)
         gram = jnp.concatenate([gram, jnp.zeros_like(gram)], axis=1)
         for q in range(4):
@@ -103,15 +104,15 @@
         out[t, 2 * PIECE :] = jnp.zeros((EXTRA, LANES), BF)
 
 
-def weave(partial, up, down_t, peers):
+def weave(partial, messages, peers):
     return pl.pallas_call(
         weave_body,
-        in_specs=[VMEM] * 6,
+        in_specs=[VMEM] * 7,
         out_specs=VMEM,
         out_shape=jax.ShapeDtypeStruct((CUTS, 2 * PIECE + EXTRA, LANES), BF),
         compiler_params=pltpu.CompilerParams(vmem_limit_bytes=16 << 20),
         cost_estimate=pl.CostEstimate(flops=10000000, bytes_accessed=1000000, transcendentals=0),
-    )(partial, up, down_t, *peers)
+    )(partial, *messages, *peers)
 
 
 def reduce_body(lengths, parts, out):
@@ -141,11 +142,10 @@
 
 def gradient_body(
     lengths, gathered, one, two, three, act_hbm, cot_hbm,
-    theirs, ours, note,
-    act, cot, first, last, hidden, slopes, steep, each, sems,
+    each, note,
+    act, cot, first, last, hidden, slopes, steep, sems,
 ):
     seg = lax.axis_index("segment")
-    core = lax.axis_index("dp")
     act_copy = pltpu.make_async_copy(act_hbm, act, sems.at[0])
     cot_copy = pltpu.make_async_copy(cot_hbm, cot, sems.at[1])
     act_copy.start()
@@ -218,10 +218,6 @@
         each[other] = up_grad
         square = jnp.sum(down_grad * down_grad + up_grad * up_grad)
         note[:, rows] = jnp.full((2 * CUTS, RANK), square, F32)
-    keep = pl.multiple_of(core * LOCAL, 128)
-    give = pl.multiple_of((1 - core) * LOCAL, 128)
-    ours[...] = each[:, pl.ds(keep, LOCAL)]
-    theirs[...] = each[:, pl.ds(give, LOCAL)].astype(BF)
 
 
 def gradients(lengths, gathered, peers, act, cot):
@@ -229,10 +225,9 @@
     return pl.pallas_call(
         gradient_body,
         in_specs=[SMEM] + [VMEM] * 4 + [HBM] * 2,
-        out_specs=[VMEM] * 3,
+        out_specs=[VMEM] * 2,
         out_shape=[
-            jax.ShapeDtypeStruct((4 * RANK, LOCAL), BF),
-            jax.ShapeDtypeStruct((4 * RANK, LOCAL), F32),
+            jax.ShapeDtypeStruct((4 * RANK, WIDTH), F32),
             jax.ShapeDtypeStruct((2 * CUTS, LANES), F32),
         ],
         scratch_shapes=[
@@ -243,7 +238,6 @@
             pltpu.VMEM(wide, BF),
             pltpu.VMEM(wide, BF),
             pltpu.VMEM(wide, F32),
-            pltpu.VMEM((4 * RANK, WIDTH), F32),
             pltpu.SemaphoreType.DMA((2,)),
         ],
         compiler_params=pltpu.CompilerParams(vmem_limit_bytes=32 << 20),
@@ -253,8 +247,25 @@
     )(lengths, gathered, *peers, act, cot)
 
 
-def scale_body(clip, notes, ours, swapped, out_down, out_up):
+def share_body(each, theirs):
+    give = pl.multiple_of((1 - lax.axis_index("dp")) * LOCAL, 128)
+    theirs[...] = each[:, pl.ds(give, LOCAL)].astype(BF)
+
+
+def share(each):
+    return pl.pallas_call(
+        share_body,
+        in_specs=[VMEM],
+        out_specs=VMEM,
+        out_shape=jax.ShapeDtypeStruct((4 * RANK, LOCAL), BF),
+        compiler_params=pltpu.CompilerParams(vmem_limit_bytes=16 << 20),
+        cost_estimate=pl.CostEstimate(flops=100000, bytes_accessed=1000000, transcendentals=0),
+    )(each)
+
+
+def scale_body(clip, notes, each, swapped, out_down, out_up):
     core = lax.axis_index("dp")
+    ours = each.at[:, pl.ds(pl.multiple_of(core * LOCAL, 128), LOCAL)]
     row = lax.broadcasted_iota(jnp.int32, (2 * CUTS, LANES), 0)
     is_own = lax.rem(row, 2) == core
     values = notes[...]
@@ -279,7 +290,7 @@
     out_up[0] = combined(2 * RANK)
 
 
-def scaled(clip, notes, ours, swapped):
+def scaled(clip, notes, each, swapped):
     return pl.pallas_call(
         scale_body,
         in_specs=[SMEM] + [VMEM] * 3,
@@ -290,28 +301,27 @@
         ],
         compiler_params=pltpu.CompilerParams(vmem_limit_bytes=16 << 20),
         cost_estimate=pl.CostEstimate(flops=300000, bytes_accessed=900000, transcendentals=0),
-    )(clip, notes, ours, swapped)
+    )(clip, notes, each, swapped)
 
 
 def shards(act_input, cotangent, lengths, clip_scale, adapt_down, adapt_up):
     seg = lax.axis_index("segment")
     up = adapt_up[0]
     down_t = adapt_down[0].T
-    peers = []
-    for k in range(1, LAYERS):
-        message = jnp.where(seg + k < LAYERS, up, down_t)
-        peers.append(
-            lax.ppermute(message, "segment", [(i, (i + k) % LAYERS) for i in range(LAYERS)])
-        )
-    partial = project(act_input, cotangent, down_t, adapt_up)
-    woven = weave(partial, adapt_up, down_t, peers)
+    messages = [jnp.where(seg + k < LAYERS, up, down_t) for k in range(1, LAYERS)]
+    peers = [
+        lax.ppermute(messages[k - 1], "segment", [(i, (i + k) % LAYERS) for i in range(LAYERS)])
+        for k in range(1, LAYERS)
+    ]
+    partial = project(act_input, cotangent, messages[0], jnp.where(seg + 1 < LAYERS, down_t, up))
+    woven = weave(partial, messages, peers)
     parts = lax.all_to_all(woven, "tensor", 0, 0, tiled=True)
     message = reduce_parts(lengths, parts)
     gathered = lax.all_to_all(message, ("segment", "tensor"), 0, 0, tiled=True)
-    theirs, ours, note = gradients(lengths, gathered, peers, act_input, cotangent)
-    swapped = lax.ppermute(theirs, "dp", [(0, 1), (1, 0)])
+    each, note = gradients(lengths, gathered, peers, act_input, cotangent)
+    swapped = lax.ppermute(share(each), "dp", [(0, 1), (1, 0)])
     notes = lax.all_to_all(note, ("tensor", "dp"), 0, 0, tiled=True)
-    grad_down, grad_up = scaled(clip_scale, notes, ours, swapped)
+    grad_down, grad_up = scaled(clip_scale, notes, each, swapped)
     return jnp.swapaxes(grad_down, 1, 2), grad_up
 
 

time: 70.2 us -> 67.7 us (0.964)
  local copies, waits for them, and re-layouts: 4.34 us -> 0.02 us
  blocking collectives: 35.2 us -> 36.8 us
    unnamed x14 -> x6, local copies, waits for them, and re-layouts: 4.34 us -> 0.02 us
    all_to_all x1, blocking collectives: 20 us -> 21.7 us  [shards(): gathered = lax.all_to_all(message, ('segment', 'tensor'), 0, 0, tiled=True)]
  transfers between devices with their start and end apart: 5 -> 5, of which waited for: 1 -> 2; matrix products, arithmetic and copies ran while one was open for 0% -> 0% of each run, Pallas kernels for 4% -> 4%
where the time goes in v4:
time: 67.7 us; the launch traced here: 67.4 us
  blocking collectives  36.8 us (54%)
  starting transfers between devices  13.3 us (20%)
  Pallas kernels  8.42 us (12%)
  waiting for transfers between devices  6.48 us (10%)
  between operations  1.37 us (2%)
  other arithmetic  0.97 us (1%)
    all_to_all x1, blocking collectives, shards(): gathered = lax.all_to_all(message, ('segment', 'tensor'), 0, 0, tiled=True)  21.7 us
    all_to_all x1, blocking collectives, shards(): parts = lax.all_to_all(woven, 'tensor', 0, 0, tiled=True)  15.2 us
    all_to_all x1, waiting for transfers between devices, shards(): notes = lax.all_to_all(note, ('tensor', 'dp'), 0, 0, tiled=True)  6.22 us
    ppermute x3, starting transfers between devices, shards(): lax.ppermute(messages[k - 1], 'segment', [(i, (i + k) % LAYERS) for i in...  5.71 us
    pallas_call x1, Pallas kernels, gradients(): pl.pallas_call(gradient_body, in_specs=[SMEM] + [VMEM] * 4 + [HBM] * 2, o...  4.12 us
    ppermute x1, starting transfers between devices, shards(): swapped = lax.ppermute(share(each), 'dp', [(0, 1), (1, 0)])  3.96 us
    all_to_all x1, starting transfers between devices, shards(): notes = lax.all_to_all(note, ('tensor', 'dp'), 0, 0, tiled=True)  3.61 us
    pallas_call x1, Pallas kernels, project(): pl.pallas_call(project_body, in_specs=[HBM, HBM, VMEM, VMEM], out_specs=V...  2.57 us
  transfers between devices with their start and end apart: 5, of which 2 were waited for; matrix products, arithmetic and copies ran while one was open for 0% of the time, Pallas kernels for 4%

profile of v4, /device:TPU:1, one launch (start us, length us, event | category | flops | bytes accessed | tf_op | source)
XLA Modules:
  0.0 67.4 jit_solution(7831059425926457843)
XLA Ops:
  0.6 1.0 %bitcast_select_fusion = (bf16[64,768]{1,0:T(8,128)(2,1)S(1)}, bf16[64,768]{1,0:T(8,128)(2,1)S(1)}, bf16[64,768]{1,0:T(8,128)(2,1)S(1)}, bf16[64,768]{1,0:T(8,128)(2,1)S(1)}) fusion(bf16[1,768,64]{1,2,0:T(8,128)(2,1)} %param.10, bf16[1,64,768]{2,1,0:T(8,128)(2,1)} %param.11, pred[]{:T(512)S(6)} %lt.12, pred[]{:T(512)S(6)} %lt.10, pred[]{:T(512)S(6)} %lt.11), kind=kLoop, calls=%fused_computation | loop fusion | flops 196608 | bytes 589827 | tf_op jit(solution)/shard_map/jit(_where)/select_n | solution.py:311
  1.6 2.1 %collective-permute-start = (bf16[64,768]{1,0:T(8,128)(2,1)S(1)}, bf16[64,768]{1,0:T(8,128)(2,1)S(1)}, u32[]{:S(2)}, u32[]{:S(2)}) collective-permute-start(bf16[64,768]{1,0:T(8,128)(2,1)S(1)} %get-tuple-element.13.sent.to_one), channel_id=1, source_target_pairs={{0,32},{32,64},{64,96},{96,0},{1,33},{33,65},{65,97},{97,1},{2,34}... | collective-permute-start | bytes 294920 | tf_op jit(solution)/shard_map/ppermute | solution.py:313
  3.7 2.5 %collective-permute-start.1 = (bf16[64,768]{1,0:T(8,128)(2,1)S(1)}, bf16[64,768]{1,0:T(8,128)(2,1)S(1)}, u32[]{:S(2)}, u32[]{:S(2)}) collective-permute-start(bf16[64,768]{1,0:T(8,128)(2,1)S(1)} %get-tuple-element.12.to_two), channel_id=1, source_target_pairs={{0,64},{32,96},{64,0},{96,32},{1,65},{33,97},{65,1},{97,33},{2,66}... | collective-permute-start | bytes 294920 | tf_op jit(solution)/shard_map/ppermute | solution.py:313
  6.2 1.2 %collective-permute-start.2 = (bf16[64,768]{1,0:T(8,128)(2,1)S(1)}, bf16[64,768]{1,0:T(8,128)(2,1)S(1)}, u32[]{:S(2)}, u32[]{:S(2)}) collective-permute-start(bf16[64,768]{1,0:T(8,128)(2,1)S(1)} %get-tuple-element.10.to_three), channel_id=1, source_target_pairs={{0,96},{32,0},{64,32},{96,64},{1,97},{33,1},{65,33},{97,65},{2,98}... | collective-permute-start | bytes 294920 | tf_op jit(solution)/shard_map/ppermute | solution.py:313
  7.3 2.6 %shard_map.77.partial = bf16[16,48,128]{2,1,0:T(8,128)(2,1)S(1)} custom-call(bf16[2,384,768]{2,1,0:T(8,128)(2,1)} %act_hbm.3, bf16[2,384,768]{2,1,0:T(8,128)(2,1)} %cot_hbm.3, bf16[64,768]{1,0:T(8,128)(2,1)S(1)} %get-tuple-element.13.sent.to_one, bf16[64,768]{1,0:T(8,128)(2,1)S(1)} %get-tuple-element.11.kept), custom_call_target="tpu_custom_call" | custom-call | flops 150000000 | bytes 2800000 | tf_op jit(solution)/shard_map/pallas_call | solution.py:73
  9.9 0.0 copy-start.2
  9.9 0.0 collective-permute-done.one
  9.9 0.3 collective-permute-done.1.two
  10.2 0.0 collective-permute-done.2.three
  10.2 0.2 shard_map.78
  10.4 15.2 %all_to_all.21.parts = bf16[16,64,128]{2,1,0:T(8,128)(2,1)S(1)} all-to-all(bf16[16,64,128]{2,1,0:T(8,128)(2,1)S(1)} %shard_map.78), channel_id=1, replica_groups=mesh['segment'=4,'tensor'=16,'dp'=2] {'tensor'}, dimensions={0} | all-to-all | bytes 524288 | tf_op jit(solution)/shard_map/all_to_all | solution.py:318
  25.6 0.0 copy-done.2
  25.6 0.0 copy-start.1
  25.6 0.7 shard_map.79
  26.3 0.0 copy-start
  26.3 21.7 %all_to_all.22.gathered = bf16[64,64,128]{2,1,0:T(8,128)(2,1)S(1)} all-to-all(bf16[64,64,128]{2,1,0:T(8,128)(2,1)S(1)} %shard_map.79), channel_id=1, replica_groups=mesh['segment'=4,'tensor'=16,'dp'=2] {'segment','tensor'}, dimensions={0} | all-to-all | bytes 2097152 | tf_op jit(solution)/shard_map/all_to_all | solution.py:320
  47.9 0.0 copy-done.1
  48.0 0.0 copy-done
  48.0 4.1 %shard_map.80 = (f32[256,768]{1,0:T(8,128)S(1)}, f32[32,128]{1,0:T(8,128)}) custom-call(s32[2]{0:T(128)S(1)} %copy-done.2, bf16[64,64,128]{2,1,0:T(8,128)(2,1)S(1)} %all_to_all.22.gathered, bf16[64,768]{1,0:T(8,128)(2,1)S(1)} %collective-permute-done.one, bf16[64,768]{1,0:T(8,128)(2,1)S(1)} %collective-permute-done.1.two, ...), custom_call_target="tpu_custom_call" | custom-call | flops 600000000 | bytes 5000000 | tf_op jit(solution)/shard_map/pallas_call | solution.py:225
  52.1 4.0 %collective-permute-start.3 = (bf16[256,384]{1,0:T(8,128)(2,1)S(1)}, bf16[256,384]{1,0:T(8,128)(2,1)S(1)}, u32[]{:S(2)}, u32[]{:S(2)}) collective-permute-start(bf16[256,384]{1,0:T(8,128)(2,1)S(1)} %shard_map.81), channel_id=1, source_target_pairs={{0,1},{1,0},{2,3},{3,2},{4,5},{5,4},{6,7},{7,6},{8,9},{9,8},{10,11... | collective-permute-start | bytes 589832 | tf_op jit(solution)/shard_map/ppermute | solution.py:322
  56.1 3.6 %all-to-all-start.2 = ((f32[32,1,128]{2,1,0:T(1,128)}), f32[32,1,128]{2,1,0:T(1,128)S(1)}, u32[]{:S(2)}, u32[]{:S(2)}) async-start(f32[32,1,128]{2,1,0:T(1,128)} %bitcast.5), calls=%async_computation.2 | async-start | bytes 32768 | tf_op jit(solution)/shard_map/all_to_all | solution.py:323
  60.3 6.2 %all-to-all-done.2 = f32[32,1,128]{2,1,0:T(1,128)S(1)} async-done(((f32[32,1,128]{2,1,0:T(1,128)}), f32[32,1,128]{2,1,0:T(1,128)S(1)}, u32[]{:S(2)}, u32[]{:S(2)}) %all-to-all-start.2) | async-done | bytes 16416 | tf_op jit(solution)/shard_map/all_to_all | solution.py:323
  66.6 0.0 collective-permute-done.3.swapped
  66.6 0.8 %shard_map.82 = (f32[1,64,384]{2,1,0:T(8,128)}, f32[1,64,384]{2,1,0:T(8,128)}) custom-call(f32[1]{0:T(128)S(6)} %copy.9.clip, f32[32,128]{1,0:T(8,128)S(1)} %bitcast.17, f32[256,768]{1,0:T(8,128)S(1)} %get-tuple-element.7.each, bf16[256,384]{1,0:T(8,128)(2,1)S(1)} %collective-permute-done.3.swapped), custom_call_target="tpu_custom_call" | custom-call | flops 300000 | bytes 900000 | tf_op jit(solution)/shard_map/pallas_call | solution.py:294
  (1 shorter events, 0.0 us)
Async XLA Ops:
  1.6 8.3 %collective-permute-start = (bf16[64,768]{1,0:T(8,128)(2,1)S(1)}, bf16[64,768]{1,0:T(8,128)(2,1)S(1)}, u32[]{:S(2)}, u32[]{:S(2)}) collective-permute-start(bf16[64,768]{1,0:T(8,128)(2,1)S(1)} %get-tuple-element.13.sent.to_one), channel_id=1, source_target_pairs={{0,32},{32,64},{64,96},{96,0},{1,33},{33,65},{65,97},{97,1},{2,34}... | collective-permute-start | bytes 294920 | tf_op jit(solution)/shard_map/ppermute | solution.py:313
  3.7 6.5 %collective-permute-start.1 = (bf16[64,768]{1,0:T(8,128)(2,1)S(1)}, bf16[64,768]{1,0:T(8,128)(2,1)S(1)}, u32[]{:S(2)}, u32[]{:S(2)}) collective-permute-start(bf16[64,768]{1,0:T(8,128)(2,1)S(1)} %get-tuple-element.12.to_two), channel_id=1, source_target_pairs={{0,64},{32,96},{64,0},{96,32},{1,65},{33,97},{65,1},{97,33},{2,66}... | collective-permute-start | bytes 294920 | tf_op jit(solution)/shard_map/ppermute | solution.py:313
  6.2 4.0 %collective-permute-start.2 = (bf16[64,768]{1,0:T(8,128)(2,1)S(1)}, bf16[64,768]{1,0:T(8,128)(2,1)S(1)}, u32[]{:S(2)}, u32[]{:S(2)}) collective-permute-start(bf16[64,768]{1,0:T(8,128)(2,1)S(1)} %get-tuple-element.10.to_three), channel_id=1, source_target_pairs={{0,96},{32,0},{64,32},{96,64},{1,97},{33,1},{65,33},{97,65},{2,98}... | collective-permute-start | bytes 294920 | tf_op jit(solution)/shard_map/ppermute | solution.py:313
  9.9 15.7 %copy-start.2 = (s32[2]{0:T(128)S(1)}, s32[2]{0:T(128)}, u32[]{:S(2)}) copy-start(s32[2]{0:T(128)} %lengths.3) | copy-start | bytes 28
  25.6 22.4 %copy-start.1 = (bf16[2,384,768]{2,1,0:T(8,128)(2,1)S(1)}, bf16[2,384,768]{2,1,0:T(8,128)(2,1)}, u32[]{:S(2)}) copy-start(bf16[2,384,768]{2,1,0:T(8,128)(2,1)} %cot_hbm.3) | copy-start | bytes 3538948
  26.3 21.7 %copy-start = (bf16[2,384,768]{2,1,0:T(8,128)(2,1)S(1)}, bf16[2,384,768]{2,1,0:T(8,128)(2,1)}, u32[]{:S(2)}) copy-start(bf16[2,384,768]{2,1,0:T(8,128)(2,1)} %act_hbm.3) | copy-start | bytes 3538948
  52.1 14.4 %collective-permute-start.3 = (bf16[256,384]{1,0:T(8,128)(2,1)S(1)}, bf16[256,384]{1,0:T(8,128)(2,1)S(1)}, u32[]{:S(2)}, u32[]{:S(2)}) collective-permute-start(bf16[256,384]{1,0:T(8,128)(2,1)S(1)} %shard_map.81), channel_id=1, source_target_pairs={{0,1},{1,0},{2,3},{3,2},{4,5},{5,4},{6,7},{7,6},{8,9},{9,8},{10,11... | collective-permute-start | bytes 589832 | tf_op jit(solution)/shard_map/ppermute | solution.py:322
  56.1 10.5 %all-to-all-start.2 = ((f32[32,1,128]{2,1,0:T(1,128)}), f32[32,1,128]{2,1,0:T(1,128)S(1)}, u32[]{:S(2)}, u32[]{:S(2)}) async-start(f32[32,1,128]{2,1,0:T(1,128)} %bitcast.5), calls=%async_computation.2 | async-start | bytes 32768 | tf_op jit(solution)/shard_map/all_to_all | solution.py:323

commit v5 on v4

--- a/solution.py
+++ b/solution.py
@@ -43,7 +43,9 @@
 STEP_ROWS = SLOTS // STEPS
 
 
-def project_body(act_hbm, cot_hbm, sent, kept, out, act, cot, sems):
+def project_body(
+    lengths, clip, act_hbm, cot_hbm, sent, kept, out, limits, bounds, act, cot, sems
+):
     copies = []
     for i in range(STEPS):
         rows = pl.ds(i * STEP_ROWS, STEP_ROWS)
@@ -53,6 +55,9 @@
             copy.start()
             pair.append(copy)
         copies.append(pair)
+    lane = lax.broadcasted_iota(jnp.int32, (8, LANES), 1)
+    limits[...] = jnp.where(lane < RANK, lengths[0], lengths[1])
+    bounds[...] = jnp.full((8, LANES), clip[0], F32)
     final = lax.axis_index("segment") == LAYERS - 1
     down = jnp.where(final, sent[...], kept[...]).T
     up_t = jnp.where(final, kept[...], sent[...]).T
@@ -69,12 +74,16 @@
             ).astype(BF)
 
 
-def project(act, cot, sent, kept):
+def project(lengths, clip, act, cot, sent, kept):
     return pl.pallas_call(
         project_body,
-        in_specs=[HBM, HBM, VMEM, VMEM],
-        out_specs=VMEM,
-        out_shape=jax.ShapeDtypeStruct((CUTS, 2 * PIECE, LANES), BF),
+        in_specs=[SMEM, SMEM, HBM, HBM, VMEM, VMEM],
+        out_specs=[VMEM] * 3,
+        out_shape=[
+            jax.ShapeDtypeStruct((CUTS, 2 * PIECE, LANES), BF),
+            jax.ShapeDtypeStruct((8, LANES), jnp.int32),
+            jax.ShapeDtypeStruct((8, LANES), F32),
+        ],
         scratch_shapes=[
             pltpu.VMEM((2, SLOTS, WIDTH), BF),
             pltpu.VMEM((2, SLOTS, WIDTH), BF),
@@ -82,7 +91,7 @@
         ],
         compiler_params=pltpu.CompilerParams(vmem_limit_bytes=53 << 20),
         cost_estimate=pl.CostEstimate(flops=150000000, bytes_accessed=2800000, transcendentals=0),
-    )(act, cot, sent, kept)
+    )(lengths, clip, act, cot, sent, kept)
 
 
 def weave_body(partial, to_one, to_two, to_three, one, two, three, out):
@@ -115,42 +124,36 @@
     )(partial, *messages, *peers)
 
 
-def reduce_body(lengths, parts, out):
+def reduce_body(limits, parts, out):
     base = lax.axis_index("tensor") * PIECE
     total = parts[0].astype(F32)
     for i in range(1, CUTS):
         total = total + parts[i].astype(F32)
     slot = lax.broadcasted_iota(jnp.int32, (PIECE, LANES), 0) + base
-    lane = lax.broadcasted_iota(jnp.int32, (PIECE, LANES), 1)
-    live = slot < jnp.where(lane < RANK, lengths[0], lengths[1])
+    live = slot < limits[:1]
     last = jnp.where(live, total[PIECE : 2 * PIECE], 0.0)
     message = jnp.concatenate([total[:PIECE], last, total[2 * PIECE :]], axis=0).astype(BF)
     for i in range(LAYERS * CUTS):
         out[i] = message
 
 
-def reduce_parts(lengths, parts):
+def reduce_parts(limits, parts):
     return pl.pallas_call(
         reduce_body,
-        in_specs=[SMEM, VMEM],
+        in_specs=[VMEM] * 2,
         out_specs=VMEM,
         out_shape=jax.ShapeDtypeStruct((LAYERS * CUTS, 2 * PIECE + EXTRA, LANES), BF),
         compiler_params=pltpu.CompilerParams(vmem_limit_bytes=16 << 20),
         cost_estimate=pl.CostEstimate(flops=200000, bytes_accessed=1300000, transcendentals=0),
-    )(lengths, parts)
+    )(limits, parts)
 
 
 def gradient_body(
-    lengths, gathered, one, two, three, act_hbm, cot_hbm,
+    limits, gathered, one, two, three, act, cot,
     each, note,
-    act, cot, first, last, hidden, slopes, steep, sems,
+    first, last, hidden, slopes, steep,
 ):
     seg = lax.axis_index("segment")
-    act_copy = pltpu.make_async_copy(act_hbm, act, sems.at[0])
-    cot_copy = pltpu.make_async_copy(cot_hbm, cot, sems.at[1])
-    act_copy.start()
-    cot_copy.start()
-
     packed = []
     for layer in range(LAYERS):
         tiles = []
@@ -188,8 +191,7 @@
         slopes[i] = (spread * steep[i]).astype(BF)
 
     slot = lax.broadcasted_iota(jnp.int32, (SLOTS, LANES), 0)
-    lane = lax.broadcasted_iota(jnp.int32, (SLOTS, LANES), 1)
-    live = slot < jnp.where(lane < RANK, lengths[0], lengths[1])
+    live = slot < limits[:1]
     mine_h = jnp.where(live, hidden[seg].astype(F32), 0.0).T.astype(BF)
     mine_s = slopes[seg].astype(F32).T.astype(BF)
 
@@ -206,8 +208,6 @@
         )
     left = jnp.concatenate(lefts, axis=1).astype(BF)
     peers = jnp.concatenate([one[...], two[...], three[...]], axis=0)
-    act_copy.wait()
-    cot_copy.wait()
     each[...] = dot(left, peers, 1, 0)
     for e in range(2):
         rows = slice(e * RANK, (e + 1) * RANK)
@@ -220,31 +220,28 @@
         note[:, rows] = jnp.full((2 * CUTS, RANK), square, F32)
 
 
-def gradients(lengths, gathered, peers, act, cot):
+def gradients(limits, gathered, peers, act, cot):
     wide = (LAYERS, SLOTS, LANES)
     return pl.pallas_call(
         gradient_body,
-        in_specs=[SMEM] + [VMEM] * 4 + [HBM] * 2,
+        in_specs=[VMEM] * 7,
         out_specs=[VMEM] * 2,
         out_shape=[
             jax.ShapeDtypeStruct((4 * RANK, WIDTH), F32),
             jax.ShapeDtypeStruct((2 * CUTS, LANES), F32),
         ],
         scratch_shapes=[
-            pltpu.VMEM((2, SLOTS, WIDTH), BF),
-            pltpu.VMEM((2, SLOTS, WIDTH), BF),
             pltpu.VMEM(wide, F32),
             pltpu.VMEM(wide, F32),
             pltpu.VMEM(wide, BF),
             pltpu.VMEM(wide, BF),
             pltpu.VMEM(wide, F32),
-            pltpu.SemaphoreType.DMA((2,)),
         ],
         compiler_params=pltpu.CompilerParams(vmem_limit_bytes=32 << 20),
         cost_estimate=pl.CostEstimate(
             flops=600000000, bytes_accessed=5000000, transcendentals=200000
         ),
-    )(lengths, gathered, *peers, act, cot)
+    )(limits, gathered, *peers, act, cot)
 
 
 def share_body(each, theirs):
@@ -263,7 +260,7 @@
     )(each)
 
 
-def scale_body(clip, notes, each, swapped, out_down, out_up):
+def scale_body(bounds, notes, each, swapped, out_down, out_up):
     core = lax.axis_index("dp")
     ours = each.at[:, pl.ds(pl.multiple_of(core * LOCAL, 128), LOCAL)]
     row = lax.broadcasted_iota(jnp.int32, (2 * CUTS, LANES), 0)
@@ -272,7 +269,7 @@
 
     def factors(picked):
         total = jnp.sum(jnp.where(picked, values, 0.0), axis=0, keepdims=True)
-        return clip[0] / (jnp.sqrt(total) + 0.01)
+        return bounds[:1] / (jnp.sqrt(total) + 0.01)
 
     own = factors(is_own)
     other = factors(jnp.logical_not(is_own))
@@ -290,10 +287,10 @@
     out_up[0] = combined(2 * RANK)
 
 
-def scaled(clip, notes, each, swapped):
+def scaled(bounds, notes, each, swapped):
     return pl.pallas_call(
         scale_body,
-        in_specs=[SMEM] + [VMEM] * 3,
+        in_specs=[VMEM] * 4,
         out_specs=[VMEM] * 2,
         out_shape=[
             jax.ShapeDtypeStruct((1, RANK, LOCAL), F32),
@@ -301,7 +298,7 @@
         ],
         compiler_params=pltpu.CompilerParams(vmem_limit_bytes=16 << 20),
         cost_estimate=pl.CostEstimate(flops=300000, bytes_accessed=900000, transcendentals=0),
-    )(clip, notes, each, swapped)
+    )(bounds, notes, each, swapped)
 
 
 def shards(act_input, cotangent, lengths, clip_scale, adapt_down, adapt_up):
@@ -313,15 +310,17 @@
         lax.ppermute(messages[k - 1], "segment", [(i, (i + k) % LAYERS) for i in range(LAYERS)])
         for k in range(1, LAYERS)
     ]
-    partial = project(act_input, cotangent, messages[0], jnp.where(seg + 1 < LAYERS, down_t, up))
+    partial, limits, bounds = project(
+        lengths, clip_scale, act_input, cotangent, messages[0], jnp.where(seg + 1 < LAYERS, down_t, up)
+    )
     woven = weave(partial, messages, peers)
     parts = lax.all_to_all(woven, "tensor", 0, 0, tiled=True)
-    message = reduce_parts(lengths, parts)
+    message = reduce_parts(limits, parts)
     gathered = lax.all_to_all(message, ("segment", "tensor"), 0, 0, tiled=True)
-    each, note = gradients(lengths, gathered, peers, act_input, cotangent)
+    each, note = gradients(limits, gathered, peers, act_input, cotangent)
     swapped = lax.ppermute(share(each), "dp", [(0, 1), (1, 0)])
     notes = lax.all_to_all(note, ("tensor", "dp"), 0, 0, tiled=True)
-    grad_down, grad_up = scaled(clip_scale, notes, each, swapped)
+    grad_down, grad_up = scaled(bounds, notes, each, swapped)
     return jnp.swapaxes(grad_down, 1, 2), grad_up
 
 

time: 67.7 us -> 65.2 us (0.963)
  blocking collectives: 36.8 us -> 45 us
  starting transfers between devices: 13.3 us -> 8 us
  waiting for transfers between devices: 6.48 us -> 2.15 us
  Pallas kernels: 8.42 us -> 6.74 us
    all_to_all x0 -> x1, blocking collectives: none -> 9.84 us  [shards(): notes = lax.all_to_all(note, ('tensor', 'dp'), 0, 0, tiled=True)]
    all_to_all x1 -> x0, waiting for transfers between devices: 6.22 us -> none  [shards(): notes = lax.all_to_all(note, ('tensor', 'dp'), 0, 0, tiled=True)]
    all_to_all x1 -> x0, starting transfers between devices: 3.61 us -> none  [shards(): notes = lax.all_to_all(note, ('tensor', 'dp'), 0, 0, tiled=True)]
    ppermute x3, waiting for transfers between devices: 0.26 us -> 2.15 us  [shards(): lax.ppermute(messages[k - 1], 'segment', [(i, (i + k) % LAYERS) for i in...]
    pallas_call x4, Pallas kernels: 8.17 us -> 6.48 us  [the longest x1 3.11 us: project(): pl.pallas_call(project_body, in_specs=[SMEM, SMEM, HBM, HBM, VMEM, VMEM],...]
    all_to_all x1, blocking collectives: 21.7 us -> 20 us  [shards(): gathered = lax.all_to_all(message, ('segment', 'tensor'), 0, 0, tiled=True)]
    ppermute x3, starting transfers between devices: 5.71 us -> 4.5 us  [shards(): lax.ppermute(messages[k - 1], 'segment', [(i, (i + k) % LAYERS) for i in...]
  transfers between devices with their start and end apart: 5 -> 4, of which waited for: 2 -> 1; matrix products, arithmetic and copies ran while one was open for 0% -> 0% of each run, Pallas kernels for 4% -> 5%
where the time goes in v5:
time: 65.2 us; the launch traced here: 64.9 us
  blocking collectives  45 us (69%)
  starting transfers between devices  8 us (12%)
  Pallas kernels  6.74 us (10%)
  waiting for transfers between devices  2.15 us (3%)
  between operations  1.37 us (2%)
  other arithmetic  0.97 us (1%)
  local copies, waits for them, and re-layouts  0.66 us (1%)
    all_to_all x1, blocking collectives, shards(): gathered = lax.all_to_all(message, ('segment', 'tensor'), 0, 0, tiled=True)  20 us
    all_to_all x1, blocking collectives, shards(): parts = lax.all_to_all(woven, 'tensor', 0, 0, tiled=True)  15.2 us
    all_to_all x1, blocking collectives, shards(): notes = lax.all_to_all(note, ('tensor', 'dp'), 0, 0, tiled=True)  9.84 us
    ppermute x3, starting transfers between devices, shards(): lax.ppermute(messages[k - 1], 'segment', [(i, (i + k) % LAYERS) for i in...  4.5 us
    ppermute x1, starting transfers between devices, shards(): swapped = lax.ppermute(share(each), 'dp', [(0, 1), (1, 0)])  3.49 us
    pallas_call x1, Pallas kernels, project(): pl.pallas_call(project_body, in_specs=[SMEM, SMEM, HBM, HBM, VMEM, VMEM],...  3.11 us
    pallas_call x1, Pallas kernels, gradients(): pl.pallas_call(gradient_body, in_specs=[VMEM] * 7, out_specs=[VMEM] * 2,...  2.42 us
    ppermute x3, waiting for transfers between devices, shards(): lax.ppermute(messages[k - 1], 'segment', [(i, (i + k) % LAYERS) for i in...  2.15 us
  transfers between devices with their start and end apart: 4, of which 1 were waited for; matrix products, arithmetic and copies ran while one was open for 0% of the time, Pallas kernels for 5%

profile of v5, /device:TPU:1, one launch (start us, length us, event | category | flops | bytes accessed | tf_op | source)
XLA Modules:
  0.0 64.9 jit_solution(15866890130242924573)
XLA Ops:
  0.6 1.0 %bitcast_select_fusion = (bf16[64,768]{1,0:T(8,128)(2,1)S(1)}, bf16[64,768]{1,0:T(8,128)(2,1)S(1)}, bf16[64,768]{1,0:T(8,128)(2,1)S(1)}, bf16[64,768]{1,0:T(8,128)(2,1)S(1)}) fusion(bf16[1,768,64]{1,2,0:T(8,128)(2,1)} %param.10, bf16[1,64,768]{2,1,0:T(8,128)(2,1)} %param.11, pred[]{:T(512)S(6)} %lt.12, pred[]{:T(512)S(6)} %lt.10, pred[]{:T(512)S(6)} %lt.11), kind=kLoop, calls=%fused_computation | loop fusion | flops 196608 | bytes 589827 | tf_op jit(solution)/shard_map/jit(_where)/select_n | solution.py:308
  1.6 3.4 %collective-permute-start.2 = (bf16[64,768]{1,0:T(8,128)(2,1)S(1)}, bf16[64,768]{1,0:T(8,128)(2,1)S(1)}, u32[]{:S(2)}, u32[]{:S(2)}) collective-permute-start(bf16[64,768]{1,0:T(8,128)(2,1)S(1)} %get-tuple-element.16.to_three), channel_id=1, source_target_pairs={{0,96},{32,0},{64,32},{96,64},{1,97},{33,1},{65,33},{97,65},{2,98}... | collective-permute-start | bytes 294920 | tf_op jit(solution)/shard_map/ppermute | solution.py:310
  5.0 0.5 collective-permute-start.1
  5.5 0.6 collective-permute-start
  6.8 0.0 copy-start.2
  6.8 0.6 copy-done.2
  7.4 3.1 %shard_map.77 = (bf16[16,48,128]{2,1,0:T(8,128)(2,1)S(1)}, s32[8,128]{1,0:T(8,128)S(1)}, f32[8,128]{1,0:T(8,128)S(1)}) custom-call(s32[2]{0:T(128)S(1)} %copy-done.2, f32[1]{0:T(128)S(6)} %copy.9.clip, bf16[2,384,768]{2,1,0:T(8,128)(2,1)} %act.1, bf16[2,384,768]{2,1,0:T(8,128)(2,1)} %cot.1, bf16[64,768]{1,0:T(8,128)(2,1)S(1)} %get-tuple-element.19.sent.to_one, ...), custom_call_target="tpu_custom_call" | custom-call | flops 150000000 | bytes 2800000 | tf_op jit(solution)/shard_map/pallas_call | solution.py:78
  10.5 0.0 collective-permute-done.2.three
  10.6 0.0 collective-permute-done.1.two
  10.6 2.1 %collective-permute-done.one = bf16[64,768]{1,0:T(8,128)(2,1)S(1)} collective-permute-done((bf16[64,768]{1,0:T(8,128)(2,1)S(1)}, bf16[64,768]{1,0:T(8,128)(2,1)S(1)}, u32[]{:S(2)}, u32[]{:S(2)}) %collective-permute-start) | collective-permute-done | bytes 98336 | tf_op jit(solution)/shard_map/ppermute | solution.py:310
  12.7 0.2 shard_map.78
  12.9 15.2 %all_to_all.21.parts = bf16[16,64,128]{2,1,0:T(8,128)(2,1)S(1)} all-to-all(bf16[16,64,128]{2,1,0:T(8,128)(2,1)S(1)} %shard_map.78), channel_id=1, replica_groups=mesh['segment'=4,'tensor'=16,'dp'=2] {'tensor'}, dimensions={0} | all-to-all | bytes 524288 | tf_op jit(solution)/shard_map/all_to_all | solution.py:317
  28.1 0.0 copy-start.1
  28.1 0.1 shard_map.79
  28.3 0.0 copy-start
  28.3 20.0 %all_to_all.22.gathered = bf16[64,64,128]{2,1,0:T(8,128)(2,1)S(1)} all-to-all(bf16[64,64,128]{2,1,0:T(8,128)(2,1)S(1)} %shard_map.79), channel_id=1, replica_groups=mesh['segment'=4,'tensor'=16,'dp'=2] {'segment','tensor'}, dimensions={0} | all-to-all | bytes 2097152 | tf_op jit(solution)/shard_map/all_to_all | solution.py:319
  48.3 0.0 copy-done.1
  48.3 0.0 copy-done
  48.3 2.4 %shard_map.80 = (f32[256,768]{1,0:T(8,128)S(1)}, f32[32,128]{1,0:T(8,128)S(1)}) custom-call(s32[8,128]{1,0:T(8,128)S(1)} %get-tuple-element.10.limits, bf16[64,64,128]{2,1,0:T(8,128)(2,1)S(1)} %all_to_all.22.gathered, bf16[64,768]{1,0:T(8,128)(2,1)S(1)} %collective-permute-done.one, bf16[64,768]{1,0:T(8,128)(2,1)S(1)} %collective-permute-done.1.two, ...), custom_call_target="tpu_custom_call" | custom-call | flops 600000000 | bytes 5000000 | tf_op jit(solution)/shard_map/pallas_call | solution.py:225
  50.8 3.5 %collective-permute-start.3 = (bf16[256,384]{1,0:T(8,128)(2,1)S(1)}, bf16[256,384]{1,0:T(8,128)(2,1)S(1)}, u32[]{:S(2)}, u32[]{:S(2)}) collective-permute-start(bf16[256,384]{1,0:T(8,128)(2,1)S(1)} %shard_map.81), channel_id=1, source_target_pairs={{0,1},{1,0},{2,3},{3,2},{4,5},{5,4},{6,7},{7,6},{8,9},{9,8},{10,11... | collective-permute-start | bytes 589832 | tf_op jit(solution)/shard_map/ppermute | solution.py:321
  54.3 9.8 %all_to_all.23 = f32[32,1,128]{2,1,0:T(1,128)S(1)} all-to-all(f32[32,1,128]{2,1,0:T(1,128)S(1)} %bitcast.18), channel_id=1, replica_groups=mesh['segment'=4,'tensor'=16,'dp'=2] {'tensor','dp'}, dimensions={0} | all-to-all | bytes 32768 | tf_op jit(solution)/shard_map/all_to_all | solution.py:322
  64.1 0.0 collective-permute-done.3.swapped
  64.1 0.8 %shard_map.82 = (f32[1,64,384]{2,1,0:T(8,128)}, f32[1,64,384]{2,1,0:T(8,128)}) custom-call(f32[8,128]{1,0:T(8,128)S(1)} %get-tuple-element.9.bounds, f32[32,128]{1,0:T(8,128)S(1)} %bitcast.17, f32[256,768]{1,0:T(8,128)S(1)} %get-tuple-element.13.each, bf16[256,384]{1,0:T(8,128)(2,1)S(1)} %collective-permute-done.3.swapped), custom_call_target="tpu_custom_call" | custom-call | flops 300000 | bytes 900000 | tf_op jit(solution)/shard_map/pallas_call | solution.py:291
  (1 shorter events, 0.0 us)
Async XLA Ops:
  1.6 8.9 %collective-permute-start.2 = (bf16[64,768]{1,0:T(8,128)(2,1)S(1)}, bf16[64,768]{1,0:T(8,128)(2,1)S(1)}, u32[]{:S(2)}, u32[]{:S(2)}) collective-permute-start(bf16[64,768]{1,0:T(8,128)(2,1)S(1)} %get-tuple-element.16.to_three), channel_id=1, source_target_pairs={{0,96},{32,0},{64,32},{96,64},{1,97},{33,1},{65,33},{97,65},{2,98}... | collective-permute-start | bytes 294920 | tf_op jit(solution)/shard_map/ppermute | solution.py:310
  5.0 5.6 %collective-permute-start.1 = (bf16[64,768]{1,0:T(8,128)(2,1)S(1)}, bf16[64,768]{1,0:T(8,128)(2,1)S(1)}, u32[]{:S(2)}, u32[]{:S(2)}) collective-permute-start(bf16[64,768]{1,0:T(8,128)(2,1)S(1)} %get-tuple-element.18.to_two), channel_id=1, source_target_pairs={{0,64},{32,96},{64,0},{96,32},{1,65},{33,97},{65,1},{97,33},{2,66}... | collective-permute-start | bytes 294920 | tf_op jit(solution)/shard_map/ppermute | solution.py:310
  5.5 7.2 %collective-permute-start = (bf16[64,768]{1,0:T(8,128)(2,1)S(1)}, bf16[64,768]{1,0:T(8,128)(2,1)S(1)}, u32[]{:S(2)}, u32[]{:S(2)}) collective-permute-start(bf16[64,768]{1,0:T(8,128)(2,1)S(1)} %get-tuple-element.19.sent.to_one), channel_id=1, source_target_pairs={{0,32},{32,64},{64,96},{96,0},{1,33},{33,65},{65,97},{97,1},{2,34}... | collective-permute-start | bytes 294920 | tf_op jit(solution)/shard_map/ppermute | solution.py:310
  6.8 0.7 %copy-start.2 = (s32[2]{0:T(128)S(1)}, s32[2]{0:T(128)}, u32[]{:S(2)}) copy-start(s32[2]{0:T(128)} %lengths.1) | copy-start | bytes 28
  28.1 20.2 %copy-start.1 = (bf16[2,384,768]{2,1,0:T(8,128)(2,1)S(1)}, bf16[2,384,768]{2,1,0:T(8,128)(2,1)}, u32[]{:S(2)}) copy-start(bf16[2,384,768]{2,1,0:T(8,128)(2,1)} %cot.1) | copy-start | bytes 3538948
  28.3 20.0 %copy-start = (bf16[2,384,768]{2,1,0:T(8,128)(2,1)S(1)}, bf16[2,384,768]{2,1,0:T(8,128)(2,1)}, u32[]{:S(2)}) copy-start(bf16[2,384,768]{2,1,0:T(8,128)(2,1)} %act.1) | copy-start | bytes 3538948
  50.8 13.3 %collective-permute-start.3 = (bf16[256,384]{1,0:T(8,128)(2,1)S(1)}, bf16[256,384]{1,0:T(8,128)(2,1)S(1)}, u32[]{:S(2)}, u32[]{:S(2)}) collective-permute-start(bf16[256,384]{1,0:T(8,128)(2,1)S(1)} %shard_map.81), channel_id=1, source_target_pairs={{0,1},{1,0},{2,3},{3,2},{4,5},{5,4},{6,7},{7,6},{8,9},{9,8},{10,11... | collective-permute-start | bytes 589832 | tf_op jit(solution)/shard_map/ppermute | solution.py:321

commit v6 on v5

--- a/solution.py
+++ b/solution.py
@@ -21,7 +21,7 @@
 HALF = RANK // 2
 LANES = 2 * RANK
 PIECE = SLOTS // CUTS
-EXTRA = 16
+EXTRA = 8
 LOCAL = WIDTH // 2
 
 
@@ -103,14 +103,13 @@
         gram = dot(left, right, 1, 1)
         gram = jnp.concatenate([gram, jnp.zeros_like(gram)], axis=1)
         for q in range(4):
+            t = (k - 1) * 4 + q
             tile = gram[q * 8 : (q + 1) * 8]
-            out[(k - 1) * 4 + q, 2 * PIECE :] = jnp.concatenate(
-                [tile, jnp.zeros_like(tile)], axis=0
-            ).astype(BF)
-    for t in range(CUTS):
-        out[t, : 2 * PIECE] = partial[t]
+            out[t] = jnp.concatenate([partial[t].astype(F32), tile], axis=0).astype(BF)
     for t in range(12, CUTS):
-        out[t, 2 * PIECE :] = jnp.zeros((EXTRA, LANES), BF)
+        out[t] = jnp.concatenate(
+            [partial[t].astype(F32), jnp.zeros((EXTRA, LANES), F32)], axis=0
+        ).astype(BF)
 
 
 def weave(partial, messages, peers):

time: 65.2 us -> 63.6 us (0.975)
  blocking collectives: 45 us -> 43.4 us
    all_to_all x1, blocking collectives: 20 us -> 18.7 us  [shards(): gathered = lax.all_to_all(message, ('segment', 'tensor'), 0, 0, tiled=True)]
where the time goes in v6:
time: 63.6 us; the launch traced here: 63.3 us
  blocking collectives  43.4 us (68%)
  starting transfers between devices  8.06 us (13%)
  Pallas kernels  6.67 us (10%)
  waiting for transfers between devices  2.15 us (3%)
  between operations  1.37 us (2%)
  other arithmetic  0.97 us (2%)
  local copies, waits for them, and re-layouts  0.66 us (1%)
    all_to_all x1, blocking collectives, shards(): gathered = lax.all_to_all(message, ('segment', 'tensor'), 0, 0, tiled=True)  18.7 us
    all_to_all x1, blocking collectives, shards(): parts = lax.all_to_all(woven, 'tensor', 0, 0, tiled=True)  14.9 us
    all_to_all x1, blocking collectives, shards(): notes = lax.all_to_all(note, ('tensor', 'dp'), 0, 0, tiled=True)  9.79 us
    ppermute x3, starting transfers between devices, shards(): lax.ppermute(messages[k - 1], 'segment', [(i, (i + k) % LAYERS) for i in...  4.5 us
    ppermute x1, starting transfers between devices, shards(): swapped = lax.ppermute(share(each), 'dp', [(0, 1), (1, 0)])  3.56 us
    pallas_call x1, Pallas kernels, project(): pl.pallas_call(project_body, in_specs=[SMEM, SMEM, HBM, HBM, VMEM, VMEM],...  3.11 us
    pallas_call x1, Pallas kernels, gradients(): pl.pallas_call(gradient_body, in_specs=[VMEM] * 7, out_specs=[VMEM] * 2,...  2.41 us
    ppermute x3, waiting for transfers between devices, shards(): lax.ppermute(messages[k - 1], 'segment', [(i, (i + k) % LAYERS) for i in...  2.15 us
  transfers between devices with their start and end apart: 4, of which 1 were waited for; matrix products, arithmetic and copies ran while one was open for 0% of the time, Pallas kernels for 5%

profile of v6, /device:TPU:1, one launch (start us, length us, event | category | flops | bytes accessed | tf_op | source)
XLA Modules:
  0.0 63.3 jit_solution(15408875620755148135)
XLA Ops:
  0.6 1.0 %bitcast_select_fusion = (bf16[64,768]{1,0:T(8,128)(2,1)S(1)}, bf16[64,768]{1,0:T(8,128)(2,1)S(1)}, bf16[64,768]{1,0:T(8,128)(2,1)S(1)}, bf16[64,768]{1,0:T(8,128)(2,1)S(1)}) fusion(bf16[1,768,64]{1,2,0:T(8,128)(2,1)} %param.10, bf16[1,64,768]{2,1,0:T(8,128)(2,1)} %param.11, pred[]{:T(512)S(6)} %lt.12, pred[]{:T(512)S(6)} %lt.10, pred[]{:T(512)S(6)} %lt.11), kind=kLoop, calls=%fused_computation | loop fusion | flops 196608 | bytes 589827 | tf_op jit(solution)/shard_map/jit(_where)/select_n | solution.py:307
  1.6 3.4 %collective-permute-start.2 = (bf16[64,768]{1,0:T(8,128)(2,1)S(1)}, bf16[64,768]{1,0:T(8,128)(2,1)S(1)}, u32[]{:S(2)}, u32[]{:S(2)}) collective-permute-start(bf16[64,768]{1,0:T(8,128)(2,1)S(1)} %get-tuple-element.16.to_three), channel_id=1, source_target_pairs={{0,96},{32,0},{64,32},{96,64},{1,97},{33,1},{65,33},{97,65},{2,98}... | collective-permute-start | bytes 294920 | tf_op jit(solution)/shard_map/ppermute | solution.py:309
  5.0 0.5 collective-permute-start.1
  5.5 0.6 collective-permute-start
  6.8 0.0 copy-start.2
  6.8 0.6 %copy-done.2 = s32[2]{0:T(128)S(1)} copy-done((s32[2]{0:T(128)S(1)}, s32[2]{0:T(128)}, u32[]{:S(2)}) %copy-start.2) | copy-done | bytes 32
  7.4 3.1 %shard_map.77 = (bf16[16,48,128]{2,1,0:T(8,128)(2,1)S(1)}, s32[8,128]{1,0:T(8,128)S(1)}, f32[8,128]{1,0:T(8,128)S(1)}) custom-call(s32[2]{0:T(128)S(1)} %copy-done.2, f32[1]{0:T(128)S(6)} %copy.9.clip, bf16[2,384,768]{2,1,0:T(8,128)(2,1)} %act.1, bf16[2,384,768]{2,1,0:T(8,128)(2,1)} %cot.1, bf16[64,768]{1,0:T(8,128)(2,1)S(1)} %get-tuple-element.19.sent.to_one, ...), custom_call_target="tpu_custom_call" | custom-call | flops 150000000 | bytes 2800000 | tf_op jit(solution)/shard_map/pallas_call | solution.py:78
  10.5 0.0 collective-permute-done.2.three
  10.6 0.0 collective-permute-done.1.two
  10.6 2.1 %collective-permute-done.one = bf16[64,768]{1,0:T(8,128)(2,1)S(1)} collective-permute-done((bf16[64,768]{1,0:T(8,128)(2,1)S(1)}, bf16[64,768]{1,0:T(8,128)(2,1)S(1)}, u32[]{:S(2)}, u32[]{:S(2)}) %collective-permute-start) | collective-permute-done | bytes 98336 | tf_op jit(solution)/shard_map/ppermute | solution.py:309
  12.7 0.2 shard_map.78
  12.9 14.9 %all_to_all.21.parts = bf16[16,56,128]{2,1,0:T(8,128)(2,1)S(1)} all-to-all(bf16[16,56,128]{2,1,0:T(8,128)(2,1)S(1)} %shard_map.78), channel_id=1, replica_groups=mesh['segment'=4,'tensor'=16,'dp'=2] {'tensor'}, dimensions={0} | all-to-all | bytes 458752 | tf_op jit(solution)/shard_map/all_to_all | solution.py:316
  27.9 0.0 copy-start.1
  27.9 0.1 shard_map.79
  28.0 0.0 copy-start
  28.0 18.7 %all_to_all.22.gathered = bf16[64,56,128]{2,1,0:T(8,128)(2,1)S(1)} all-to-all(bf16[64,56,128]{2,1,0:T(8,128)(2,1)S(1)} %shard_map.79), channel_id=1, replica_groups=mesh['segment'=4,'tensor'=16,'dp'=2] {'segment','tensor'}, dimensions={0} | all-to-all | bytes 1835008 | tf_op jit(solution)/shard_map/all_to_all | solution.py:318
  46.6 0.0 copy-done.1
  46.6 0.0 copy-done
  46.6 2.4 %shard_map.80 = (f32[256,768]{1,0:T(8,128)S(1)}, f32[32,128]{1,0:T(8,128)S(1)}) custom-call(s32[8,128]{1,0:T(8,128)S(1)} %get-tuple-element.10.limits, bf16[64,56,128]{2,1,0:T(8,128)(2,1)S(1)} %all_to_all.22.gathered, bf16[64,768]{1,0:T(8,128)(2,1)S(1)} %collective-permute-done.one, bf16[64,768]{1,0:T(8,128)(2,1)S(1)} %collective-permute-done.1.two, ...), custom_call_target="tpu_custom_call" | custom-call | flops 600000000 | bytes 5000000 | tf_op jit(solution)/shard_map/pallas_call | solution.py:224
  49.1 3.6 %collective-permute-start.3 = (bf16[256,384]{1,0:T(8,128)(2,1)S(1)}, bf16[256,384]{1,0:T(8,128)(2,1)S(1)}, u32[]{:S(2)}, u32[]{:S(2)}) collective-permute-start(bf16[256,384]{1,0:T(8,128)(2,1)S(1)} %shard_map.81), channel_id=1, source_target_pairs={{0,1},{1,0},{2,3},{3,2},{4,5},{5,4},{6,7},{7,6},{8,9},{9,8},{10,11... | collective-permute-start | bytes 589832 | tf_op jit(solution)/shard_map/ppermute | solution.py:320
  52.7 9.8 %all_to_all.23 = f32[32,1,128]{2,1,0:T(1,128)S(1)} all-to-all(f32[32,1,128]{2,1,0:T(1,128)S(1)} %bitcast.18), channel_id=1, replica_groups=mesh['segment'=4,'tensor'=16,'dp'=2] {'tensor','dp'}, dimensions={0} | all-to-all | bytes 32768 | tf_op jit(solution)/shard_map/all_to_all | solution.py:321
  62.5 0.0 collective-permute-done.3.swapped
  62.5 0.8 %shard_map.82 = (f32[1,64,384]{2,1,0:T(8,128)}, f32[1,64,384]{2,1,0:T(8,128)}) custom-call(f32[8,128]{1,0:T(8,128)S(1)} %get-tuple-element.9.bounds, f32[32,128]{1,0:T(8,128)S(1)} %bitcast.17, f32[256,768]{1,0:T(8,128)S(1)} %get-tuple-element.13.each, bf16[256,384]{1,0:T(8,128)(2,1)S(1)} %collective-permute-done.3.swapped), custom_call_target="tpu_custom_call" | custom-call | flops 300000 | bytes 900000 | tf_op jit(solution)/shard_map/pallas_call | solution.py:290
  (1 shorter events, 0.0 us)
Async XLA Ops:
  1.6 8.9 %collective-permute-start.2 = (bf16[64,768]{1,0:T(8,128)(2,1)S(1)}, bf16[64,768]{1,0:T(8,128)(2,1)S(1)}, u32[]{:S(2)}, u32[]{:S(2)}) collective-permute-start(bf16[64,768]{1,0:T(8,128)(2,1)S(1)} %get-tuple-element.16.to_three), channel_id=1, source_target_pairs={{0,96},{32,0},{64,32},{96,64},{1,97},{33,1},{65,33},{97,65},{2,98}... | collective-permute-start | bytes 294920 | tf_op jit(solution)/shard_map/ppermute | solution.py:309
  5.0 5.6 %collective-permute-start.1 = (bf16[64,768]{1,0:T(8,128)(2,1)S(1)}, bf16[64,768]{1,0:T(8,128)(2,1)S(1)}, u32[]{:S(2)}, u32[]{:S(2)}) collective-permute-start(bf16[64,768]{1,0:T(8,128)(2,1)S(1)} %get-tuple-element.18.to_two), channel_id=1, source_target_pairs={{0,64},{32,96},{64,0},{96,32},{1,65},{33,97},{65,1},{97,33},{2,66}... | collective-permute-start | bytes 294920 | tf_op jit(solution)/shard_map/ppermute | solution.py:309
  5.5 7.2 %collective-permute-start = (bf16[64,768]{1,0:T(8,128)(2,1)S(1)}, bf16[64,768]{1,0:T(8,128)(2,1)S(1)}, u32[]{:S(2)}, u32[]{:S(2)}) collective-permute-start(bf16[64,768]{1,0:T(8,128)(2,1)S(1)} %get-tuple-element.19.sent.to_one), channel_id=1, source_target_pairs={{0,32},{32,64},{64,96},{96,0},{1,33},{33,65},{65,97},{97,1},{2,34}... | collective-permute-start | bytes 294920 | tf_op jit(solution)/shard_map/ppermute | solution.py:309
  6.8 0.7 %copy-start.2 = (s32[2]{0:T(128)S(1)}, s32[2]{0:T(128)}, u32[]{:S(2)}) copy-start(s32[2]{0:T(128)} %lengths.1) | copy-start | bytes 28
  27.9 18.8 %copy-start.1 = (bf16[2,384,768]{2,1,0:T(8,128)(2,1)S(1)}, bf16[2,384,768]{2,1,0:T(8,128)(2,1)}, u32[]{:S(2)}) copy-start(bf16[2,384,768]{2,1,0:T(8,128)(2,1)} %cot.1) | copy-start | bytes 3538948
  28.0 18.7 %copy-start = (bf16[2,384,768]{2,1,0:T(8,128)(2,1)S(1)}, bf16[2,384,768]{2,1,0:T(8,128)(2,1)}, u32[]{:S(2)}) copy-start(bf16[2,384,768]{2,1,0:T(8,128)(2,1)} %act.1) | copy-start | bytes 3538948
  49.1 13.4 %collective-permute-start.3 = (bf16[256,384]{1,0:T(8,128)(2,1)S(1)}, bf16[256,384]{1,0:T(8,128)(2,1)S(1)}, u32[]{:S(2)}, u32[]{:S(2)}) collective-permute-start(bf16[256,384]{1,0:T(8,128)(2,1)S(1)} %shard_map.81), channel_id=1, source_target_pairs={{0,1},{1,0},{2,3},{3,2},{4,5},{5,4},{6,7},{7,6},{8,9},{9,8},{10,11... | collective-permute-start | bytes 589832 | tf_op jit(solution)/shard_map/ppermute | solution.py:320

commit v7 on v6

--- a/solution.py
+++ b/solution.py
@@ -10,7 +10,6 @@
 BF = jnp.bfloat16
 F32 = jnp.float32
 VMEM = pl.BlockSpec(memory_space=pltpu.VMEM)
-SMEM = pl.BlockSpec(memory_space=pltpu.SMEM)
 HBM = pl.BlockSpec(memory_space=pltpu.HBM)
 
 LAYERS = 4
@@ -43,9 +42,7 @@
 STEP_ROWS = SLOTS // STEPS
 
 
-def project_body(
-    lengths, clip, act_hbm, cot_hbm, sent, kept, out, limits, bounds, act, cot, sems
-):
+def project_body(act_hbm, cot_hbm, sent, kept, out, act, cot, sems):
     copies = []
     for i in range(STEPS):
         rows = pl.ds(i * STEP_ROWS, STEP_ROWS)
@@ -55,12 +52,9 @@
             copy.start()
             pair.append(copy)
         copies.append(pair)
-    lane = lax.broadcasted_iota(jnp.int32, (8, LANES), 1)
-    limits[...] = jnp.where(lane < RANK, lengths[0], lengths[1])
-    bounds[...] = jnp.full((8, LANES), clip[0], F32)
-    final = lax.axis_index("segment") == LAYERS - 1
-    down = jnp.where(final, sent[...], kept[...]).T
-    up_t = jnp.where(final, kept[...], sent[...]).T
+    begin = lax.axis_index("segment") == 0
+    down = jnp.where(begin, kept[...], sent[...]).T
+    up_t = jnp.where(begin, sent[...], kept[...]).T
     for i in range(STEPS):
         rows = pl.ds(i * STEP_ROWS, STEP_ROWS)
         copies[i][0].wait()
@@ -74,16 +68,12 @@
             ).astype(BF)
 
 
-def project(lengths, clip, act, cot, sent, kept):
+def project(act, cot, sent, kept):
     return pl.pallas_call(
         project_body,
-        in_specs=[SMEM, SMEM, HBM, HBM, VMEM, VMEM],
-        out_specs=[VMEM] * 3,
-        out_shape=[
-            jax.ShapeDtypeStruct((CUTS, 2 * PIECE, LANES), BF),
-            jax.ShapeDtypeStruct((8, LANES), jnp.int32),
-            jax.ShapeDtypeStruct((8, LANES), F32),
-        ],
+        in_specs=[HBM, HBM, VMEM, VMEM],
+        out_specs=VMEM,
+        out_shape=jax.ShapeDtypeStruct((CUTS, 2 * PIECE, LANES), BF),
         scratch_shapes=[
             pltpu.VMEM((2, SLOTS, WIDTH), BF),
             pltpu.VMEM((2, SLOTS, WIDTH), BF),
@@ -91,10 +81,15 @@
         ],
         compiler_params=pltpu.CompilerParams(vmem_limit_bytes=53 << 20),
         cost_estimate=pl.CostEstimate(flops=150000000, bytes_accessed=2800000, transcendentals=0),
-    )(lengths, clip, act, cot, sent, kept)
-
-
-def weave_body(partial, to_one, to_two, to_three, one, two, three, out):
+    )(act, cot, sent, kept)
+
+
+def weave_body(
+    lengths, clip, partial, to_three, to_two, to_one, three, two, one, out, limits, bounds
+):
+    lane = lax.broadcasted_iota(jnp.int32, (8, LANES), 1)
+    limits[...] = jnp.where(lane < RANK, lengths[:, :1], lengths[:, 1:])
+    bounds[...] = jnp.broadcast_to(clip[...], (8, LANES))
     seg = lax.axis_index("segment")
     for k, own, other in ((1, to_three, one), (2, to_two, two), (3, to_one, three)):
         lower = seg >= k
@@ -112,15 +107,19 @@
         ).astype(BF)
 
 
-def weave(partial, messages, peers):
+def weave(lengths, clip, partial, messages, peers):
     return pl.pallas_call(
         weave_body,
-        in_specs=[VMEM] * 7,
-        out_specs=VMEM,
-        out_shape=jax.ShapeDtypeStruct((CUTS, 2 * PIECE + EXTRA, LANES), BF),
+        in_specs=[VMEM] * 9,
+        out_specs=[VMEM] * 3,
+        out_shape=[
+            jax.ShapeDtypeStruct((CUTS, 2 * PIECE + EXTRA, LANES), BF),
+            jax.ShapeDtypeStruct((8, LANES), jnp.int32),
+            jax.ShapeDtypeStruct((8, LANES), F32),
+        ],
         compiler_params=pltpu.CompilerParams(vmem_limit_bytes=16 << 20),
         cost_estimate=pl.CostEstimate(flops=10000000, bytes_accessed=1000000, transcendentals=0),
-    )(partial, *messages, *peers)
+    )(lengths, clip, partial, messages[2], messages[1], messages[0], peers[2], peers[1], peers[0])
 
 
 def reduce_body(limits, parts, out):
@@ -240,7 +239,7 @@
         cost_estimate=pl.CostEstimate(
             flops=600000000, bytes_accessed=5000000, transcendentals=200000
         ),
-    )(limits, gathered, *peers, act, cot)
+    )(limits, gathered, peers[0], peers[1], peers[2], act, cot)
 
 
 def share_body(each, theirs):
@@ -309,10 +308,12 @@
         lax.ppermute(messages[k - 1], "segment", [(i, (i + k) % LAYERS) for i in range(LAYERS)])
         for k in range(1, LAYERS)
     ]
-    partial, limits, bounds = project(
-        lengths, clip_scale, act_input, cotangent, messages[0], jnp.where(seg + 1 < LAYERS, down_t, up)
+    partial = project(
+        act_input, cotangent, messages[2], jnp.where(seg + 3 < LAYERS, down_t, up)
     )
-    woven = weave(partial, messages, peers)
+    woven, limits, bounds = weave(
+        lengths.reshape(1, 2), clip_scale.reshape(1, 1), partial, messages, peers
+    )
     parts = lax.all_to_all(woven, "tensor", 0, 0, tiled=True)
     message = reduce_parts(limits, parts)
     gathered = lax.all_to_all(message, ("segment", "tensor"), 0, 0, tiled=True)

time: 63.6 us -> 63.2 us (level)
  waiting for transfers between devices: 2.15 us -> 0.01 us
  starting transfers between devices: 8.06 us -> 9.89 us
  blocking collectives: 43.4 us -> 44.5 us
  local copies, waits for them, and re-layouts: 0.66 us -> 0.02 us
    ppermute x3, waiting for transfers between devices: 2.15 us -> 0.01 us  [shards(): lax.ppermute(messages[k - 1], 'segment', [(i, (i + k) % LAYERS) for i in...]
    ppermute x3, starting transfers between devices: 4.5 us -> 5.71 us  [shards(): lax.ppermute(messages[k - 1], 'segment', [(i, (i + k) % LAYERS) for i in...]
    all_to_all x1, blocking collectives: 18.7 us -> 19.7 us  [shards(): gathered = lax.all_to_all(message, ('segment', 'tensor'), 0, 0, tiled=True)]
    unnamed x6, local copies, waits for them, and re-layouts: 0.66 us -> 0.02 us
  transfers between devices with their start and end apart: 4 -> 4, of which waited for: 1 -> 0; matrix products, arithmetic and copies ran while one was open for 0% -> 0% of each run, Pallas kernels for 5% -> 4%
where the time goes in v7:
time: 63.2 us; the launch traced here: 62.9 us
  blocking collectives  44.5 us (70%)
  starting transfers between devices  9.89 us (16%)
  Pallas kernels  6.17 us (10%)
  between operations  1.38 us (2%)
  other arithmetic  0.97 us (2%)
    all_to_all x1, blocking collectives, shards(): gathered = lax.all_to_all(message, ('segment', 'tensor'), 0, 0, tiled=True)  19.7 us
    all_to_all x1, blocking collectives, shards(): parts = lax.all_to_all(woven, 'tensor', 0, 0, tiled=True)  14.9 us
    all_to_all x1, blocking collectives, shards(): notes = lax.all_to_all(note, ('tensor', 'dp'), 0, 0, tiled=True)  9.79 us
    ppermute x3, starting transfers between devices, shards(): lax.ppermute(messages[k - 1], 'segment', [(i, (i + k) % LAYERS) for i in...  5.71 us
    ppermute x1, starting transfers between devices, shards(): swapped = lax.ppermute(share(each), 'dp', [(0, 1), (1, 0)])  4.18 us
    pallas_call x1, Pallas kernels, project(): pl.pallas_call(project_body, in_specs=[HBM, HBM, VMEM, VMEM], out_specs=V...  2.59 us
    pallas_call x1, Pallas kernels, gradients(): pl.pallas_call(gradient_body, in_specs=[VMEM] * 7, out_specs=[VMEM] * 2,...  2.41 us
  transfers between devices with their start and end apart: 4, of which 0 were waited for; matrix products, arithmetic and copies ran while one was open for 0% of the time, Pallas kernels for 4%

profile of v7, /device:TPU:1, one launch (start us, length us, event | category | flops | bytes accessed | tf_op | source)
XLA Modules:
  0.0 62.9 jit_solution(13388995462250465128)
XLA Ops:
  0.6 1.0 %bitcast_select_fusion = (bf16[64,768]{1,0:T(8,128)(2,1)S(1)}, bf16[64,768]{1,0:T(8,128)(2,1)S(1)}, bf16[64,768]{1,0:T(8,128)(2,1)S(1)}, bf16[64,768]{1,0:T(8,128)(2,1)S(1)}) fusion(bf16[1,768,64]{1,2,0:T(8,128)(2,1)} %param.10, bf16[1,64,768]{2,1,0:T(8,128)(2,1)} %param.11, pred[]{:T(512)S(6)} %lt.12, pred[]{:T(512)S(6)} %lt.10, pred[]{:T(512)S(6)} %lt.11), kind=kLoop, calls=%fused_computation | loop fusion | flops 196608 | bytes 589827 | tf_op jit(solution)/shard_map/jit(_where)/select_n | solution.py:306
  1.6 2.1 %collective-permute-start.2 = (bf16[64,768]{1,0:T(8,128)(2,1)S(1)}, bf16[64,768]{1,0:T(8,128)(2,1)S(1)}, u32[]{:S(2)}, u32[]{:S(2)}) collective-permute-start(bf16[64,768]{1,0:T(8,128)(2,1)S(1)} %get-tuple-element.16.to_one), channel_id=1, source_target_pairs={{0,32},{32,64},{64,96},{96,0},{1,33},{33,65},{65,97},{97,1},{2,34}... | collective-permute-start | bytes 294920 | tf_op jit(solution)/shard_map/ppermute | solution.py:308
  3.7 2.5 %collective-permute-start.1 = (bf16[64,768]{1,0:T(8,128)(2,1)S(1)}, bf16[64,768]{1,0:T(8,128)(2,1)S(1)}, u32[]{:S(2)}, u32[]{:S(2)}) collective-permute-start(bf16[64,768]{1,0:T(8,128)(2,1)S(1)} %get-tuple-element.18.to_two), channel_id=1, source_target_pairs={{0,64},{32,96},{64,0},{96,32},{1,65},{33,97},{65,1},{97,33},{2,66}... | collective-permute-start | bytes 294920 | tf_op jit(solution)/shard_map/ppermute | solution.py:308
  6.2 1.2 %collective-permute-start = (bf16[64,768]{1,0:T(8,128)(2,1)S(1)}, bf16[64,768]{1,0:T(8,128)(2,1)S(1)}, u32[]{:S(2)}, u32[]{:S(2)}) collective-permute-start(bf16[64,768]{1,0:T(8,128)(2,1)S(1)} %get-tuple-element.19.sent.to_three), channel_id=1, source_target_pairs={{0,96},{32,0},{64,32},{96,64},{1,97},{33,1},{65,33},{97,65},{2,98}... | collective-permute-start | bytes 294920 | tf_op jit(solution)/shard_map/ppermute | solution.py:308
  8.0 0.0 copy-start.2
  8.0 2.6 %shard_map.77.partial = bf16[16,48,128]{2,1,0:T(8,128)(2,1)S(1)} custom-call(bf16[2,384,768]{2,1,0:T(8,128)(2,1)} %act.1, bf16[2,384,768]{2,1,0:T(8,128)(2,1)} %cot.1, bf16[64,768]{1,0:T(8,128)(2,1)S(1)} %get-tuple-element.19.sent.to_three, bf16[64,768]{1,0:T(8,128)(2,1)S(1)} %get-tuple-element.17.kept), custom_call_target="tpu_custom_call" | custom-call | flops 150000000 | bytes 2800000 | tf_op jit(solution)/shard_map/pallas_call | solution.py:72
  10.6 0.0 collective-permute-done.2.one
  10.6 0.0 collective-permute-done.1.two
  10.6 0.0 collective-permute-done.three
  10.6 0.0 copy-done.2
  10.6 0.2 shard_map.78
  10.9 14.9 %all_to_all.21.parts = bf16[16,56,128]{2,1,0:T(8,128)(2,1)S(1)} all-to-all(bf16[16,56,128]{2,1,0:T(8,128)(2,1)S(1)} %get-tuple-element.11), channel_id=1, replica_groups=mesh['segment'=4,'tensor'=16,'dp'=2] {'tensor'}, dimensions={0} | all-to-all | bytes 458752 | tf_op jit(solution)/shard_map/all_to_all | solution.py:317
  25.8 0.0 copy-start.1
  25.8 0.1 shard_map.79
  25.9 0.0 copy-start
  25.9 19.7 %all_to_all.22.gathered = bf16[64,56,128]{2,1,0:T(8,128)(2,1)S(1)} all-to-all(bf16[64,56,128]{2,1,0:T(8,128)(2,1)S(1)} %shard_map.79), channel_id=1, replica_groups=mesh['segment'=4,'tensor'=16,'dp'=2] {'segment','tensor'}, dimensions={0} | all-to-all | bytes 1835008 | tf_op jit(solution)/shard_map/all_to_all | solution.py:319
  45.7 0.0 copy-done.1
  45.7 0.0 copy-done
  45.7 2.4 %shard_map.80 = (f32[256,768]{1,0:T(8,128)S(1)}, f32[32,128]{1,0:T(8,128)S(1)}) custom-call(s32[8,128]{1,0:T(8,128)S(1)} %get-tuple-element.10.limits, bf16[64,56,128]{2,1,0:T(8,128)(2,1)S(1)} %all_to_all.22.gathered, bf16[64,768]{1,0:T(8,128)(2,1)S(1)} %collective-permute-done.2.one, bf16[64,768]{1,0:T(8,128)(2,1)S(1)} %collective-permute-done.1.two, ...), custom_call_target="tpu_custom_call" | custom-call | flops 600000000 | bytes 5000000 | tf_op jit(solution)/shard_map/pallas_call | solution.py:223
  48.1 4.2 %collective-permute-start.3 = (bf16[256,384]{1,0:T(8,128)(2,1)S(1)}, bf16[256,384]{1,0:T(8,128)(2,1)S(1)}, u32[]{:S(2)}, u32[]{:S(2)}) collective-permute-start(bf16[256,384]{1,0:T(8,128)(2,1)S(1)} %shard_map.81), channel_id=1, source_target_pairs={{0,1},{1,0},{2,3},{3,2},{4,5},{5,4},{6,7},{7,6},{8,9},{9,8},{10,11... | collective-permute-start | bytes 589832 | tf_op jit(solution)/shard_map/ppermute | solution.py:321
  52.3 9.8 %all_to_all.23 = f32[32,1,128]{2,1,0:T(1,128)S(1)} all-to-all(f32[32,1,128]{2,1,0:T(1,128)S(1)} %bitcast.21), channel_id=1, replica_groups=mesh['segment'=4,'tensor'=16,'dp'=2] {'tensor','dp'}, dimensions={0} | all-to-all | bytes 32768 | tf_op jit(solution)/shard_map/all_to_all | solution.py:322
  62.1 0.0 collective-permute-done.3.swapped
  62.1 0.8 %shard_map.82 = (f32[1,64,384]{2,1,0:T(8,128)}, f32[1,64,384]{2,1,0:T(8,128)}) custom-call(f32[8,128]{1,0:T(8,128)S(1)} %get-tuple-element.9.bounds, f32[32,128]{1,0:T(8,128)S(1)} %bitcast.20, f32[256,768]{1,0:T(8,128)S(1)} %get-tuple-element.13.each, bf16[256,384]{1,0:T(8,128)(2,1)S(1)} %collective-permute-done.3.swapped), custom_call_target="tpu_custom_call" | custom-call | flops 300000 | bytes 900000 | tf_op jit(solution)/shard_map/pallas_call | solution.py:289
  (1 shorter events, 0.0 us)
Async XLA Ops:
  1.6 9.0 %collective-permute-start.2 = (bf16[64,768]{1,0:T(8,128)(2,1)S(1)}, bf16[64,768]{1,0:T(8,128)(2,1)S(1)}, u32[]{:S(2)}, u32[]{:S(2)}) collective-permute-start(bf16[64,768]{1,0:T(8,128)(2,1)S(1)} %get-tuple-element.16.to_one), channel_id=1, source_target_pairs={{0,32},{32,64},{64,96},{96,0},{1,33},{33,65},{65,97},{97,1},{2,34}... | collective-permute-start | bytes 294920 | tf_op jit(solution)/shard_map/ppermute | solution.py:308
  3.7 6.9 %collective-permute-start.1 = (bf16[64,768]{1,0:T(8,128)(2,1)S(1)}, bf16[64,768]{1,0:T(8,128)(2,1)S(1)}, u32[]{:S(2)}, u32[]{:S(2)}) collective-permute-start(bf16[64,768]{1,0:T(8,128)(2,1)S(1)} %get-tuple-element.18.to_two), channel_id=1, source_target_pairs={{0,64},{32,96},{64,0},{96,32},{1,65},{33,97},{65,1},{97,33},{2,66}... | collective-permute-start | bytes 294920 | tf_op jit(solution)/shard_map/ppermute | solution.py:308
  6.2 4.4 %collective-permute-start = (bf16[64,768]{1,0:T(8,128)(2,1)S(1)}, bf16[64,768]{1,0:T(8,128)(2,1)S(1)}, u32[]{:S(2)}, u32[]{:S(2)}) collective-permute-start(bf16[64,768]{1,0:T(8,128)(2,1)S(1)} %get-tuple-element.19.sent.to_three), channel_id=1, source_target_pairs={{0,96},{32,0},{64,32},{96,64},{1,97},{33,1},{65,33},{97,65},{2,98}... | collective-permute-start | bytes 294920 | tf_op jit(solution)/shard_map/ppermute | solution.py:308
  8.0 2.6 %copy-start.2 = (s32[2]{0:T(128)S(1)}, s32[2]{0:T(128)}, u32[]{:S(2)}) copy-start(s32[2]{0:T(128)} %param.8) | copy-start | bytes 28
  25.8 19.8 %copy-start.1 = (bf16[2,384,768]{2,1,0:T(8,128)(2,1)S(1)}, bf16[2,384,768]{2,1,0:T(8,128)(2,1)}, u32[]{:S(2)}) copy-start(bf16[2,384,768]{2,1,0:T(8,128)(2,1)} %cot.1) | copy-start | bytes 3538948
  25.9 19.8 %copy-start = (bf16[2,384,768]{2,1,0:T(8,128)(2,1)S(1)}, bf16[2,384,768]{2,1,0:T(8,128)(2,1)}, u32[]{:S(2)}) copy-start(bf16[2,384,768]{2,1,0:T(8,128)(2,1)} %act.1) | copy-start | bytes 3538948
  48.1 14.0 %collective-permute-start.3 = (bf16[256,384]{1,0:T(8,128)(2,1)S(1)}, bf16[256,384]{1,0:T(8,128)(2,1)S(1)}, u32[]{:S(2)}, u32[]{:S(2)}) collective-permute-start(bf16[256,384]{1,0:T(8,128)(2,1)S(1)} %shard_map.81), channel_id=1, source_target_pairs={{0,1},{1,0},{2,3},{3,2},{4,5},{5,4},{6,7},{7,6},{8,9},{9,8},{10,11... | collective-permute-start | bytes 589832 | tf_op jit(solution)/shard_map/ppermute | solution.py:321

commit v8 on v7

--- a/solution.py
+++ b/solution.py
@@ -38,7 +38,7 @@
     return values * half, slope
 
 
-STEPS = 2
+STEPS = 1
 STEP_ROWS = SLOTS // STEPS
 
 
@@ -85,22 +85,24 @@
 
 
 def weave_body(
-    lengths, clip, partial, to_three, to_two, to_one, three, two, one, out, limits, bounds
+    lengths, clip, partial, to_three, to_two, one, two, out, limits, bounds
 ):
     lane = lax.broadcasted_iota(jnp.int32, (8, LANES), 1)
     limits[...] = jnp.where(lane < RANK, lengths[:, :1], lengths[:, 1:])
     bounds[...] = jnp.broadcast_to(clip[...], (8, LANES))
     seg = lax.axis_index("segment")
-    for k, own, other in ((1, to_three, one), (2, to_two, two), (3, to_one, three)):
-        lower = seg >= k
-        left = jnp.where(lower, other[HALF:], own[:HALF])
-        right = jnp.where(lower, own[...], other[...])
-        gram = dot(left, right, 1, 1)
-        gram = jnp.concatenate([gram, jnp.zeros_like(gram)], axis=1)
-        for q in range(4):
-            t = (k - 1) * 4 + q
-            tile = gram[q * 8 : (q + 1) * 8]
-            out[t] = jnp.concatenate([partial[t].astype(F32), tile], axis=0).astype(BF)
+    lower = seg >= 1
+    left = jnp.where(lower, one[...], to_three[...])
+    right = jnp.where(lower, to_three[...], one[...])
+    near = dot(left, right, 1, 1)
+    lower = seg >= 2
+    left = jnp.where(lower, two[HALF:], to_two[:HALF])
+    right = jnp.where(lower, to_two[...], two[...])
+    gram = jnp.concatenate([near, dot(left, right, 1, 1)], axis=0)
+    gram = jnp.concatenate([gram, jnp.zeros_like(gram)], axis=1)
+    for t in range(12):
+        tile = gram[t * 8 : (t + 1) * 8]
+        out[t] = jnp.concatenate([partial[t].astype(F32), tile], axis=0).astype(BF)
     for t in range(12, CUTS):
         out[t] = jnp.concatenate(
             [partial[t].astype(F32), jnp.zeros((EXTRA, LANES), F32)], axis=0
@@ -110,7 +112,7 @@
 def weave(lengths, clip, partial, messages, peers):
     return pl.pallas_call(
         weave_body,
-        in_specs=[VMEM] * 9,
+        in_specs=[VMEM] * 7,
         out_specs=[VMEM] * 3,
         out_shape=[
             jax.ShapeDtypeStruct((CUTS, 2 * PIECE + EXTRA, LANES), BF),
@@ -119,10 +121,10 @@
         ],
         compiler_params=pltpu.CompilerParams(vmem_limit_bytes=16 << 20),
         cost_estimate=pl.CostEstimate(flops=10000000, bytes_accessed=1000000, transcendentals=0),
-    )(lengths, clip, partial, messages[2], messages[1], messages[0], peers[2], peers[1], peers[0])
-
-
-def reduce_body(limits, parts, out):
+    )(lengths, clip, partial, messages[2], messages[1], peers[0], peers[1])
+
+
+def reduce_body(limits, parts, far, out):
     base = lax.axis_index("tensor") * PIECE
     total = parts[0].astype(F32)
     for i in range(1, CUTS):
@@ -135,20 +137,20 @@
         out[i] = message
 
 
-def reduce_parts(limits, parts):
+def reduce_parts(limits, parts, far):
     return pl.pallas_call(
         reduce_body,
-        in_specs=[VMEM] * 2,
+        in_specs=[VMEM] * 3,
         out_specs=VMEM,
         out_shape=jax.ShapeDtypeStruct((LAYERS * CUTS, 2 * PIECE + EXTRA, LANES), BF),
         compiler_params=pltpu.CompilerParams(vmem_limit_bytes=16 << 20),
         cost_estimate=pl.CostEstimate(flops=200000, bytes_accessed=1300000, transcendentals=0),
-    )(limits, parts)
+    )(limits, parts, far)
 
 
 def gradient_body(
     limits, gathered, one, two, three, act, cot,
-    each, note,
+    each, note, theirs,
     first, last, hidden, slopes, steep,
 ):
     seg = lax.axis_index("segment")
@@ -164,10 +166,10 @@
         packed.append(jnp.concatenate(tiles, axis=0))
 
     def gram_of(i, j):
-        a, b = (i - j) % LAYERS - 1, (j - i) % LAYERS - 1
-        gram = jnp.concatenate(
-            [packed[i][a * HALF : (a + 1) * HALF], packed[j][b * HALF : (b + 1) * HALF]], axis=0
-        )
+        if j - i == 2:
+            gram = jnp.concatenate([packed[i][RANK:], packed[j][RANK:]], axis=0)
+        else:
+            gram = packed[(i + 1 if j - i == 1 else 0)][:RANK]
         zero = jnp.zeros_like(gram)
         return jnp.concatenate(
             [jnp.concatenate([gram, zero], axis=1), jnp.concatenate([zero, gram], axis=1)], axis=0
@@ -206,16 +208,18 @@
         )
     left = jnp.concatenate(lefts, axis=1).astype(BF)
     peers = jnp.concatenate([one[...], two[...], three[...]], axis=0)
-    each[...] = dot(left, peers, 1, 0)
+    extra = dot(left, peers, 1, 0)
+    give = pl.multiple_of((1 - lax.axis_index("dp")) * LOCAL, 128)
     for e in range(2):
         rows = slice(e * RANK, (e + 1) * RANK)
         other = slice((2 + e) * RANK, (3 + e) * RANK)
-        down_grad = each[rows] + dot(mine_s[rows], act[e], 1, 0)
-        up_grad = each[other] + dot(mine_h[rows], cot[e], 1, 0)
+        down_grad = extra[rows] + dot(mine_s[rows], act[e], 1, 0)
+        up_grad = extra[other] + dot(mine_h[rows], cot[e], 1, 0)
         each[rows] = down_grad
         each[other] = up_grad
         square = jnp.sum(down_grad * down_grad + up_grad * up_grad)
         note[:, rows] = jnp.full((2 * CUTS, RANK), square, F32)
+    theirs[...] = each[:, pl.ds(give, LOCAL)].astype(BF)
 
 
 def gradients(limits, gathered, peers, act, cot):
@@ -223,10 +227,11 @@
     return pl.pallas_call(
         gradient_body,
         in_specs=[VMEM] * 7,
-        out_specs=[VMEM] * 2,
+        out_specs=[VMEM] * 3,
         out_shape=[
             jax.ShapeDtypeStruct((4 * RANK, WIDTH), F32),
             jax.ShapeDtypeStruct((2 * CUTS, LANES), F32),
+            jax.ShapeDtypeStruct((4 * RANK, LOCAL), BF),
         ],
         scratch_shapes=[
             pltpu.VMEM(wide, F32),
@@ -240,22 +245,6 @@
             flops=600000000, bytes_accessed=5000000, transcendentals=200000
         ),
     )(limits, gathered, peers[0], peers[1], peers[2], act, cot)
-
-
-def share_body(each, theirs):
-    give = pl.multiple_of((1 - lax.axis_index("dp")) * LOCAL, 128)
-    theirs[...] = each[:, pl.ds(give, LOCAL)].astype(BF)
-
-
-def share(each):
-    return pl.pallas_call(
-        share_body,
-        in_specs=[VMEM],
-        out_specs=VMEM,
-        out_shape=jax.ShapeDtypeStruct((4 * RANK, LOCAL), BF),
-        compiler_params=pltpu.CompilerParams(vmem_limit_bytes=16 << 20),
-        cost_estimate=pl.CostEstimate(flops=100000, bytes_accessed=1000000, transcendentals=0),
-    )(each)
 
 
 def scale_body(bounds, notes, each, swapped, out_down, out_up):
@@ -315,10 +304,10 @@
         lengths.reshape(1, 2), clip_scale.reshape(1, 1), partial, messages, peers
     )
     parts = lax.all_to_all(woven, "tensor", 0, 0, tiled=True)
-    message = reduce_parts(limits, parts)
+    message = reduce_parts(limits, parts, peers[2])
     gathered = lax.all_to_all(message, ("segment", "tensor"), 0, 0, tiled=True)
-    each, note = gradients(limits, gathered, peers, act_input, cotangent)
-    swapped = lax.ppermute(share(each), "dp", [(0, 1), (1, 0)])
+    each, note, theirs = gradients(limits, gathered, peers, act_input, cotangent)
+    swapped = lax.ppermute(theirs, "dp", [(0, 1), (1, 0)])
     notes = lax.all_to_all(note, ("tensor", "dp"), 0, 0, tiled=True)
     grad_down, grad_up = scaled(bounds, notes, each, swapped)
     return jnp.swapaxes(grad_down, 1, 2), grad_up

time: 63.2 us -> 62.8 us (level)
  blocking collectives: 44.5 us -> 27.8 us
  waiting for transfers between devices: 0.01 us -> 8.11 us
  starting transfers between devices: 9.89 us -> 17.7 us
    all_to_all x1 -> x0, blocking collectives: 14.9 us -> none  [shards(): parts = lax.all_to_all(woven, 'tensor', 0, 0, tiled=True)]
    all_to_all x0 -> x1, starting transfers between devices: none -> 7.77 us  [shards(): parts = lax.all_to_all(woven, 'tensor', 0, 0, tiled=True)]
    ppermute x3, waiting for transfers between devices: 0.01 us -> 4.28 us  [shards(): lax.ppermute(messages[k - 1], 'segment', [(i, (i + k) % LAYERS) for i in...]
    all_to_all x0 -> x1, waiting for transfers between devices: none -> 3.83 us  [shards(): parts = lax.all_to_all(woven, 'tensor', 0, 0, tiled=True)]
    all_to_all x1, blocking collectives: 19.7 us -> 18 us  [shards(): gathered = lax.all_to_all(message, ('segment', 'tensor'), 0, 0, tiled=True)]
    ppermute x1, starting transfers between devices: 4.18 us -> 5.13 us  [shards(): swapped = lax.ppermute(theirs, 'dp', [(0, 1), (1, 0)])]
    ppermute x3, starting transfers between devices: 5.71 us -> 4.81 us  [shards(): lax.ppermute(messages[k - 1], 'segment', [(i, (i + k) % LAYERS) for i in...]
    pallas_call x4 -> x3, Pallas kernels: 2.75 us -> 3.41 us  [the longest x1 2.43 us: gradients(): pl.pallas_call(gradient_body, in_specs=[VMEM] * 7, out_specs=[VMEM] * 3,...]
  transfers between devices with their start and end apart: 4 -> 5, of which waited for: 0 -> 3; matrix products, arithmetic and copies ran while one was open for 0% -> 0% of each run, Pallas kernels for 4% -> 4%
where the time goes in v8:
time: 62.8 us; the launch traced here: 62.5 us
  blocking collectives  27.8 us (44%)
  starting transfers between devices  17.7 us (28%)
  waiting for transfers between devices  8.11 us (13%)
  Pallas kernels  6.58 us (10%)
  between operations  1.35 us (2%)
  other arithmetic  0.97 us (2%)
    all_to_all x1, blocking collectives, shards(): gathered = lax.all_to_all(message, ('segment', 'tensor'), 0, 0, tiled=True)  18 us
    all_to_all x1, blocking collectives, shards(): notes = lax.all_to_all(note, ('tensor', 'dp'), 0, 0, tiled=True)  9.79 us
    all_to_all x1, starting transfers between devices, shards(): parts = lax.all_to_all(woven, 'tensor', 0, 0, tiled=True)  7.77 us
    ppermute x1, starting transfers between devices, shards(): swapped = lax.ppermute(theirs, 'dp', [(0, 1), (1, 0)])  5.13 us
    ppermute x3, starting transfers between devices, shards(): lax.ppermute(messages[k - 1], 'segment', [(i, (i + k) % LAYERS) for i in...  4.81 us
    ppermute x3, waiting for transfers between devices, shards(): lax.ppermute(messages[k - 1], 'segment', [(i, (i + k) % LAYERS) for i in...  4.28 us
    all_to_all x1, waiting for transfers between devices, shards(): parts = lax.all_to_all(woven, 'tensor', 0, 0, tiled=True)  3.83 us
    pallas_call x1, Pallas kernels, gradients(): pl.pallas_call(gradient_body, in_specs=[VMEM] * 7, out_specs=[VMEM] * 3,...  2.43 us
  transfers between devices with their start and end apart: 5, of which 3 were waited for; matrix products, arithmetic and copies ran while one was open for 0% of the time, Pallas kernels for 4%

profile of v8, /device:TPU:1, one launch (start us, length us, event | category | flops | bytes accessed | tf_op | source)
XLA Modules:
  0.0 62.5 jit_solution(251380152034806890)
XLA Ops:
  0.6 1.0 %bitcast_select_fusion = (bf16[64,768]{1,0:T(8,128)(2,1)S(1)}, bf16[64,768]{1,0:T(8,128)(2,1)S(1)}, bf16[64,768]{1,0:T(8,128)(2,1)S(1)}, bf16[64,768]{1,0:T(8,128)(2,1)S(1)}) fusion(bf16[1,768,64]{1,2,0:T(8,128)(2,1)} %param.10, bf16[1,64,768]{2,1,0:T(8,128)(2,1)} %param.11, pred[]{:T(512)S(6)} %lt.12, pred[]{:T(512)S(6)} %lt.10, pred[]{:T(512)S(6)} %lt.11), kind=kLoop, calls=%fused_computation | loop fusion | flops 196608 | bytes 589827 | tf_op jit(solution)/shard_map/jit(_where)/select_n | solution.py:295
  1.6 2.1 %collective-permute-start = (bf16[64,768]{1,0:T(8,128)(2,1)S(1)}, bf16[64,768]{1,0:T(8,128)(2,1)S(1)}, u32[]{:S(2)}, u32[]{:S(2)}) collective-permute-start(bf16[64,768]{1,0:T(8,128)(2,1)S(1)} %get-tuple-element.18), channel_id=1, source_target_pairs={{0,32},{32,64},{64,96},{96,0},{1,33},{33,65},{65,97},{97,1},{2,34}... | collective-permute-start | bytes 294920 | tf_op jit(solution)/shard_map/ppermute | solution.py:297
  3.7 2.5 %collective-permute-start.1 = (bf16[64,768]{1,0:T(8,128)(2,1)S(1)}, bf16[64,768]{1,0:T(8,128)(2,1)S(1)}, u32[]{:S(2)}, u32[]{:S(2)}) collective-permute-start(bf16[64,768]{1,0:T(8,128)(2,1)S(1)} %get-tuple-element.20.to_two), channel_id=1, source_target_pairs={{0,64},{32,96},{64,0},{96,32},{1,65},{33,97},{65,1},{97,33},{2,66}... | collective-permute-start | bytes 294920 | tf_op jit(solution)/shard_map/ppermute | solution.py:297
  6.8 0.0 copy-start.2
  6.8 2.3 %shard_map.77.partial = bf16[16,48,128]{2,1,0:T(8,128)(2,1)S(1)} custom-call(bf16[2,384,768]{2,1,0:T(8,128)(2,1)} %act.1, bf16[2,384,768]{2,1,0:T(8,128)(2,1)} %cot.1, bf16[64,768]{1,0:T(8,128)(2,1)S(1)} %get-tuple-element.21.sent.to_three, bf16[64,768]{1,0:T(8,128)(2,1)S(1)} %get-tuple-element.19.kept), custom_call_target="tpu_custom_call" | custom-call | flops 150000000 | bytes 2800000 | tf_op jit(solution)/shard_map/pallas_call | solution.py:72
  9.2 0.0 collective-permute-done.one
  9.2 1.0 %collective-permute-done.1.two = bf16[64,768]{1,0:T(8,128)(2,1)S(1)} collective-permute-done((bf16[64,768]{1,0:T(8,128)(2,1)S(1)}, bf16[64,768]{1,0:T(8,128)(2,1)S(1)}, u32[]{:S(2)}, u32[]{:S(2)}) %collective-permute-start.1) | collective-permute-done | bytes 98336 | tf_op jit(solution)/shard_map/ppermute | solution.py:297
  10.2 0.0 copy-done.2
  10.2 0.9 %shard_map.78 = (bf16[16,56,128]{2,1,0:T(8,128)(2,1)}, s32[8,128]{1,0:T(8,128)S(1)}, f32[8,128]{1,0:T(8,128)S(1)}) custom-call(s32[1,2]{1,0:T(1,128)S(1)} %bitcast.22, f32[1,1]{1,0:T(1,128)} %bitcast.19.clip, bf16[16,48,128]{2,1,0:T(8,128)(2,1)S(1)} %shard_map.77.partial, bf16[64,768]{1,0:T(8,128)(2,1)S(1)} %get-tuple-element.21.sent.to_three, ...), custom_call_target="tpu_custom_call" | custom-call | flops 10000000 | bytes 1000000 | tf_op jit(solution)/shard_map/pallas_call | solution.py:113
  11.1 7.8 %all-to-all-start = ((bf16[16,56,128]{2,1,0:T(8,128)(2,1)}), bf16[16,56,128]{2,1,0:T(8,128)(2,1)S(1)}, u32[]{:S(2)}, u32[]{:S(2)}) async-start(bf16[16,56,128]{2,1,0:T(8,128)(2,1)} %get-tuple-element.12), calls=%async_computation | async-start | bytes 458752 | tf_op jit(solution)/shard_map/all_to_all | solution.py:306
  18.9 0.3 collective-permute-start.2
  19.1 3.3 %collective-permute-done.2.far.three = bf16[64,768]{1,0:T(8,128)(2,1)S(1)} collective-permute-done((bf16[64,768]{1,0:T(8,128)(2,1)S(1)}, bf16[64,768]{1,0:T(8,128)(2,1)S(1)}, u32[]{:S(2)}, u32[]{:S(2)}) %collective-permute-start.2) | collective-permute-done | bytes 98336 | tf_op jit(solution)/shard_map/ppermute | solution.py:297
  22.4 3.8 %all-to-all-done.parts = bf16[16,56,128]{2,1,0:T(8,128)(2,1)S(1)} async-done(((bf16[16,56,128]{2,1,0:T(8,128)(2,1)}), bf16[16,56,128]{2,1,0:T(8,128)(2,1)S(1)}, u32[]{:S(2)}, u32[]{:S(2)}) %all-to-all-start) | async-done | bytes 229408 | tf_op jit(solution)/shard_map/all_to_all | solution.py:306
  26.2 0.0 copy-start.1
  26.2 0.1 shard_map.79
  26.3 0.0 copy-start
  26.3 18.0 %all_to_all.21.gathered = bf16[64,56,128]{2,1,0:T(8,128)(2,1)S(1)} all-to-all(bf16[64,56,128]{2,1,0:T(8,128)(2,1)S(1)} %shard_map.79), channel_id=1, replica_groups=mesh['segment'=4,'tensor'=16,'dp'=2] {'segment','tensor'}, dimensions={0} | all-to-all | bytes 1835008 | tf_op jit(solution)/shard_map/all_to_all | solution.py:308
  44.3 0.0 copy-done.1
  44.3 0.0 copy-done
  44.3 2.4 %shard_map.80 = (f32[256,768]{1,0:T(8,128)S(1)}, f32[32,128]{1,0:T(8,128)S(1)}, bf16[256,384]{1,0:T(8,128)(2,1)S(1)}) custom-call(s32[8,128]{1,0:T(8,128)S(1)} %get-tuple-element.11.limits, bf16[64,56,128]{2,1,0:T(8,128)(2,1)S(1)} %all_to_all.21.gathered, bf16[64,768]{1,0:T(8,128)(2,1)S(1)} %collective-permute-done.one, ...), custom_call_target="tpu_custom_call" | custom-call | flops 600000000 | bytes 5000000 | tf_op jit(solution)/shard_map/pallas_call | solution.py:227
  46.7 5.1 %collective-permute-start.3 = (bf16[256,384]{1,0:T(8,128)(2,1)S(1)}, bf16[256,384]{1,0:T(8,128)(2,1)S(1)}, u32[]{:S(2)}, u32[]{:S(2)}) collective-permute-start(bf16[256,384]{1,0:T(8,128)(2,1)S(1)} %get-tuple-element.15), channel_id=1, source_target_pairs={{0,1},{1,0},{2,3},{3,2},{4,5},{5,4},{6,7},{7,6},{8,9},{9,8},{10,11... | collective-permute-start | bytes 589832 | tf_op jit(solution)/shard_map/ppermute | solution.py:310
  51.9 9.8 %all_to_all.22 = f32[32,1,128]{2,1,0:T(1,128)S(1)} all-to-all(f32[32,1,128]{2,1,0:T(1,128)S(1)} %bitcast.21), channel_id=1, replica_groups=mesh['segment'=4,'tensor'=16,'dp'=2] {'tensor','dp'}, dimensions={0} | all-to-all | bytes 32768 | tf_op jit(solution)/shard_map/all_to_all | solution.py:311
  61.7 0.0 collective-permute-done.3.swapped
  61.7 0.8 %shard_map.81 = (f32[1,64,384]{2,1,0:T(8,128)}, f32[1,64,384]{2,1,0:T(8,128)}) custom-call(f32[8,128]{1,0:T(8,128)S(1)} %get-tuple-element.10.bounds, f32[32,128]{1,0:T(8,128)S(1)} %bitcast.20, f32[256,768]{1,0:T(8,128)S(1)} %get-tuple-element.14.each, bf16[256,384]{1,0:T(8,128)(2,1)S(1)} %collective-permute-done.3.swapped), custom_call_target="tpu_custom_call" | custom-call | flops 300000 | bytes 900000 | tf_op jit(solution)/shard_map/pallas_call | solution.py:278
Async XLA Ops:
  1.6 7.6 %collective-permute-start = (bf16[64,768]{1,0:T(8,128)(2,1)S(1)}, bf16[64,768]{1,0:T(8,128)(2,1)S(1)}, u32[]{:S(2)}, u32[]{:S(2)}) collective-permute-start(bf16[64,768]{1,0:T(8,128)(2,1)S(1)} %get-tuple-element.18), channel_id=1, source_target_pairs={{0,32},{32,64},{64,96},{96,0},{1,33},{33,65},{65,97},{97,1},{2,34}... | collective-permute-start | bytes 294920 | tf_op jit(solution)/shard_map/ppermute | solution.py:297
  3.7 6.5 %collective-permute-start.1 = (bf16[64,768]{1,0:T(8,128)(2,1)S(1)}, bf16[64,768]{1,0:T(8,128)(2,1)S(1)}, u32[]{:S(2)}, u32[]{:S(2)}) collective-permute-start(bf16[64,768]{1,0:T(8,128)(2,1)S(1)} %get-tuple-element.20.to_two), channel_id=1, source_target_pairs={{0,64},{32,96},{64,0},{96,32},{1,65},{33,97},{65,1},{97,33},{2,66}... | collective-permute-start | bytes 294920 | tf_op jit(solution)/shard_map/ppermute | solution.py:297
  6.8 3.4 %copy-start.2 = (s32[2]{0:T(128)S(1)}, s32[2]{0:T(128)}, u32[]{:S(2)}) copy-start(s32[2]{0:T(128)} %param.8) | copy-start | bytes 28
  11.1 15.1 %all-to-all-start = ((bf16[16,56,128]{2,1,0:T(8,128)(2,1)}), bf16[16,56,128]{2,1,0:T(8,128)(2,1)S(1)}, u32[]{:S(2)}, u32[]{:S(2)}) async-start(bf16[16,56,128]{2,1,0:T(8,128)(2,1)} %get-tuple-element.12), calls=%async_computation | async-start | bytes 458752 | tf_op jit(solution)/shard_map/all_to_all | solution.py:306
  18.9 3.5 %collective-permute-start.2 = (bf16[64,768]{1,0:T(8,128)(2,1)S(1)}, bf16[64,768]{1,0:T(8,128)(2,1)S(1)}, u32[]{:S(2)}, u32[]{:S(2)}) collective-permute-start(bf16[64,768]{1,0:T(8,128)(2,1)S(1)} %get-tuple-element.21.sent.to_three), channel_id=1, source_target_pairs={{0,96},{32,0},{64,32},{96,64},{1,97},{33,1},{65,33},{97,65},{2,98}... | collective-permute-start | bytes 294920 | tf_op jit(solution)/shard_map/ppermute | solution.py:297
  26.2 18.1 %copy-start.1 = (bf16[2,384,768]{2,1,0:T(8,128)(2,1)S(1)}, bf16[2,384,768]{2,1,0:T(8,128)(2,1)}, u32[]{:S(2)}) copy-start(bf16[2,384,768]{2,1,0:T(8,128)(2,1)} %cot.1) | copy-start | bytes 3538948
  26.3 18.0 %copy-start = (bf16[2,384,768]{2,1,0:T(8,128)(2,1)S(1)}, bf16[2,384,768]{2,1,0:T(8,128)(2,1)}, u32[]{:S(2)}) copy-start(bf16[2,384,768]{2,1,0:T(8,128)(2,1)} %act.1) | copy-start | bytes 3538948
  46.7 14.9 %collective-permute-start.3 = (bf16[256,384]{1,0:T(8,128)(2,1)S(1)}, bf16[256,384]{1,0:T(8,128)(2,1)S(1)}, u32[]{:S(2)}, u32[]{:S(2)}) collective-permute-start(bf16[256,384]{1,0:T(8,128)(2,1)S(1)} %get-tuple-element.15), channel_id=1, source_target_pairs={{0,1},{1,0},{2,3},{3,2},{4,5},{5,4},{6,7},{7,6},{8,9},{9,8},{10,11... | collective-permute-start | bytes 589832 | tf_op jit(solution)/shard_map/ppermute | solution.py:310

commit v9 on v8

--- a/solution.py
+++ b/solution.py
@@ -85,7 +85,8 @@
 
 
 def weave_body(
-    lengths, clip, partial, to_three, to_two, one, two, out, limits, bounds
+    lengths, clip, partial, to_two, to_three, one, two, out, limits, bounds,
+    woven, sems,
 ):
     lane = lax.broadcasted_iota(jnp.int32, (8, LANES), 1)
     limits[...] = jnp.where(lane < RANK, lengths[:, :1], lengths[:, 1:])
@@ -98,30 +99,49 @@
     lower = seg >= 2
     left = jnp.where(lower, two[HALF:], to_two[:HALF])
     right = jnp.where(lower, to_two[...], two[...])
-    gram = jnp.concatenate([near, dot(left, right, 1, 1)], axis=0)
-    gram = jnp.concatenate([gram, jnp.zeros_like(gram)], axis=1)
-    for t in range(12):
-        tile = gram[t * 8 : (t + 1) * 8]
-        out[t] = jnp.concatenate([partial[t].astype(F32), tile], axis=0).astype(BF)
-    for t in range(12, CUTS):
-        out[t] = jnp.concatenate(
-            [partial[t].astype(F32), jnp.zeros((EXTRA, LANES), F32)], axis=0
-        ).astype(BF)
+    stores = []
+
+    def store(first, last):
+        block = pl.ds(first, last - first)
+        copy = pltpu.make_async_copy(woven.at[block], out.at[block], sems.at[len(stores)])
+        copy.start()
+        stores.append(copy)
+
+    def fill(first, tiles):
+        for i in range(tiles.shape[0] // 8):
+            tile = tiles[i * 8 : (i + 1) * 8]
+            tile = jnp.concatenate([tile, jnp.zeros_like(tile)], axis=1)
+            woven[first + i] = jnp.concatenate(
+                [partial[first + i].astype(F32), tile], axis=0
+            ).astype(BF)
+
+    fill(12, jnp.zeros((32, RANK), F32))
+    store(12, CUTS)
+    fill(0, near)
+    store(0, 8)
+    fill(8, dot(left, right, 1, 1))
+    store(8, 12)
+    for copy in stores:
+        copy.wait()
 
 
 def weave(lengths, clip, partial, messages, peers):
     return pl.pallas_call(
         weave_body,
         in_specs=[VMEM] * 7,
-        out_specs=[VMEM] * 3,
+        out_specs=[HBM] + [VMEM] * 2,
         out_shape=[
             jax.ShapeDtypeStruct((CUTS, 2 * PIECE + EXTRA, LANES), BF),
             jax.ShapeDtypeStruct((8, LANES), jnp.int32),
             jax.ShapeDtypeStruct((8, LANES), F32),
         ],
+        scratch_shapes=[
+            pltpu.VMEM((CUTS, 2 * PIECE + EXTRA, LANES), BF),
+            pltpu.SemaphoreType.DMA((3,)),
+        ],
         compiler_params=pltpu.CompilerParams(vmem_limit_bytes=16 << 20),
         cost_estimate=pl.CostEstimate(flops=10000000, bytes_accessed=1000000, transcendentals=0),
-    )(lengths, clip, partial, messages[2], messages[1], peers[0], peers[1])
+    )(lengths, clip, partial, messages[1], messages[2], peers[0], peers[1])
 
 
 def reduce_body(limits, parts, far, out):

time: 62.8 us -> 62.9 us (level)
  no operation moved by 1% of the time
where the time goes in v9:
time: 62.9 us; the launch traced here: 62.5 us
  blocking collectives  27.8 us (44%)
  starting transfers between devices  17.7 us (28%)
  waiting for transfers between devices  8.11 us (13%)
  Pallas kernels  6.57 us (10%)
  between operations  1.36 us (2%)
  other arithmetic  0.97 us (2%)
    all_to_all x1, blocking collectives, shards(): gathered = lax.all_to_all(message, ('segment', 'tensor'), 0, 0, tiled=True)  18 us
    all_to_all x1, blocking collectives, shards(): notes = lax.all_to_all(note, ('tensor', 'dp'), 0, 0, tiled=True)  9.8 us
    all_to_all x1, starting transfers between devices, shards(): parts = lax.all_to_all(woven, 'tensor', 0, 0, tiled=True)  7.78 us
    ppermute x1, starting transfers between devices, shards(): swapped = lax.ppermute(theirs, 'dp', [(0, 1), (1, 0)])  5.13 us
    ppermute x3, starting transfers between devices, shards(): lax.ppermute(messages[k - 1], 'segment', [(i, (i + k) % LAYERS) for i in...  4.81 us
    ppermute x3, waiting for transfers between devices, shards(): lax.ppermute(messages[k - 1], 'segment', [(i, (i + k) % LAYERS) for i in...  4.28 us
    all_to_all x1, waiting for transfers between devices, shards(): parts = lax.all_to_all(woven, 'tensor', 0, 0, tiled=True)  3.83 us
    pallas_call x1, Pallas kernels, gradients(): pl.pallas_call(gradient_body, in_specs=[VMEM] * 7, out_specs=[VMEM] * 3,...  2.43 us
  transfers between devices with their start and end apart: 5, of which 3 were waited for; matrix products, arithmetic and copies ran while one was open for 0% of the time, Pallas kernels for 4%

profile of v9, /device:TPU:1, one launch (start us, length us, event | category | flops | bytes accessed | tf_op | source)
XLA Modules:
  0.0 62.5 jit_solution(11184200127108744733)
XLA Ops:
  0.6 1.0 %bitcast_select_fusion = (bf16[64,768]{1,0:T(8,128)(2,1)S(1)}, bf16[64,768]{1,0:T(8,128)(2,1)S(1)}, bf16[64,768]{1,0:T(8,128)(2,1)S(1)}, bf16[64,768]{1,0:T(8,128)(2,1)S(1)}) fusion(bf16[1,768,64]{1,2,0:T(8,128)(2,1)} %param.10, bf16[1,64,768]{2,1,0:T(8,128)(2,1)} %param.11, pred[]{:T(512)S(6)} %lt.12, pred[]{:T(512)S(6)} %lt.10, pred[]{:T(512)S(6)} %lt.11), kind=kLoop, calls=%fused_computation | loop fusion | flops 196608 | bytes 589827 | tf_op jit(solution)/shard_map/jit(_where)/select_n | solution.py:315
  1.6 2.1 %collective-permute-start = (bf16[64,768]{1,0:T(8,128)(2,1)S(1)}, bf16[64,768]{1,0:T(8,128)(2,1)S(1)}, u32[]{:S(2)}, u32[]{:S(2)}) collective-permute-start(bf16[64,768]{1,0:T(8,128)(2,1)S(1)} %get-tuple-element.18), channel_id=1, source_target_pairs={{0,32},{32,64},{64,96},{96,0},{1,33},{33,65},{65,97},{97,1},{2,34}... | collective-permute-start | bytes 294920 | tf_op jit(solution)/shard_map/ppermute | solution.py:317
  3.7 2.5 %collective-permute-start.1 = (bf16[64,768]{1,0:T(8,128)(2,1)S(1)}, bf16[64,768]{1,0:T(8,128)(2,1)S(1)}, u32[]{:S(2)}, u32[]{:S(2)}) collective-permute-start(bf16[64,768]{1,0:T(8,128)(2,1)S(1)} %get-tuple-element.20.to_two), channel_id=1, source_target_pairs={{0,64},{32,96},{64,0},{96,32},{1,65},{33,97},{65,1},{97,33},{2,66}... | collective-permute-start | bytes 294920 | tf_op jit(solution)/shard_map/ppermute | solution.py:317
  6.8 0.0 copy-start.2
  6.8 2.3 %shard_map.77.partial = bf16[16,48,128]{2,1,0:T(8,128)(2,1)S(1)} custom-call(bf16[2,384,768]{2,1,0:T(8,128)(2,1)} %act.1, bf16[2,384,768]{2,1,0:T(8,128)(2,1)} %cot.1, bf16[64,768]{1,0:T(8,128)(2,1)S(1)} %get-tuple-element.21.sent.to_three, bf16[64,768]{1,0:T(8,128)(2,1)S(1)} %get-tuple-element.19.kept), custom_call_target="tpu_custom_call" | custom-call | flops 150000000 | bytes 2800000 | tf_op jit(solution)/shard_map/pallas_call | solution.py:72
  9.2 0.0 collective-permute-done.one
  9.2 1.0 %collective-permute-done.1.two = bf16[64,768]{1,0:T(8,128)(2,1)S(1)} collective-permute-done((bf16[64,768]{1,0:T(8,128)(2,1)S(1)}, bf16[64,768]{1,0:T(8,128)(2,1)S(1)}, u32[]{:S(2)}, u32[]{:S(2)}) %collective-permute-start.1) | collective-permute-done | bytes 98336 | tf_op jit(solution)/shard_map/ppermute | solution.py:317
  10.2 0.0 copy-done.2
  10.2 0.9 %shard_map.78 = (bf16[16,56,128]{2,1,0:T(8,128)(2,1)}, s32[8,128]{1,0:T(8,128)S(1)}, f32[8,128]{1,0:T(8,128)S(1)}) custom-call(s32[1,2]{1,0:T(1,128)S(1)} %bitcast.22, f32[1,1]{1,0:T(1,128)} %bitcast.19.clip, bf16[16,48,128]{2,1,0:T(8,128)(2,1)S(1)} %shard_map.77.partial, bf16[64,768]{1,0:T(8,128)(2,1)S(1)} %get-tuple-element.20.to_two, ...), custom_call_target="tpu_custom_call" | custom-call | flops 10000000 | bytes 1000000 | tf_op jit(solution)/shard_map/pallas_call | solution.py:129
  11.1 7.8 %all-to-all-start = ((bf16[16,56,128]{2,1,0:T(8,128)(2,1)}), bf16[16,56,128]{2,1,0:T(8,128)(2,1)S(1)}, u32[]{:S(2)}, u32[]{:S(2)}) async-start(bf16[16,56,128]{2,1,0:T(8,128)(2,1)} %get-tuple-element.12), calls=%async_computation | async-start | bytes 458752 | tf_op jit(solution)/shard_map/all_to_all | solution.py:326
  18.9 0.3 collective-permute-start.2
  19.1 3.3 %collective-permute-done.2.far.three = bf16[64,768]{1,0:T(8,128)(2,1)S(1)} collective-permute-done((bf16[64,768]{1,0:T(8,128)(2,1)S(1)}, bf16[64,768]{1,0:T(8,128)(2,1)S(1)}, u32[]{:S(2)}, u32[]{:S(2)}) %collective-permute-start.2) | collective-permute-done | bytes 98336 | tf_op jit(solution)/shard_map/ppermute | solution.py:317
  22.4 3.8 %all-to-all-done.parts = bf16[16,56,128]{2,1,0:T(8,128)(2,1)S(1)} async-done(((bf16[16,56,128]{2,1,0:T(8,128)(2,1)}), bf16[16,56,128]{2,1,0:T(8,128)(2,1)S(1)}, u32[]{:S(2)}, u32[]{:S(2)}) %all-to-all-start) | async-done | bytes 229408 | tf_op jit(solution)/shard_map/all_to_all | solution.py:326
  26.3 0.0 copy-start.1
  26.3 0.1 shard_map.79
  26.3 0.0 copy-start
  26.4 18.0 %all_to_all.21.gathered = bf16[64,56,128]{2,1,0:T(8,128)(2,1)S(1)} all-to-all(bf16[64,56,128]{2,1,0:T(8,128)(2,1)S(1)} %shard_map.79), channel_id=1, replica_groups=mesh['segment'=4,'tensor'=16,'dp'=2] {'segment','tensor'}, dimensions={0} | all-to-all | bytes 1835008 | tf_op jit(solution)/shard_map/all_to_all | solution.py:328
  44.3 0.0 copy-done.1
  44.3 0.0 copy-done
  44.3 2.4 %shard_map.80 = (f32[256,768]{1,0:T(8,128)S(1)}, f32[32,128]{1,0:T(8,128)S(1)}, bf16[256,384]{1,0:T(8,128)(2,1)S(1)}) custom-call(s32[8,128]{1,0:T(8,128)S(1)} %get-tuple-element.11.limits, bf16[64,56,128]{2,1,0:T(8,128)(2,1)S(1)} %all_to_all.21.gathered, bf16[64,768]{1,0:T(8,128)(2,1)S(1)} %collective-permute-done.one, ...), custom_call_target="tpu_custom_call" | custom-call | flops 600000000 | bytes 5000000 | tf_op jit(solution)/shard_map/pallas_call | solution.py:247
  46.8 5.1 %collective-permute-start.3 = (bf16[256,384]{1,0:T(8,128)(2,1)S(1)}, bf16[256,384]{1,0:T(8,128)(2,1)S(1)}, u32[]{:S(2)}, u32[]{:S(2)}) collective-permute-start(bf16[256,384]{1,0:T(8,128)(2,1)S(1)} %get-tuple-element.15), channel_id=1, source_target_pairs={{0,1},{1,0},{2,3},{3,2},{4,5},{5,4},{6,7},{7,6},{8,9},{9,8},{10,11... | collective-permute-start | bytes 589832 | tf_op jit(solution)/shard_map/ppermute | solution.py:330
  51.9 9.8 %all_to_all.22 = f32[32,1,128]{2,1,0:T(1,128)S(1)} all-to-all(f32[32,1,128]{2,1,0:T(1,128)S(1)} %bitcast.21), channel_id=1, replica_groups=mesh['segment'=4,'tensor'=16,'dp'=2] {'tensor','dp'}, dimensions={0} | all-to-all | bytes 32768 | tf_op jit(solution)/shard_map/all_to_all | solution.py:331
  61.7 0.0 collective-permute-done.3.swapped
  61.7 0.8 %shard_map.81 = (f32[1,64,384]{2,1,0:T(8,128)}, f32[1,64,384]{2,1,0:T(8,128)}) custom-call(f32[8,128]{1,0:T(8,128)S(1)} %get-tuple-element.10.bounds, f32[32,128]{1,0:T(8,128)S(1)} %bitcast.20, f32[256,768]{1,0:T(8,128)S(1)} %get-tuple-element.14.each, bf16[256,384]{1,0:T(8,128)(2,1)S(1)} %collective-permute-done.3.swapped), custom_call_target="tpu_custom_call" | custom-call | flops 300000 | bytes 900000 | tf_op jit(solution)/shard_map/pallas_call | solution.py:298
Async XLA Ops:
  1.6 7.6 %collective-permute-start = (bf16[64,768]{1,0:T(8,128)(2,1)S(1)}, bf16[64,768]{1,0:T(8,128)(2,1)S(1)}, u32[]{:S(2)}, u32[]{:S(2)}) collective-permute-start(bf16[64,768]{1,0:T(8,128)(2,1)S(1)} %get-tuple-element.18), channel_id=1, source_target_pairs={{0,32},{32,64},{64,96},{96,0},{1,33},{33,65},{65,97},{97,1},{2,34}... | collective-permute-start | bytes 294920 | tf_op jit(solution)/shard_map/ppermute | solution.py:317
  3.7 6.5 %collective-permute-start.1 = (bf16[64,768]{1,0:T(8,128)(2,1)S(1)}, bf16[64,768]{1,0:T(8,128)(2,1)S(1)}, u32[]{:S(2)}, u32[]{:S(2)}) collective-permute-start(bf16[64,768]{1,0:T(8,128)(2,1)S(1)} %get-tuple-element.20.to_two), channel_id=1, source_target_pairs={{0,64},{32,96},{64,0},{96,32},{1,65},{33,97},{65,1},{97,33},{2,66}... | collective-permute-start | bytes 294920 | tf_op jit(solution)/shard_map/ppermute | solution.py:317
  6.8 3.4 %copy-start.2 = (s32[2]{0:T(128)S(1)}, s32[2]{0:T(128)}, u32[]{:S(2)}) copy-start(s32[2]{0:T(128)} %param.8) | copy-start | bytes 28
  11.1 15.2 %all-to-all-start = ((bf16[16,56,128]{2,1,0:T(8,128)(2,1)}), bf16[16,56,128]{2,1,0:T(8,128)(2,1)S(1)}, u32[]{:S(2)}, u32[]{:S(2)}) async-start(bf16[16,56,128]{2,1,0:T(8,128)(2,1)} %get-tuple-element.12), calls=%async_computation | async-start | bytes 458752 | tf_op jit(solution)/shard_map/all_to_all | solution.py:326
  18.9 3.5 %collective-permute-start.2 = (bf16[64,768]{1,0:T(8,128)(2,1)S(1)}, bf16[64,768]{1,0:T(8,128)(2,1)S(1)}, u32[]{:S(2)}, u32[]{:S(2)}) collective-permute-start(bf16[64,768]{1,0:T(8,128)(2,1)S(1)} %get-tuple-element.21.sent.to_three), channel_id=1, source_target_pairs={{0,96},{32,0},{64,32},{96,64},{1,97},{33,1},{65,33},{97,65},{2,98}... | collective-permute-start | bytes 294920 | tf_op jit(solution)/shard_map/ppermute | solution.py:317
  26.3 18.1 %copy-start.1 = (bf16[2,384,768]{2,1,0:T(8,128)(2,1)S(1)}, bf16[2,384,768]{2,1,0:T(8,128)(2,1)}, u32[]{:S(2)}) copy-start(bf16[2,384,768]{2,1,0:T(8,128)(2,1)} %cot.1) | copy-start | bytes 3538948
  26.3 18.0 %copy-start = (bf16[2,384,768]{2,1,0:T(8,128)(2,1)S(1)}, bf16[2,384,768]{2,1,0:T(8,128)(2,1)}, u32[]{:S(2)}) copy-start(bf16[2,384,768]{2,1,0:T(8,128)(2,1)} %act.1) | copy-start | bytes 3538948
  46.8 14.9 %collective-permute-start.3 = (bf16[256,384]{1,0:T(8,128)(2,1)S(1)}, bf16[256,384]{1,0:T(8,128)(2,1)S(1)}, u32[]{:S(2)}, u32[]{:S(2)}) collective-permute-start(bf16[256,384]{1,0:T(8,128)(2,1)S(1)} %get-tuple-element.15), channel_id=1, source_target_pairs={{0,1},{1,0},{2,3},{3,2},{4,5},{5,4},{6,7},{7,6},{8,9},{9,8},{10,11... | collective-permute-start | bytes 589832 | tf_op jit(solution)/shard_map/ppermute | solution.py:330
